TPU v7x, 128 devices: a whole 4x4x4 slice. The times are simulated.
128 devices in a mesh: blk: 64 (over y, z_lo, x, core), team: 2 (over z_hi).
Axes of the slice: x: 4, y: 4, z: 4 (z_hi: 2, z_lo: 2; z = z_hi * 2 + z_lo), core: 2. Of those that a mesh axis runs over, the one named last changes fastest.
Arguments:
- queries: bfloat16 [4096, 64, 128], P('blk'), may hold values from -6 to 6
- head_weights: float32 [4096, 64], P('blk'), may hold values from -0.75 to 0.75
- keys: bfloat16 [16384, 128], P('blk'), may hold values from -6 to 6
- query_pos: int32 [4096], P('blk'), may hold values from 0 to 16383
- block_limits: int32 [256], P('blk'), may hold values from 1 to 64
Outputs:
- block_logits: float32 [4096, 256], P('blk')
All inputs are finite; a program needn't handle non-finite values.
Results may differ from a plain program's by a relative error of at most 0.0022.
Values may be sent and summed in bfloat16 or wider, within the bound.
No kernel may reach another device: no remote copies, remote signals or barrier semaphores. Data moves between devices by JAX's collectives and lax.ppermute only.
A program may use at most 64 MiB of HBM per device.

v0:
```python
import jax
import jax.numpy as jnp
from jax import lax
from jax.sharding import PartitionSpec as P

BLOCK = 64


mask_value = -8.0


def passed_along(value, axis, steps):
    count = lax.axis_size(axis)
    pairs = [(source, (source + steps) % count) for source in range(count)]
    return lax.ppermute(value, axis, pairs)


def shard_logits(flat_queries, weights, positions, key_slab, limit_slab, source):
    rows = weights.shape[0]
    heads = weights.shape[1]
    key_count = key_slab.shape[0]
    scale = key_slab.shape[1] ** (-0.5)
    raw = lax.dot_general(
        flat_queries, key_slab, (((1,), (1,)), ((), ())), preferred_element_type=jnp.float32
    )
    raw = jax.nn.relu(raw).reshape(rows, heads, 256)
    pieces = [jnp.sum(raw * weights[:, :, None], axis=1) * scale]
    score = jnp.concatenate(pieces, axis=1)
    local = jnp.arange(key_count, dtype=jnp.int32)
    key_position = source * key_count + local
    filled = local % BLOCK < jnp.repeat(limit_slab, BLOCK)
    visible = filled[None, :] & (key_position[None, :] <= positions[:, None])
    masked = jnp.where(visible, score, mask_value)
    return jnp.max(masked.reshape(rows, key_count // BLOCK, BLOCK), axis=-1)


def place(output, pooled, source):
    return lax.dynamic_update_slice(output, pooled, (jnp.int32(0), source * pooled.shape[1]))


def body(queries, head_weights, keys, query_pos, block_limits):
    cycle_size = lax.axis_size("blk")
    half = cycle_size // 2
    mine = lax.axis_index("blk")
    member = lax.axis_index("team")
    head_size = queries.shape[-1]
    shard_blocks = keys.shape[0] // BLOCK
    flat_queries = queries.reshape(-1, head_size)
    far_keys, far_limits = passed_along((keys, block_limits), "blk", half)
    anchor = (mine - member * half) % cycle_size
    stride = 1
    key_slab = jnp.where(member == 1, far_keys, keys)
    limit_slab = jnp.where(member == 1, far_limits, block_limits)
    output = jnp.zeros((queries.shape[0], shard_blocks * cycle_size), jnp.float32)

    def visit(stop, carry):
        output, key_slab, limit_slab = carry
        source = (anchor - stride * stop) % cycle_size
        pooled = shard_logits(flat_queries, head_weights, query_pos, key_slab, limit_slab, source)
        output = place(output, pooled, source)
        key_slab, limit_slab = passed_along((key_slab, limit_slab), "blk", 1)
        return (output, key_slab, limit_slab)

    output, key_slab, limit_slab = lax.fori_loop(0, half - 1, visit, (output, key_slab, limit_slab))
    source = (anchor - stride * (half - 1)) % cycle_size
    output = place(
        output,
        shard_logits(flat_queries, head_weights, query_pos, key_slab, limit_slab, source),
        source,
    )
    return lax.psum(output.astype(jnp.bfloat16), "team").astype(jnp.float32)


def solution(mesh):
    in_specs = (P("blk", None, None), P("blk", None), P("blk", None), P("blk"), P("blk"))
    out_specs = P("blk", None)
    return jax.shard_map(body, mesh=mesh, in_specs=in_specs, out_specs=out_specs, check_vma=False)
```

profile of v0, /device:TPU:0, one launch (start us, length us, event | category | flops | bytes accessed | tf_op | source)
XLA Modules:
  0.0 284.0 jit_solution(2399459358640469129)
XLA Ops:
  3.5 4.9 %collective-permute-done.3 = s32[4]{0:T(128)S(1)} collective-permute-done((s32[4]{0:T(128)}, s32[4]{0:T(128)S(1)}, u32[]{:S(2)}, u32[]{:S(2)}) %collective-permute-start.3) | collective-permute-done | bytes 48 | tf_op jit(solution)/shard_map/ppermute | solution.py:15
  10.0 249.6 %while.19 = (s32[]{:T(128)}, bf16[64,256]{0,1:T(8,128)(2,1)S(1)}, bf16[256,128]{1,0:T(8,128)(2,1)S(1)}, s32[4]{0:T(128)S(1)}, s32[]{:T(128)}, /*index=5*/s32[64]...) while((s32[]{:T(128)}, bf16[64,256]{0,1:T(8,128)(2,1)S(1)}, ...), condition=%wide.region_3.4_spmd, body=%wide.region_0.3_spmd.sunk | while | flops 271667200 | bytes 1792768 | solution.py:64
  21.5 4.6 %collective-permute-done.1 = s32[4]{0:T(128)S(1)} collective-permute-done((s32[4]{0:T(128)S(1)}, s32[4]{0:T(128)S(1)}, u32[]{:S(2)}, u32[]{:S(2)}) %collective-permute-start.1) | collective-permute-done | bytes 48 | tf_op jit(solution)/shard_map/while/body/eval_jaxpr/ppermute | solution.py:15
  29.6 4.6 %collective-permute-done.1 = s32[4]{0:T(128)S(1)} collective-permute-done((s32[4]{0:T(128)S(1)}, s32[4]{0:T(128)S(1)}, u32[]{:S(2)}, u32[]{:S(2)}) %collective-permute-start.1) | collective-permute-done | bytes 48 | tf_op jit(solution)/shard_map/while/body/eval_jaxpr/ppermute | solution.py:15
  37.6 4.6 %collective-permute-done.1 = s32[4]{0:T(128)S(1)} collective-permute-done((s32[4]{0:T(128)S(1)}, s32[4]{0:T(128)S(1)}, u32[]{:S(2)}, u32[]{:S(2)}) %collective-permute-start.1) | collective-permute-done | bytes 48 | tf_op jit(solution)/shard_map/while/body/eval_jaxpr/ppermute | solution.py:15
  45.7 4.6 %collective-permute-done.1 = s32[4]{0:T(128)S(1)} collective-permute-done((s32[4]{0:T(128)S(1)}, s32[4]{0:T(128)S(1)}, u32[]{:S(2)}, u32[]{:S(2)}) %collective-permute-start.1) | collective-permute-done | bytes 48 | tf_op jit(solution)/shard_map/while/body/eval_jaxpr/ppermute | solution.py:15
  53.7 4.6 %collective-permute-done.1 = s32[4]{0:T(128)S(1)} collective-permute-done((s32[4]{0:T(128)S(1)}, s32[4]{0:T(128)S(1)}, u32[]{:S(2)}, u32[]{:S(2)}) %collective-permute-start.1) | collective-permute-done | bytes 48 | tf_op jit(solution)/shard_map/while/body/eval_jaxpr/ppermute | solution.py:15
  61.8 4.6 %collective-permute-done.1 = s32[4]{0:T(128)S(1)} collective-permute-done((s32[4]{0:T(128)S(1)}, s32[4]{0:T(128)S(1)}, u32[]{:S(2)}, u32[]{:S(2)}) %collective-permute-start.1) | collective-permute-done | bytes 48 | tf_op jit(solution)/shard_map/while/body/eval_jaxpr/ppermute | solution.py:15
  69.8 4.6 %collective-permute-done.1 = s32[4]{0:T(128)S(1)} collective-permute-done((s32[4]{0:T(128)S(1)}, s32[4]{0:T(128)S(1)}, u32[]{:S(2)}, u32[]{:S(2)}) %collective-permute-start.1) | collective-permute-done | bytes 48 | tf_op jit(solution)/shard_map/while/body/eval_jaxpr/ppermute | solution.py:15
  77.9 4.6 %collective-permute-done.1 = s32[4]{0:T(128)S(1)} collective-permute-done((s32[4]{0:T(128)S(1)}, s32[4]{0:T(128)S(1)}, u32[]{:S(2)}, u32[]{:S(2)}) %collective-permute-start.1) | collective-permute-done | bytes 48 | tf_op jit(solution)/shard_map/while/body/eval_jaxpr/ppermute | solution.py:15
  85.9 4.6 %collective-permute-done.1 = s32[4]{0:T(128)S(1)} collective-permute-done((s32[4]{0:T(128)S(1)}, s32[4]{0:T(128)S(1)}, u32[]{:S(2)}, u32[]{:S(2)}) %collective-permute-start.1) | collective-permute-done | bytes 48 | tf_op jit(solution)/shard_map/while/body/eval_jaxpr/ppermute | solution.py:15
  94.0 4.6 %collective-permute-done.1 = s32[4]{0:T(128)S(1)} collective-permute-done((s32[4]{0:T(128)S(1)}, s32[4]{0:T(128)S(1)}, u32[]{:S(2)}, u32[]{:S(2)}) %collective-permute-start.1) | collective-permute-done | bytes 48 | tf_op jit(solution)/shard_map/while/body/eval_jaxpr/ppermute | solution.py:15
  102.0 4.6 %collective-permute-done.1 = s32[4]{0:T(128)S(1)} collective-permute-done((s32[4]{0:T(128)S(1)}, s32[4]{0:T(128)S(1)}, u32[]{:S(2)}, u32[]{:S(2)}) %collective-permute-start.1) | collective-permute-done | bytes 48 | tf_op jit(solution)/shard_map/while/body/eval_jaxpr/ppermute | solution.py:15
  110.1 4.6 %collective-permute-done.1 = s32[4]{0:T(128)S(1)} collective-permute-done((s32[4]{0:T(128)S(1)}, s32[4]{0:T(128)S(1)}, u32[]{:S(2)}, u32[]{:S(2)}) %collective-permute-start.1) | collective-permute-done | bytes 48 | tf_op jit(solution)/shard_map/while/body/eval_jaxpr/ppermute | solution.py:15
  118.2 4.6 %collective-permute-done.1 = s32[4]{0:T(128)S(1)} collective-permute-done((s32[4]{0:T(128)S(1)}, s32[4]{0:T(128)S(1)}, u32[]{:S(2)}, u32[]{:S(2)}) %collective-permute-start.1) | collective-permute-done | bytes 48 | tf_op jit(solution)/shard_map/while/body/eval_jaxpr/ppermute | solution.py:15
  126.2 4.6 %collective-permute-done.1 = s32[4]{0:T(128)S(1)} collective-permute-done((s32[4]{0:T(128)S(1)}, s32[4]{0:T(128)S(1)}, u32[]{:S(2)}, u32[]{:S(2)}) %collective-permute-start.1) | collective-permute-done | bytes 48 | tf_op jit(solution)/shard_map/while/body/eval_jaxpr/ppermute | solution.py:15
  134.3 4.6 %collective-permute-done.1 = s32[4]{0:T(128)S(1)} collective-permute-done((s32[4]{0:T(128)S(1)}, s32[4]{0:T(128)S(1)}, u32[]{:S(2)}, u32[]{:S(2)}) %collective-permute-start.1) | collective-permute-done | bytes 48 | tf_op jit(solution)/shard_map/while/body/eval_jaxpr/ppermute | solution.py:15
  142.3 4.6 %collective-permute-done.1 = s32[4]{0:T(128)S(1)} collective-permute-done((s32[4]{0:T(128)S(1)}, s32[4]{0:T(128)S(1)}, u32[]{:S(2)}, u32[]{:S(2)}) %collective-permute-start.1) | collective-permute-done | bytes 48 | tf_op jit(solution)/shard_map/while/body/eval_jaxpr/ppermute | solution.py:15
  150.4 4.6 %collective-permute-done.1 = s32[4]{0:T(128)S(1)} collective-permute-done((s32[4]{0:T(128)S(1)}, s32[4]{0:T(128)S(1)}, u32[]{:S(2)}, u32[]{:S(2)}) %collective-permute-start.1) | collective-permute-done | bytes 48 | tf_op jit(solution)/shard_map/while/body/eval_jaxpr/ppermute | solution.py:15
  158.4 4.6 %collective-permute-done.1 = s32[4]{0:T(128)S(1)} collective-permute-done((s32[4]{0:T(128)S(1)}, s32[4]{0:T(128)S(1)}, u32[]{:S(2)}, u32[]{:S(2)}) %collective-permute-start.1) | collective-permute-done | bytes 48 | tf_op jit(solution)/shard_map/while/body/eval_jaxpr/ppermute | solution.py:15
  166.5 4.6 %collective-permute-done.1 = s32[4]{0:T(128)S(1)} collective-permute-done((s32[4]{0:T(128)S(1)}, s32[4]{0:T(128)S(1)}, u32[]{:S(2)}, u32[]{:S(2)}) %collective-permute-start.1) | collective-permute-done | bytes 48 | tf_op jit(solution)/shard_map/while/body/eval_jaxpr/ppermute | solution.py:15
  174.5 4.6 %collective-permute-done.1 = s32[4]{0:T(128)S(1)} collective-permute-done((s32[4]{0:T(128)S(1)}, s32[4]{0:T(128)S(1)}, u32[]{:S(2)}, u32[]{:S(2)}) %collective-permute-start.1) | collective-permute-done | bytes 48 | tf_op jit(solution)/shard_map/while/body/eval_jaxpr/ppermute | solution.py:15
  182.6 4.6 %collective-permute-done.1 = s32[4]{0:T(128)S(1)} collective-permute-done((s32[4]{0:T(128)S(1)}, s32[4]{0:T(128)S(1)}, u32[]{:S(2)}, u32[]{:S(2)}) %collective-permute-start.1) | collective-permute-done | bytes 48 | tf_op jit(solution)/shard_map/while/body/eval_jaxpr/ppermute | solution.py:15
  190.6 4.6 %collective-permute-done.1 = s32[4]{0:T(128)S(1)} collective-permute-done((s32[4]{0:T(128)S(1)}, s32[4]{0:T(128)S(1)}, u32[]{:S(2)}, u32[]{:S(2)}) %collective-permute-start.1) | collective-permute-done | bytes 48 | tf_op jit(solution)/shard_map/while/body/eval_jaxpr/ppermute | solution.py:15
  206.7 4.6 %collective-permute-done.1 = s32[4]{0:T(128)S(1)} collective-permute-done((s32[4]{0:T(128)S(1)}, s32[4]{0:T(128)S(1)}, u32[]{:S(2)}, u32[]{:S(2)}) %collective-permute-start.1) | collective-permute-done | bytes 48 | tf_op jit(solution)/shard_map/while/body/eval_jaxpr/ppermute | solution.py:15
  214.8 4.6 %collective-permute-done.1 = s32[4]{0:T(128)S(1)} collective-permute-done((s32[4]{0:T(128)S(1)}, s32[4]{0:T(128)S(1)}, u32[]{:S(2)}, u32[]{:S(2)}) %collective-permute-start.1) | collective-permute-done | bytes 48 | tf_op jit(solution)/shard_map/while/body/eval_jaxpr/ppermute | solution.py:15
  222.8 4.6 %collective-permute-done.1 = s32[4]{0:T(128)S(1)} collective-permute-done((s32[4]{0:T(128)S(1)}, s32[4]{0:T(128)S(1)}, u32[]{:S(2)}, u32[]{:S(2)}) %collective-permute-start.1) | collective-permute-done | bytes 48 | tf_op jit(solution)/shard_map/while/body/eval_jaxpr/ppermute | solution.py:15
  238.9 4.6 %collective-permute-done.1 = s32[4]{0:T(128)S(1)} collective-permute-done((s32[4]{0:T(128)S(1)}, s32[4]{0:T(128)S(1)}, u32[]{:S(2)}, u32[]{:S(2)}) %collective-permute-start.1) | collective-permute-done | bytes 48 | tf_op jit(solution)/shard_map/while/body/eval_jaxpr/ppermute | solution.py:15
  247.0 4.6 %collective-permute-done.1 = s32[4]{0:T(128)S(1)} collective-permute-done((s32[4]{0:T(128)S(1)}, s32[4]{0:T(128)S(1)}, u32[]{:S(2)}, u32[]{:S(2)}) %collective-permute-start.1) | collective-permute-done | bytes 48 | tf_op jit(solution)/shard_map/while/body/eval_jaxpr/ppermute | solution.py:15
  255.0 4.6 %collective-permute-done.1 = s32[4]{0:T(128)S(1)} collective-permute-done((s32[4]{0:T(128)S(1)}, s32[4]{0:T(128)S(1)}, u32[]{:S(2)}, u32[]{:S(2)}) %collective-permute-start.1) | collective-permute-done | bytes 48 | tf_op jit(solution)/shard_map/while/body/eval_jaxpr/ppermute | solution.py:15
  263.6 5.6 %copy.11 = f32[4096,256]{1,0:T(8,128)} copy(f32[4096,256]{0,1:T(8,128)} %fusion.3) | data formatting | bytes 8388608 | tf_op jit(solution)/shard_map/jit(relu)/max | solution.py:26
  272.6 10.8 %psum.7 = bf16[64,256]{1,0:T(8,128)(2,1)S(1)} all-reduce(bf16[64,256]{1,0:T(8,128)(2,1)S(1)} %dynamic_update_slice.13), channel_id=1, replica_groups=mesh['blk'=64,'team'=2] {'team'}, use_global_device_ids=true, to_apply=%region_6.7 | all-reduce | flops 16384 | bytes 65536 | tf_op jit(solution)/shard_map/psum | solution.py:71
  (426 shorter events, 131.8 us)
Async XLA Ops:
  0.0 9.1 %collective-permute-start.2 = (bf16[256,128]{1,0:T(8,128)(2,1)}, bf16[256,128]{1,0:T(8,128)(2,1)S(1)}, u32[]{:S(2)}, u32[]{:S(2)}) collective-permute-start(bf16[256,128]{1,0:T(8,128)(2,1)} %param.9), channel_id=1, source_target_pairs={{0,64},{2,66},{4,68},{6,70},{8,72},{10,74},{12,76},{14,78},{16,80}... | collective-permute-start | bytes 196616 | tf_op jit(solution)/shard_map/ppermute | solution.py:15
  10.0 8.0 %collective-permute-start = (bf16[256,128]{1,0:T(8,128)(2,1)S(1)}, bf16[256,128]{1,0:T(8,128)(2,1)S(1)}, u32[]{:S(2)}, u32[]{:S(2)}) collective-permute-start(bf16[256,128]{1,0:T(8,128)(2,1)S(1)} %copy.26), channel_id=1, source_target_pairs={{0,2},{2,4},{4,6},{6,8},{8,10},{10,12},{12,14},{14,16},{16,18},{18... | collective-permute-start | bytes 196616 | tf_op jit(solution)/shard_map/while/body/eval_jaxpr/ppermute | solution.py:15
  18.1 8.0 %collective-permute-start = (bf16[256,128]{1,0:T(8,128)(2,1)S(1)}, bf16[256,128]{1,0:T(8,128)(2,1)S(1)}, u32[]{:S(2)}, u32[]{:S(2)}) collective-permute-start(bf16[256,128]{1,0:T(8,128)(2,1)S(1)} %copy.26), channel_id=1, source_target_pairs={{0,2},{2,4},{4,6},{6,8},{8,10},{10,12},{12,14},{14,16},{16,18},{18... | collective-permute-start | bytes 196616 | tf_op jit(solution)/shard_map/while/body/eval_jaxpr/ppermute | solution.py:15
  26.1 8.0 %collective-permute-start = (bf16[256,128]{1,0:T(8,128)(2,1)S(1)}, bf16[256,128]{1,0:T(8,128)(2,1)S(1)}, u32[]{:S(2)}, u32[]{:S(2)}) collective-permute-start(bf16[256,128]{1,0:T(8,128)(2,1)S(1)} %copy.26), channel_id=1, source_target_pairs={{0,2},{2,4},{4,6},{6,8},{8,10},{10,12},{12,14},{14,16},{16,18},{18... | collective-permute-start | bytes 196616 | tf_op jit(solution)/shard_map/while/body/eval_jaxpr/ppermute | solution.py:15
  34.2 8.0 %collective-permute-start = (bf16[256,128]{1,0:T(8,128)(2,1)S(1)}, bf16[256,128]{1,0:T(8,128)(2,1)S(1)}, u32[]{:S(2)}, u32[]{:S(2)}) collective-permute-start(bf16[256,128]{1,0:T(8,128)(2,1)S(1)} %copy.26), channel_id=1, source_target_pairs={{0,2},{2,4},{4,6},{6,8},{8,10},{10,12},{12,14},{14,16},{16,18},{18... | collective-permute-start | bytes 196616 | tf_op jit(solution)/shard_map/while/body/eval_jaxpr/ppermute | solution.py:15
  42.2 8.0 %collective-permute-start = (bf16[256,128]{1,0:T(8,128)(2,1)S(1)}, bf16[256,128]{1,0:T(8,128)(2,1)S(1)}, u32[]{:S(2)}, u32[]{:S(2)}) collective-permute-start(bf16[256,128]{1,0:T(8,128)(2,1)S(1)} %copy.26), channel_id=1, source_target_pairs={{0,2},{2,4},{4,6},{6,8},{8,10},{10,12},{12,14},{14,16},{16,18},{18... | collective-permute-start | bytes 196616 | tf_op jit(solution)/shard_map/while/body/eval_jaxpr/ppermute | solution.py:15
  50.3 8.0 %collective-permute-start = (bf16[256,128]{1,0:T(8,128)(2,1)S(1)}, bf16[256,128]{1,0:T(8,128)(2,1)S(1)}, u32[]{:S(2)}, u32[]{:S(2)}) collective-permute-start(bf16[256,128]{1,0:T(8,128)(2,1)S(1)} %copy.26), channel_id=1, source_target_pairs={{0,2},{2,4},{4,6},{6,8},{8,10},{10,12},{12,14},{14,16},{16,18},{18... | collective-permute-start | bytes 196616 | tf_op jit(solution)/shard_map/while/body/eval_jaxpr/ppermute | solution.py:15
  58.3 8.0 %collective-permute-start = (bf16[256,128]{1,0:T(8,128)(2,1)S(1)}, bf16[256,128]{1,0:T(8,128)(2,1)S(1)}, u32[]{:S(2)}, u32[]{:S(2)}) collective-permute-start(bf16[256,128]{1,0:T(8,128)(2,1)S(1)} %copy.26), channel_id=1, source_target_pairs={{0,2},{2,4},{4,6},{6,8},{8,10},{10,12},{12,14},{14,16},{16,18},{18... | collective-permute-start | bytes 196616 | tf_op jit(solution)/shard_map/while/body/eval_jaxpr/ppermute | solution.py:15
  66.4 8.0 %collective-permute-start = (bf16[256,128]{1,0:T(8,128)(2,1)S(1)}, bf16[256,128]{1,0:T(8,128)(2,1)S(1)}, u32[]{:S(2)}, u32[]{:S(2)}) collective-permute-start(bf16[256,128]{1,0:T(8,128)(2,1)S(1)} %copy.26), channel_id=1, source_target_pairs={{0,2},{2,4},{4,6},{6,8},{8,10},{10,12},{12,14},{14,16},{16,18},{18... | collective-permute-start | bytes 196616 | tf_op jit(solution)/shard_map/while/body/eval_jaxpr/ppermute | solution.py:15
  74.4 8.0 %collective-permute-start = (bf16[256,128]{1,0:T(8,128)(2,1)S(1)}, bf16[256,128]{1,0:T(8,128)(2,1)S(1)}, u32[]{:S(2)}, u32[]{:S(2)}) collective-permute-start(bf16[256,128]{1,0:T(8,128)(2,1)S(1)} %copy.26), channel_id=1, source_target_pairs={{0,2},{2,4},{4,6},{6,8},{8,10},{10,12},{12,14},{14,16},{16,18},{18... | collective-permute-start | bytes 196616 | tf_op jit(solution)/shard_map/while/body/eval_jaxpr/ppermute | solution.py:15
  82.5 8.0 %collective-permute-start = (bf16[256,128]{1,0:T(8,128)(2,1)S(1)}, bf16[256,128]{1,0:T(8,128)(2,1)S(1)}, u32[]{:S(2)}, u32[]{:S(2)}) collective-permute-start(bf16[256,128]{1,0:T(8,128)(2,1)S(1)} %copy.26), channel_id=1, source_target_pairs={{0,2},{2,4},{4,6},{6,8},{8,10},{10,12},{12,14},{14,16},{16,18},{18... | collective-permute-start | bytes 196616 | tf_op jit(solution)/shard_map/while/body/eval_jaxpr/ppermute | solution.py:15
  90.5 8.0 %collective-permute-start = (bf16[256,128]{1,0:T(8,128)(2,1)S(1)}, bf16[256,128]{1,0:T(8,128)(2,1)S(1)}, u32[]{:S(2)}, u32[]{:S(2)}) collective-permute-start(bf16[256,128]{1,0:T(8,128)(2,1)S(1)} %copy.26), channel_id=1, source_target_pairs={{0,2},{2,4},{4,6},{6,8},{8,10},{10,12},{12,14},{14,16},{16,18},{18... | collective-permute-start | bytes 196616 | tf_op jit(solution)/shard_map/while/body/eval_jaxpr/ppermute | solution.py:15
  98.6 8.0 %collective-permute-start = (bf16[256,128]{1,0:T(8,128)(2,1)S(1)}, bf16[256,128]{1,0:T(8,128)(2,1)S(1)}, u32[]{:S(2)}, u32[]{:S(2)}) collective-permute-start(bf16[256,128]{1,0:T(8,128)(2,1)S(1)} %copy.26), channel_id=1, source_target_pairs={{0,2},{2,4},{4,6},{6,8},{8,10},{10,12},{12,14},{14,16},{16,18},{18... | collective-permute-start | bytes 196616 | tf_op jit(solution)/shard_map/while/body/eval_jaxpr/ppermute | solution.py:15
  106.6 8.0 %collective-permute-start = (bf16[256,128]{1,0:T(8,128)(2,1)S(1)}, bf16[256,128]{1,0:T(8,128)(2,1)S(1)}, u32[]{:S(2)}, u32[]{:S(2)}) collective-permute-start(bf16[256,128]{1,0:T(8,128)(2,1)S(1)} %copy.26), channel_id=1, source_target_pairs={{0,2},{2,4},{4,6},{6,8},{8,10},{10,12},{12,14},{14,16},{16,18},{18... | collective-permute-start | bytes 196616 | tf_op jit(solution)/shard_map/while/body/eval_jaxpr/ppermute | solution.py:15
  114.7 8.0 %collective-permute-start = (bf16[256,128]{1,0:T(8,128)(2,1)S(1)}, bf16[256,128]{1,0:T(8,128)(2,1)S(1)}, u32[]{:S(2)}, u32[]{:S(2)}) collective-permute-start(bf16[256,128]{1,0:T(8,128)(2,1)S(1)} %copy.26), channel_id=1, source_target_pairs={{0,2},{2,4},{4,6},{6,8},{8,10},{10,12},{12,14},{14,16},{16,18},{18... | collective-permute-start | bytes 196616 | tf_op jit(solution)/shard_map/while/body/eval_jaxpr/ppermute | solution.py:15
  122.7 8.0 %collective-permute-start = (bf16[256,128]{1,0:T(8,128)(2,1)S(1)}, bf16[256,128]{1,0:T(8,128)(2,1)S(1)}, u32[]{:S(2)}, u32[]{:S(2)}) collective-permute-start(bf16[256,128]{1,0:T(8,128)(2,1)S(1)} %copy.26), channel_id=1, source_target_pairs={{0,2},{2,4},{4,6},{6,8},{8,10},{10,12},{12,14},{14,16},{16,18},{18... | collective-permute-start | bytes 196616 | tf_op jit(solution)/shard_map/while/body/eval_jaxpr/ppermute | solution.py:15
  130.8 8.0 %collective-permute-start = (bf16[256,128]{1,0:T(8,128)(2,1)S(1)}, bf16[256,128]{1,0:T(8,128)(2,1)S(1)}, u32[]{:S(2)}, u32[]{:S(2)}) collective-permute-start(bf16[256,128]{1,0:T(8,128)(2,1)S(1)} %copy.26), channel_id=1, source_target_pairs={{0,2},{2,4},{4,6},{6,8},{8,10},{10,12},{12,14},{14,16},{16,18},{18... | collective-permute-start | bytes 196616 | tf_op jit(solution)/shard_map/while/body/eval_jaxpr/ppermute | solution.py:15
  138.9 8.0 %collective-permute-start = (bf16[256,128]{1,0:T(8,128)(2,1)S(1)}, bf16[256,128]{1,0:T(8,128)(2,1)S(1)}, u32[]{:S(2)}, u32[]{:S(2)}) collective-permute-start(bf16[256,128]{1,0:T(8,128)(2,1)S(1)} %copy.26), channel_id=1, source_target_pairs={{0,2},{2,4},{4,6},{6,8},{8,10},{10,12},{12,14},{14,16},{16,18},{18... | collective-permute-start | bytes 196616 | tf_op jit(solution)/shard_map/while/body/eval_jaxpr/ppermute | solution.py:15
  146.9 8.0 %collective-permute-start = (bf16[256,128]{1,0:T(8,128)(2,1)S(1)}, bf16[256,128]{1,0:T(8,128)(2,1)S(1)}, u32[]{:S(2)}, u32[]{:S(2)}) collective-permute-start(bf16[256,128]{1,0:T(8,128)(2,1)S(1)} %copy.26), channel_id=1, source_target_pairs={{0,2},{2,4},{4,6},{6,8},{8,10},{10,12},{12,14},{14,16},{16,18},{18... | collective-permute-start | bytes 196616 | tf_op jit(solution)/shard_map/while/body/eval_jaxpr/ppermute | solution.py:15
  155.0 8.0 %collective-permute-start = (bf16[256,128]{1,0:T(8,128)(2,1)S(1)}, bf16[256,128]{1,0:T(8,128)(2,1)S(1)}, u32[]{:S(2)}, u32[]{:S(2)}) collective-permute-start(bf16[256,128]{1,0:T(8,128)(2,1)S(1)} %copy.26), channel_id=1, source_target_pairs={{0,2},{2,4},{4,6},{6,8},{8,10},{10,12},{12,14},{14,16},{16,18},{18... | collective-permute-start | bytes 196616 | tf_op jit(solution)/shard_map/while/body/eval_jaxpr/ppermute | solution.py:15
  163.0 8.0 %collective-permute-start = (bf16[256,128]{1,0:T(8,128)(2,1)S(1)}, bf16[256,128]{1,0:T(8,128)(2,1)S(1)}, u32[]{:S(2)}, u32[]{:S(2)}) collective-permute-start(bf16[256,128]{1,0:T(8,128)(2,1)S(1)} %copy.26), channel_id=1, source_target_pairs={{0,2},{2,4},{4,6},{6,8},{8,10},{10,12},{12,14},{14,16},{16,18},{18... | collective-permute-start | bytes 196616 | tf_op jit(solution)/shard_map/while/body/eval_jaxpr/ppermute | solution.py:15
  171.1 8.0 %collective-permute-start = (bf16[256,128]{1,0:T(8,128)(2,1)S(1)}, bf16[256,128]{1,0:T(8,128)(2,1)S(1)}, u32[]{:S(2)}, u32[]{:S(2)}) collective-permute-start(bf16[256,128]{1,0:T(8,128)(2,1)S(1)} %copy.26), channel_id=1, source_target_pairs={{0,2},{2,4},{4,6},{6,8},{8,10},{10,12},{12,14},{14,16},{16,18},{18... | collective-permute-start | bytes 196616 | tf_op jit(solution)/shard_map/while/body/eval_jaxpr/ppermute | solution.py:15
  179.1 8.0 %collective-permute-start = (bf16[256,128]{1,0:T(8,128)(2,1)S(1)}, bf16[256,128]{1,0:T(8,128)(2,1)S(1)}, u32[]{:S(2)}, u32[]{:S(2)}) collective-permute-start(bf16[256,128]{1,0:T(8,128)(2,1)S(1)} %copy.26), channel_id=1, source_target_pairs={{0,2},{2,4},{4,6},{6,8},{8,10},{10,12},{12,14},{14,16},{16,18},{18... | collective-permute-start | bytes 196616 | tf_op jit(solution)/shard_map/while/body/eval_jaxpr/ppermute | solution.py:15
  187.2 8.0 %collective-permute-start = (bf16[256,128]{1,0:T(8,128)(2,1)S(1)}, bf16[256,128]{1,0:T(8,128)(2,1)S(1)}, u32[]{:S(2)}, u32[]{:S(2)}) collective-permute-start(bf16[256,128]{1,0:T(8,128)(2,1)S(1)} %copy.26), channel_id=1, source_target_pairs={{0,2},{2,4},{4,6},{6,8},{8,10},{10,12},{12,14},{14,16},{16,18},{18... | collective-permute-start | bytes 196616 | tf_op jit(solution)/shard_map/while/body/eval_jaxpr/ppermute | solution.py:15
  195.2 8.0 %collective-permute-start = (bf16[256,128]{1,0:T(8,128)(2,1)S(1)}, bf16[256,128]{1,0:T(8,128)(2,1)S(1)}, u32[]{:S(2)}, u32[]{:S(2)}) collective-permute-start(bf16[256,128]{1,0:T(8,128)(2,1)S(1)} %copy.26), channel_id=1, source_target_pairs={{0,2},{2,4},{4,6},{6,8},{8,10},{10,12},{12,14},{14,16},{16,18},{18... | collective-permute-start | bytes 196616 | tf_op jit(solution)/shard_map/while/body/eval_jaxpr/ppermute | solution.py:15
  203.3 8.0 %collective-permute-start = (bf16[256,128]{1,0:T(8,128)(2,1)S(1)}, bf16[256,128]{1,0:T(8,128)(2,1)S(1)}, u32[]{:S(2)}, u32[]{:S(2)}) collective-permute-start(bf16[256,128]{1,0:T(8,128)(2,1)S(1)} %copy.26), channel_id=1, source_target_pairs={{0,2},{2,4},{4,6},{6,8},{8,10},{10,12},{12,14},{14,16},{16,18},{18... | collective-permute-start | bytes 196616 | tf_op jit(solution)/shard_map/while/body/eval_jaxpr/ppermute | solution.py:15
  211.3 8.0 %collective-permute-start = (bf16[256,128]{1,0:T(8,128)(2,1)S(1)}, bf16[256,128]{1,0:T(8,128)(2,1)S(1)}, u32[]{:S(2)}, u32[]{:S(2)}) collective-permute-start(bf16[256,128]{1,0:T(8,128)(2,1)S(1)} %copy.26), channel_id=1, source_target_pairs={{0,2},{2,4},{4,6},{6,8},{8,10},{10,12},{12,14},{14,16},{16,18},{18... | collective-permute-start | bytes 196616 | tf_op jit(solution)/shard_map/while/body/eval_jaxpr/ppermute | solution.py:15
  219.4 8.0 %collective-permute-start = (bf16[256,128]{1,0:T(8,128)(2,1)S(1)}, bf16[256,128]{1,0:T(8,128)(2,1)S(1)}, u32[]{:S(2)}, u32[]{:S(2)}) collective-permute-start(bf16[256,128]{1,0:T(8,128)(2,1)S(1)} %copy.26), channel_id=1, source_target_pairs={{0,2},{2,4},{4,6},{6,8},{8,10},{10,12},{12,14},{14,16},{16,18},{18... | collective-permute-start | bytes 196616 | tf_op jit(solution)/shard_map/while/body/eval_jaxpr/ppermute | solution.py:15
  227.4 8.0 %collective-permute-start = (bf16[256,128]{1,0:T(8,128)(2,1)S(1)}, bf16[256,128]{1,0:T(8,128)(2,1)S(1)}, u32[]{:S(2)}, u32[]{:S(2)}) collective-permute-start(bf16[256,128]{1,0:T(8,128)(2,1)S(1)} %copy.26), channel_id=1, source_target_pairs={{0,2},{2,4},{4,6},{6,8},{8,10},{10,12},{12,14},{14,16},{16,18},{18... | collective-permute-start | bytes 196616 | tf_op jit(solution)/shard_map/while/body/eval_jaxpr/ppermute | solution.py:15
  235.5 8.0 %collective-permute-start = (bf16[256,128]{1,0:T(8,128)(2,1)S(1)}, bf16[256,128]{1,0:T(8,128)(2,1)S(1)}, u32[]{:S(2)}, u32[]{:S(2)}) collective-permute-start(bf16[256,128]{1,0:T(8,128)(2,1)S(1)} %copy.26), channel_id=1, source_target_pairs={{0,2},{2,4},{4,6},{6,8},{8,10},{10,12},{12,14},{14,16},{16,18},{18... | collective-permute-start | bytes 196616 | tf_op jit(solution)/shard_map/while/body/eval_jaxpr/ppermute | solution.py:15
  243.5 8.0 %collective-permute-start = (bf16[256,128]{1,0:T(8,128)(2,1)S(1)}, bf16[256,128]{1,0:T(8,128)(2,1)S(1)}, u32[]{:S(2)}, u32[]{:S(2)}) collective-permute-start(bf16[256,128]{1,0:T(8,128)(2,1)S(1)} %copy.26), channel_id=1, source_target_pairs={{0,2},{2,4},{4,6},{6,8},{8,10},{10,12},{12,14},{14,16},{16,18},{18... | collective-permute-start | bytes 196616 | tf_op jit(solution)/shard_map/while/body/eval_jaxpr/ppermute | solution.py:15
  251.6 8.0 %collective-permute-start = (bf16[256,128]{1,0:T(8,128)(2,1)S(1)}, bf16[256,128]{1,0:T(8,128)(2,1)S(1)}, u32[]{:S(2)}, u32[]{:S(2)}) collective-permute-start(bf16[256,128]{1,0:T(8,128)(2,1)S(1)} %copy.26), channel_id=1, source_target_pairs={{0,2},{2,4},{4,6},{6,8},{8,10},{10,12},{12,14},{14,16},{16,18},{18... | collective-permute-start | bytes 196616 | tf_op jit(solution)/shard_map/while/body/eval_jaxpr/ppermute | solution.py:15
  (34 other events, 259.9 us)
where the time goes:
time: 285 us; the launch traced here: 284 us
  waiting for transfers between devices  146 us (51%)
  matrix products  67.5 us (24%)
  other arithmetic  35.4 us (12%)
  local copies, waits for them, and re-layouts  12.4 us (4%)
  blocking collectives  10.8 us (4%)
  starting transfers between devices  9.67 us (3%)
    ppermute x64, waiting for transfers between devices, passed_along(): return lax.ppermute(value, axis, pairs)  146 us
    dot_general x32, matrix products, shard_logits(): lax.dot_general(flat_queries, key_slab, (((1,), (1,)), ((), ())), preferr...  67.5 us
    reduce_max x32, other arithmetic, shard_logits(): return jnp.max(masked.reshape(rows, key_count // BLOCK, BLOCK), axis=-1)  27.7 us
    psum x1, blocking collectives, body(): return lax.psum(output.astype(jnp.bfloat16), 'team').astype(jnp.float32)  10.8 us
    ppermute x64, starting transfers between devices, passed_along(): return lax.ppermute(value, axis, pairs)  9.67 us
  transfers between devices with their start and end apart: 64, of which 32 were waited for; matrix products, arithmetic and copies ran while one was open for 35% of the time, Pallas kernels for 0%

commit v1 on v0

v1 whole, which is shorter than its diff:
```python
import jax
import jax.numpy as jnp
from jax import lax
from jax.experimental import pallas as pl
from jax.experimental.pallas import tpu as pltpu
from jax.sharding import PartitionSpec as P

BLOCK = 64
CHUNK = 16
GROUP = 16
TILE = 512
MARK = 100.0
FAR = 1 << 30
mask_value = -8.0


def swapped(value, pairs, axis):
    return lax.ppermute(value, axis, pairs)


def kernel(tokens, heads, rank_ref, sorted_ref, base_ref, own_ref, other_ref, weight_ref, key_ref,
           seen_ref, at_ref, unsort_ref, spread_ref, mine_ref, theirs_ref, q_ref, w_ref, max_ref):
    half = tokens // 2
    tiles = key_ref.shape[0] // TILE
    head_size = key_ref.shape[1]
    per_tile = TILE // BLOCK
    parts = BLOCK // CHUNK

    def arrange(token, _):
        for ref, first in ((own_ref, 0), (other_ref, half)):
            to = pl.multiple_of(rank_ref[first + token] * heads, heads)
            start = pl.multiple_of(token * heads, heads)
            q_ref[pl.ds(to, heads), :] = ref[pl.ds(start, heads), :]
            w_ref[pl.ds(to, heads), :] = weight_ref[pl.ds(pl.multiple_of((first + token) * heads, heads), heads), :]
        return 0

    lax.fori_loop(0, half, arrange, 0)
    max_ref[...] = jnp.full(max_ref.shape, mask_value, jnp.float32)

    def tile_step(tile, _):
        first = base_ref[0] + tile * (per_tile * 4 * BLOCK)
        groups = jnp.int32(0)
        for group in range(tokens // GROUP):
            groups = groups + (sorted_ref[group * GROUP] >= first).astype(jnp.int32)
        keys = jnp.concatenate(
            [
                key_ref[pl.ds(pl.multiple_of(tile * TILE + block * BLOCK + part * CHUNK, CHUNK), CHUNK), :]
                for part in range(parts)
                for block in range(per_tile)
            ],
            axis=0,
        )

        def group_step(group):
            row = pl.multiple_of(group * GROUP * heads, GROUP * heads)
            token = pl.multiple_of(group * GROUP, GROUP)
            raw = lax.dot_general(
                q_ref[pl.ds(row, GROUP * heads), :], keys, (((1,), (1,)), ((), ())), preferred_element_type=jnp.float32
            )
            weights = w_ref[pl.ds(row, GROUP * heads), :]
            at = at_ref[pl.ds(token, GROUP), :]
            best = None
            for part in range(parts):
                lanes = slice(part * 128, part * 128 + 128)
                terms = jnp.maximum(raw[:, lanes], 0.0) * weights
                score = terms.reshape(GROUP, heads // 8, 8, 128).sum(1).sum(1)
                seen = seen_ref[tile, 0:1, lanes]
                score = jnp.where(seen <= at, score, mask_value)
                best = score if best is None else jnp.maximum(best, score)
            max_ref[tile, pl.ds(token, GROUP), :] = best

        def pair_step(pair, _):
            group_step(2 * pair)
            group_step(2 * pair + 1)
            return 0

        lax.fori_loop(0, groups // 2, pair_step, 0)

        @pl.when(groups % 2 == 1)
        def _():
            group_step(groups - 1)

        return 0

    lax.fori_loop(0, tiles, tile_step, 0)
    lane = lax.broadcasted_iota(jnp.int32, (tokens, 128), 1)
    found = [max_ref[tile] for tile in range(tiles)]
    step = CHUNK // 2
    while step:
        low = (lane & step) == 0
        if len(found) > 1:
            found = [
                jnp.where(
                    low,
                    jnp.maximum(a, pltpu.roll(a, 128 - step, 1)),
                    jnp.maximum(b, pltpu.roll(b, step, 1)),
                )
                for a, b in zip(found[::2], found[1::2])
            ]
        else:
            found = [jnp.maximum(found[0], pltpu.roll(found[0], 128 - step, 1))]
        step //= 2
    pooled = found[0].astype(jnp.bfloat16)
    ordered = jnp.dot(unsort_ref[...], pooled, preferred_element_type=jnp.float32).astype(jnp.bfloat16)
    placed = jnp.dot(ordered, spread_ref[...], preferred_element_type=jnp.float32).astype(jnp.bfloat16)
    mine_ref[...] = placed[:half]
    theirs_ref[...] = placed[half:]


def body(queries, head_weights, keys, query_pos, block_limits):
    shards = lax.axis_size("blk")
    me = lax.axis_index("blk")
    core = me % 2
    member = lax.axis_index("team")
    quarter = 2 * member + core
    count, heads, head_size = queries.shape
    tokens = 2 * count
    local_blocks = keys.shape[0] // BLOCK
    cores = [(i, i ^ 1) for i in range(shards)]

    own = queries.reshape(count * heads, head_size)
    other = swapped(own, cores, "blk")
    positions = jnp.concatenate([query_pos, swapped(query_pos, cores, "blk")])
    weights = jnp.concatenate([head_weights, swapped(head_weights, cores, "blk")]) * head_size ** (-0.5)
    wide = jnp.broadcast_to(weights.reshape(tokens * heads, 1), (tokens * heads, 128))

    blocks = keys.reshape(local_blocks, BLOCK, head_size)
    row = lax.broadcasted_iota(jnp.int32, (local_blocks, BLOCK, 1), 1)
    limit = block_limits[:, None, None]
    blocks = jnp.where((row == BLOCK - 1) & (limit < BLOCK), (limit + MARK).astype(keys.dtype), blocks)
    keep = lax.dynamic_index_in_dim(blocks, quarter, 0, False)
    give = lax.dynamic_index_in_dim(blocks, quarter ^ 1, 0, False)
    got = swapped(give, cores, "blk")
    piece = jnp.where(core == 0, jnp.stack([keep, got]), jnp.stack([got, keep]))
    chips = shards // 2
    groups = [[2 * chip + c for chip in range(chips)] for c in range(2)]
    gathered = lax.all_to_all(
        jnp.broadcast_to(piece[None], (chips,) + piece.shape), "blk", 0, 0, axis_index_groups=groups
    )
    slab = gathered.reshape(shards, BLOCK, head_size)

    mark = slab[:, BLOCK - 1, 0].astype(jnp.float32)
    filled = jnp.where(mark > MARK / 2, mark - MARK, float(BLOCK)).astype(jnp.int32)
    tiles = shards * BLOCK // TILE
    per_tile = TILE // BLOCK
    shape = (tiles, BLOCK // CHUNK, per_tile, CHUNK)
    axis = lambda n: lax.broadcasted_iota(jnp.int32, shape, n)
    offset = axis(1) * CHUNK + axis(3)
    key_at = (axis(0) * per_tile + axis(2)) * (local_blocks * BLOCK) + quarter * BLOCK + offset
    seen = jnp.where(offset < filled.reshape(tiles, 1, per_tile, 1), key_at, FAR).reshape(tiles, 1, TILE)

    index = jnp.arange(tokens, dtype=jnp.int32)
    ahead = (positions[None, :] > positions[:, None]) | (
        (positions[None, :] == positions[:, None]) & (index[None, :] < index[:, None])
    )
    rank = jnp.sum(ahead.astype(jnp.int32), axis=1)
    hit = rank[None, :] == index[:, None]
    in_order = jnp.sum(jnp.where(hit, positions[None, :], 0), axis=1)
    at = jnp.broadcast_to(in_order[:, None], (tokens, 128))
    unsort = (rank[:, None] == index[None, :]).astype(jnp.bfloat16)
    lane = jnp.arange(128, dtype=jnp.int32)
    tile_of = ((lane >> 3) & 1) + 2 * ((lane >> 2) & 1) + 4 * ((lane >> 1) & 1)
    block_of = tile_of * per_tile + lane // CHUNK
    column = block_of * local_blocks + quarter
    spread = ((lane % 2 == 0)[:, None] & (column[:, None] == jnp.arange(shards * local_blocks)[None, :])).astype(jnp.bfloat16)

    smem = pl.BlockSpec(memory_space=pltpu.SMEM)
    vmem = pl.BlockSpec(memory_space=pltpu.VMEM)
    result = jax.ShapeDtypeStruct((count, shards * local_blocks), jnp.bfloat16)
    mine, theirs = pl.pallas_call(
        lambda *refs: kernel(tokens, heads, *refs),
        out_shape=(result, result),
        in_specs=[smem] * 3 + [vmem] * 8,
        out_specs=(vmem, vmem),
        scratch_shapes=[
            pltpu.VMEM((tokens * heads, head_size), jnp.bfloat16),
            pltpu.VMEM((tokens * heads, 128), jnp.float32),
            pltpu.VMEM((tiles, tokens, 128), jnp.float32),
        ],
        compiler_params=pltpu.CompilerParams(vmem_limit_bytes=40 * 2**20),
        name="pooled_scores",
    )(rank, in_order, (quarter * BLOCK)[None].astype(jnp.int32), own, other, wide, slab.reshape(-1, head_size), seen, at, unsort, spread)
    chip = mine + swapped(theirs, cores, "blk")
    return (chip + swapped(chip, [(0, 1), (1, 0)], "team")).astype(jnp.float32)


def solution(mesh):
    in_specs = (P("blk", None, None), P("blk", None), P("blk", None), P("blk"), P("blk"))
    out_specs = P("blk", None)
    return jax.shard_map(body, mesh=mesh, in_specs=in_specs, out_specs=out_specs, check_vma=False)
```

time: 285 us -> 59.4 us (0.21)
  waiting for transfers between devices: 146 us -> 18.5 us
  matrix products: 67.5 us -> 0 us
  other arithmetic: 35.4 us -> 6.44 us
  Pallas kernels: 0 us -> 18.1 us
  blocking collectives: 10.8 us -> 0 us
  local copies, waits for them, and re-layouts: 12.4 us -> 2.98 us
  starting transfers between devices: 9.67 us -> 13.2 us
    ppermute x64 -> x6, waiting for transfers between devices: 146 us -> 3.93 us  [swapped(): return lax.ppermute(value, axis, pairs)]
    dot_general x32 -> x0, matrix products: 67.5 us -> none  [shard_logits(): lax.dot_general(flat_queries, key_slab, (((1,), (1,)), ((), ())), preferr...]
    reduce_max x32 -> x0, other arithmetic: 27.7 us -> none  [shard_logits(): return jnp.max(masked.reshape(rows, key_count // BLOCK, BLOCK), axis=-1)]
    pallas_call x0 -> x1, Pallas kernels: none -> 18.1 us  [body(): pl.pallas_call(lambda *refs: kernel(tokens, heads, *refs), out_shape=(res...]
    all_to_all x0 -> x1, waiting for transfers between devices: none -> 14.5 us  [body(): lax.all_to_all(jnp.broadcast_to(piece[None], (chips,) + piece.shape), 'bl...]
    psum x1 -> x0, blocking collectives: 10.8 us -> none  [body(): return lax.psum(output.astype(jnp.bfloat16), 'team').astype(jnp.float32)]
    all_to_all x0 -> x1, starting transfers between devices: none -> 8.75 us  [body(): lax.all_to_all(jnp.broadcast_to(piece[None], (chips,) + piece.shape), 'bl...]
    max x1 -> x0, local copies, waits for them, and re-layouts: 5.61 us -> none  [shard_logits(): raw = jax.nn.relu(raw).reshape(rows, heads, 256)]
  transfers between devices with their start and end apart: 64 -> 7, of which waited for: 32 -> 4; matrix products, arithmetic and copies ran while one was open for 35% -> 13% of each run, Pallas kernels for 0% -> 0%
where the time goes in v1:
time: 59.4 us
  waiting for transfers between devices  18.5 us (31%)
  Pallas kernels  18.1 us (30%)
  starting transfers between devices  13.2 us (22%)
  other arithmetic  6.44 us (11%)
  local copies, waits for them, and re-layouts  2.98 us (5%)
    pallas_call x1, Pallas kernels, body(): pl.pallas_call(lambda *refs: kernel(tokens, heads, *refs), out_shape=(res...  18.1 us
    all_to_all x1, waiting for transfers between devices, body(): lax.all_to_all(jnp.broadcast_to(piece[None], (chips,) + piece.shape), 'bl...  14.5 us
    all_to_all x1, starting transfers between devices, body(): lax.all_to_all(jnp.broadcast_to(piece[None], (chips,) + piece.shape), 'bl...  8.75 us
    ppermute x6, starting transfers between devices, swapped(): return lax.ppermute(value, axis, pairs)  4.48 us
    ppermute x6, waiting for transfers between devices, swapped(): return lax.ppermute(value, axis, pairs)  3.93 us
    convert_element_type x1, other arithmetic, body(): jnp.where(mark > MARK / 2, mark - MARK, float(BLOCK)).astype(jnp.int32)  1.27 us
    broadcast_in_dim x1, local copies, waits for them, and re-layouts, body(): jnp.broadcast_to(piece[None], (chips,) + piece.shape)  1.23 us
  transfers between devices with their start and end apart: 7, of which 4 were waited for; matrix products, arithmetic and copies ran while one was open for 13% of the time, Pallas kernels for 0%

profile of v1, /device:TPU:0, one launch (start us, length us, event | category | flops | bytes accessed | tf_op | source)
XLA Modules:
  0.0 59.4 jit_solution(17311372507594827934)
XLA Ops:
  0.0 0.5 collective-permute-start.2
  0.5 0.7 %add_convert_fusion.1 = bf16[4]{0:T(256)(128)(2,1)S(1)} fusion(s32[4]{0:T(128)} %param.9), kind=kLoop, calls=%fused_computation.46 | loop fusion | flops 12 | bytes 24 | tf_op jit(solution)/shard_map/convert_element_type | solution.py:130
  1.2 0.7 %broadcast_compare_fusion = pred[4]{0:T(512)(128)(4,1)S(1)} fusion(s32[4]{0:T(128)} %param.9), kind=kLoop, calls=%fused_computation.49 | loop fusion | flops 4 | bytes 20 | tf_op jit(solution)/shard_map/lt | solution.py:130
  1.8 0.1 broadcast_and_fusion
  1.9 0.9 %broadcast_select_fusion = bf16[4,64,128]{2,1,0:T(8,128)(2,1)S(1)} fusion(bf16[4,64,128]{2,1,0:T(8,128)(2,1)} %bitcast.14, pred[4,64]{1,0:T(4,128)(4,1)S(1)} %broadcast_and_fusion, bf16[4]{0:T(256)(128)(2,1)S(1)} %add_convert_fusion.1), kind=kLoop, calls=%fused_computation.14 | loop fusion | flops 32768 | bytes 131336 | tf_op jit(solution)/shard_map/jit(_where)/select_n | solution.py:130
  2.9 0.1 collective-permute-start.3
  3.0 0.5 collective-permute-start.1
  3.5 0.1 fusion.1.refs_10_
  3.6 0.5 collective-permute-done.3
  4.2 1.2 %broadcast_in_dim.47 = bf16[32,2,64,128]{3,2,1,0:T(8,128)(2,1)} broadcast(bf16[2,64,128]{2,1,0:T(8,128)(2,1)S(1)} %maximum_select_fusion), dimensions={1,2,3} | broadcast | bytes 1081344 | tf_op jit(solution)/shard_map/broadcast_in_dim | solution.py:138
  5.4 8.8 %all-to-all-start = ((bf16[32,2,64,128]{3,2,1,0:T(8,128)(2,1)}), bf16[32,2,64,128]{3,2,1,0:T(8,128)(2,1)S(1)}, u32[]{:S(2)}, u32[]{:S(2)}) async-start(bf16[32,2,64,128]{3,2,1,0:T(8,128)(2,1)} %broadcast_in_dim.47), calls=%async_computation | async-start | bytes 2097152 | tf_op jit(solution)/shard_map/all_to_all | solution.py:137
  14.2 0.1 add.127
  14.3 0.1 iota.75
  14.4 0.7 %pad_add_fusion = s32[128]{0:T(128)S(1)} fusion(s32[64]{0:T(128)S(1)} %collective-permute-done, s32[64]{0:T(128)} %param.8), kind=kLoop, calls=%fused_computation.43 | loop fusion | flops 128 | bytes 1024 | tf_op jit(solution)/shard_map/concatenate | solution.py:123
  15.1 0.2 convert_reduce_fusion.refs_0_
  15.3 0.1 fusion.4.refs_9_
  15.4 0.1 select_reduce_fusion.refs_1_
  15.5 0.8 %maximum_multiply_fusion = f32[128,64]{1,0:T(8,128)S(1)} fusion(f32[64,64]{1,0:T(8,128)S(1)} %collective-permute-done.2, f32[64,64]{1,0:T(8,128)} %param.6), kind=kLoop, calls=%fused_computation.4 | loop fusion | flops 16384 | bytes 65536 | tf_op jit(solution)/shard_map/mul | solution.py:124
  16.3 0.1 mul.84
  16.4 14.5 %all-to-all-done = bf16[32,2,64,128]{3,2,1,0:T(8,128)(2,1)S(1)} async-done(((bf16[32,2,64,128]{3,2,1,0:T(8,128)(2,1)}), bf16[32,2,64,128]{3,2,1,0:T(8,128)(2,1)S(1)}, u32[]{:S(2)}, u32[]{:S(2)}) %all-to-all-start) | async-done | bytes 1048608 | tf_op jit(solution)/shard_map/all_to_all | solution.py:137
  30.9 1.3 %fusion.6 = s32[64]{0:T(128)S(1)} fusion(bf16[64,64,128]{2,1,0:T(8,128)(2,1)S(1)} %bitcast.10), kind=kLoop, calls=%fused_computation.19 | loop fusion | flops 320 | bytes 384 | tf_op jit(solution)/shard_map/convert_element_type | solution.py:143
  32.2 0.1 convert_element_type.43
  32.3 0.1 lt.65
  32.4 0.1 lt.66
  32.5 0.1 compare_select_fusion.1.refs_7_
  32.7 1.1 %broadcast_in_dim.44.refs_5_ = f32[8192,128]{1,0:T(8,128)S(1)} broadcast(f32[8192]{0:T(1024)S(1)} %mul.84), dimensions={0} | broadcast | bytes 4227072 | tf_op jit(solution)/shard_map/broadcast_in_dim | solution.py:125
  33.8 18.1 %pooled_scores.1 = (bf16[64,256]{1,0:T(8,128)(2,1)S(1)}, bf16[64,256]{1,0:T(8,128)(2,1)S(1)}) custom-call(s32[128]{0:T(128)S(1)} %convert_reduce_fusion.refs_0_, s32[128]{0:T(128)S(1)} %select_reduce_fusion.refs_1_, s32[1]{0:T(128)} %bitcast.refs_2_, bf16[4096,128]{1,0:T(8,128)(2,1)S(1)} %bitcast.13, bf16[4096,128]{1,0:T(8,128)(2,1)S(1)} %collective-permute-done.1.refs_4_, ...), custom_call_target="tpu_custom_call" | custom-call | tf_op jit(solution)/shard_map/pooled_scores/pallas_call | solution.py:170
  51.9 0.1 collective-permute-start.4
  52.0 1.2 %collective-permute-done.4 = bf16[64,256]{1,0:T(8,128)(2,1)S(1)} collective-permute-done((bf16[64,256]{1,0:T(8,128)(2,1)S(1)}, bf16[64,256]{1,0:T(8,128)(2,1)S(1)}, u32[]{:S(2)}, u32[]{:S(2)}) %collective-permute-start.4) | collective-permute-done | bytes 32800 | tf_op jit(solution)/shard_map/ppermute | solution.py:18
  53.2 3.3 %collective-permute-start.5 = (bf16[64,256]{1,0:T(8,128)(2,1)S(1)}, bf16[64,256]{1,0:T(8,128)(2,1)S(1)}, u32[]{:S(2)}, u32[]{:S(2)}) collective-permute-start(bf16[64,256]{1,0:T(8,128)(2,1)S(1)} %add.138), channel_id=1, source_target_pairs={{0,1},{1,0},{2,3},{3,2},{4,5},{5,4},{6,7},{7,6},{8,9},{9,8},{10,11... | collective-permute-start | bytes 98312 | tf_op jit(solution)/shard_map/ppermute | solution.py:18
  56.5 2.2 %collective-permute-done.5 = bf16[64,256]{1,0:T(8,128)(2,1)S(1)} collective-permute-done((bf16[64,256]{1,0:T(8,128)(2,1)S(1)}, bf16[64,256]{1,0:T(8,128)(2,1)S(1)}, u32[]{:S(2)}, u32[]{:S(2)}) %collective-permute-start.5) | collective-permute-done | bytes 32800 | tf_op jit(solution)/shard_map/ppermute | solution.py:18
  58.7 0.6 %add_convert_fusion = f32[64,256]{1,0:T(8,128)} fusion(bf16[64,256]{1,0:T(8,128)(2,1)S(1)} %add.138, bf16[64,256]{1,0:T(8,128)(2,1)S(1)} %collective-permute-done.5), kind=kLoop, calls=%fused_computation.18 | loop fusion | flops 32768 | bytes 131072 | tf_op jit(solution)/shard_map/convert_element_type | solution.py:184
  (17 shorter events, 0.2 us)
Async XLA Ops:
  0.0 14.4 %collective-permute-start = (s32[64]{0:T(128)}, s32[64]{0:T(128)S(1)}, u32[]{:S(2)}, u32[]{:S(2)}) collective-permute-start(s32[64]{0:T(128)} %param.8), channel_id=1, source_target_pairs={{0,2},{2,0},{4,6},{6,4},{8,10},{10,8},{12,14},{14,12},{16,18},{18,... | collective-permute-start | bytes 776 | tf_op jit(solution)/shard_map/ppermute | solution.py:18
  0.0 15.5 %collective-permute-start.2 = (f32[64,64]{1,0:T(8,128)}, f32[64,64]{1,0:T(8,128)S(1)}, u32[]{:S(2)}, u32[]{:S(2)}) collective-permute-start(f32[64,64]{1,0:T(8,128)} %param.6), channel_id=1, source_target_pairs={{0,2},{2,0},{4,6},{6,4},{8,10},{10,8},{12,14},{14,12},{16,18},{18,... | collective-permute-start | bytes 49160 | tf_op jit(solution)/shard_map/ppermute | solution.py:18
  2.9 31.0 %copy-start = (bf16[64,64,128]{2,1,0:T(8,128)(2,1)S(1)}, bf16[64,64,128]{2,1,0:T(8,128)(2,1)}, u32[]{:S(2)}) copy-start(bf16[64,64,128]{2,1,0:T(8,128)(2,1)} %param.5) | copy-start | bytes 3145732
  2.9 1.3 %collective-permute-start.3 = (bf16[64,128]{1,0:T(8,128)(2,1)S(1)}, bf16[64,128]{1,0:T(8,128)(2,1)S(1)}, u32[]{:S(2)}, u32[]{:S(2)}) collective-permute-start(bf16[64,128]{1,0:T(8,128)(2,1)S(1)} %get-tuple-element.10), channel_id=1, source_target_pairs={{0,2},{2,0},{4,6},{6,4},{8,10},{10,8},{12,14},{14,12},{16,18},{18,... | collective-permute-start | bytes 49160 | tf_op jit(solution)/shard_map/ppermute | solution.py:18
  3.0 29.6 %collective-permute-start.1 = (bf16[4096,128]{1,0:T(8,128)(2,1)}, bf16[4096,128]{1,0:T(8,128)(2,1)S(1)}, u32[]{:S(2)}, u32[]{:S(2)}) collective-permute-start(bf16[4096,128]{1,0:T(8,128)(2,1)} %bitcast.12), channel_id=1, source_target_pairs={{0,2},{2,0},{4,6},{6,4},{8,10},{10,8},{12,14},{14,12},{16,18},{18,... | collective-permute-start | bytes 3145736 | tf_op jit(solution)/shard_map/ppermute | solution.py:18
  5.4 25.5 %all-to-all-start = ((bf16[32,2,64,128]{3,2,1,0:T(8,128)(2,1)}), bf16[32,2,64,128]{3,2,1,0:T(8,128)(2,1)S(1)}, u32[]{:S(2)}, u32[]{:S(2)}) async-start(bf16[32,2,64,128]{3,2,1,0:T(8,128)(2,1)} %broadcast_in_dim.47), calls=%async_computation | async-start | bytes 2097152 | tf_op jit(solution)/shard_map/all_to_all | solution.py:137
  51.9 1.3 %collective-permute-start.4 = (bf16[64,256]{1,0:T(8,128)(2,1)S(1)}, bf16[64,256]{1,0:T(8,128)(2,1)S(1)}, u32[]{:S(2)}, u32[]{:S(2)}) collective-permute-start(bf16[64,256]{1,0:T(8,128)(2,1)S(1)} %get-tuple-element.8), channel_id=1, source_target_pairs={{0,2},{2,0},{4,6},{6,4},{8,10},{10,8},{12,14},{14,12},{16,18},{18,... | collective-permute-start | bytes 98312 | tf_op jit(solution)/shard_map/ppermute | solution.py:18
  53.2 5.5 %collective-permute-start.5 = (bf16[64,256]{1,0:T(8,128)(2,1)S(1)}, bf16[64,256]{1,0:T(8,128)(2,1)S(1)}, u32[]{:S(2)}, u32[]{:S(2)}) collective-permute-start(bf16[64,256]{1,0:T(8,128)(2,1)S(1)} %add.138), channel_id=1, source_target_pairs={{0,1},{1,0},{2,3},{3,2},{4,5},{5,4},{6,7},{7,6},{8,9},{9,8},{10,11... | collective-permute-start | bytes 98312 | tf_op jit(solution)/shard_map/ppermute | solution.py:18

commit v2 on v1

v2 whole, which is shorter than its diff:
```python
import jax
import jax.numpy as jnp
from jax import lax
from jax.experimental import pallas as pl
from jax.experimental.pallas import tpu as pltpu
from jax.sharding import PartitionSpec as P

BLOCK = 64
CHUNK = 16
GROUP = 16
TILE = 256
PARTS = BLOCK // CHUNK
SLOTS = TILE // CHUNK
MARK = 100.0
SIDES = 4
STEPS = (0, 1, 3, 2)
FAR = 1 << 30
mask_value = -8.0


def swapped(value, pairs, axis):
    return lax.ppermute(value, axis, pairs)


def marked(limit_hbm, key_hbm, keep_ref, give_ref, limit_ref, sems):
    me = lax.axis_index("blk")
    keep = 2 * lax.axis_index("team") + me % 2
    picks = ((keep_ref, keep), (give_ref, keep + 1 - 2 * (keep % 2)))
    copies = [pltpu.make_async_copy(limit_hbm, limit_ref, sems.at[2])]
    for n, (ref, block) in enumerate(picks):
        start = pl.multiple_of(block * BLOCK, BLOCK)
        copies.append(pltpu.make_async_copy(key_hbm.at[pl.ds(start, BLOCK), :], ref, sems.at[n]))
    for copy in copies:
        copy.start()
    for copy in copies:
        copy.wait()
    for ref, block in picks:
        limit = limit_ref[block]
        last = ref[BLOCK - CHUNK:, :].astype(jnp.float32)
        row = lax.broadcasted_iota(jnp.int32, last.shape, 0)
        column = lax.broadcasted_iota(jnp.int32, last.shape, 1)
        mark = jnp.where(column == me, (limit + MARK).astype(jnp.float32), 0.0)
        unfilled = jnp.where(limit < BLOCK, CHUNK - 1, CHUNK)
        ref[BLOCK - CHUNK:, :] = jnp.where(row == unfilled, mark, last).astype(ref.dtype)


def arrange(tokens, heads, rank_ref, own_ref, other_ref, weight_ref, q_ref, w_ref):
    half = tokens // 2

    def step(token, _):
        for ref, first in ((own_ref, 0), (other_ref, half)):
            to = pl.multiple_of(rank_ref[first + token] * heads, heads)
            start = pl.multiple_of(token * heads, heads)
            q_ref[pl.ds(to, heads), :] = ref[pl.ds(start, heads), :]
            w_ref[pl.ds(to, heads), :] = weight_ref[pl.ds(pl.multiple_of((first + token) * heads, heads), heads), :]
        return 0

    lax.fori_loop(0, half, step, 0, unroll=2)


def lane_of(chunk):
    return (chunk & 7) * 16 + ((chunk >> 3) & 1) * 8 + ((chunk >> 4) & 1) * 4 + ((chunk >> 5) & 1) * 2 + ((chunk >> 6) & 1)


def folded(a, b, step, lane):
    return jnp.where(
        (lane & step) == 0,
        jnp.maximum(a, pltpu.roll(a, 128 - step, 1)),
        jnp.maximum(b, pltpu.roll(b, step, 1)),
    )


def scores(tokens, heads, stride, sorted_ref, place_ref, q_ref, w_ref, at_ref, row0_ref, row1_ref, row2_ref, row3_ref,
           pooled_ref, slab_ref, packed_ref, seen_ref, score_ref, max_ref, limit_ref, limit_smem, first_smem, sem, *accs):
    blocks = slab_ref.shape[0] // BLOCK
    piece = 2 * BLOCK
    per_row = SIDES * 2
    most = max_ref.shape[0]
    rows = GROUP // 2 * heads
    plane = place_ref[2]
    lane1 = lax.broadcasted_iota(jnp.int32, (1, 128), 1)
    lane = lax.broadcasted_iota(jnp.int32, (8, 128), 1)
    wide = lax.broadcasted_iota(jnp.int32, (tokens, 128), 1)

    for y_step, row_ref in zip(STEPS, (row0_ref, row1_ref, row2_ref, row3_ref)):
        y = (place_ref[0] + SIDES - y_step) % SIDES
        for spot, x_step in enumerate(STEPS):
            x = (place_ref[1] + SIDES - x_step) % SIDES
            to = pl.multiple_of((y * SIDES + x) * piece, piece)
            slab_ref[pl.ds(to, piece), :] = row_ref[spot * piece:(spot + 1) * piece, :]

    def shard_of(block):
        return (block // per_row) * (2 * per_row) + plane * per_row + block % per_row

    marks = slab_ref[pl.ds(BLOCK - CHUNK, CHUNK), :]
    for block in range(1, blocks):
        marks = jnp.maximum(marks, slab_ref[pl.ds(block * BLOCK + BLOCK - CHUNK, CHUNK), :])
    mark = marks.astype(jnp.float32)[CHUNK - 1:CHUNK, :]
    limit = jnp.where(mark > MARK / 2, mark - MARK, float(BLOCK)).astype(jnp.int32)
    limit_ref[...] = jnp.broadcast_to(limit, limit_ref.shape)
    copy = pltpu.make_async_copy(limit_ref, limit_smem, sem)
    copy.start()
    max_ref[...] = jnp.full(max_ref.shape, mask_value, jnp.float32)
    copy.wait()

    inside = lane % CHUNK

    def pack(block, at):
        shard = shard_of(block)
        filled = limit_smem[0, shard]
        first = place_ref[3] + shard * stride
        for part in range(PARTS):
            packed_ref[pl.ds(pl.multiple_of((at + part) * CHUNK, CHUNK), CHUNK), :] = slab_ref[
                pl.ds(pl.multiple_of(block * BLOCK + part * CHUNK, CHUNK), CHUNK), :
            ]
            offset = inside + part * CHUNK
            seen_ref[at + part] = jnp.where(offset < filled, offset + first, FAR)
            first_smem[at + part] = first + part * CHUNK
        return at + (filled + (CHUNK - 1)) // CHUNK

    total = lax.fori_loop(0, blocks, pack, jnp.int32(0), unroll=4)
    for slot in range(SLOTS):
        seen_ref[total + slot] = jnp.full((8, 128), FAR, jnp.int32)

    def count(tile):
        first = first_smem[tile * SLOTS]
        groups = jnp.int32(0)
        for group in range(tokens // GROUP):
            groups = groups + (sorted_ref[group * GROUP] >= first).astype(jnp.int32)
        return groups

    tiles = (total + SLOTS - 1) // SLOTS
    active = jnp.int32(0)
    for tile in range(most):
        active = active + ((tile < tiles) & (sorted_ref[0] >= first_smem[tile * SLOTS])).astype(jnp.int32)

    def push(tile):
        keys = packed_ref[pl.ds(pl.multiple_of(tile * TILE, TILE), TILE), :]
        keys = jnp.concatenate([keys, jnp.zeros_like(keys)], axis=1)
        for side in range(2):
            pltpu.matmul_push_rhs(keys, 0, side, transpose=True)

    def issue(group, pair, load=None):
        for side, acc in enumerate(pair):
            start = pl.multiple_of(group * (2 * rows) + side * rows, rows)
            left = q_ref[pl.ds(start, rows), :]
            pltpu.matmul_acc_lhs(acc, jnp.concatenate([left, left], axis=1), load)

    def finish(tile, group, pair):
        halves = []
        for side, acc in enumerate(pair):
            weights = w_ref[pl.ds(pl.multiple_of(group * (2 * rows) + side * rows, rows), rows), :]
            raw = pltpu.matmul_pop(acc)
            halves.append(
                [
                    (jnp.maximum(raw[:, part * 128:part * 128 + 128], 0.0) * weights).reshape(-1, heads // 8, 8, 128).sum(1)
                    for part in range(2)
                ]
            )
        for part in range(2):
            both = jnp.concatenate([halves[0][part], halves[1][part]], axis=0)
            score_ref[2 * tile + part, pl.ds(pl.multiple_of(group * GROUP, GROUP), GROUP), :] = both.sum(1)

    @pl.when(active > 0)
    def _():
        push(0)
        issue(0, accs[:2], 0)

        def tile_step(tile, _):
            groups = count(tile)
            odd = groups % 2
            push(jnp.minimum(tile + 1, active - 1))

            def pair_step(pair, _):
                issue(2 * pair + 1, accs[2:])
                finish(tile, 2 * pair, accs[:2])
                issue(2 * pair + 2, accs[:2])
                finish(tile, 2 * pair + 1, accs[2:])
                return 0

            lax.fori_loop(0, groups // 2 - 1 + odd, pair_step, 0)

            @pl.when(odd == 1)
            def _():
                finish(tile, groups - 1, accs[:2])
                issue(0, accs[:2], 0)

            @pl.when(odd == 0)
            def _():
                issue(groups - 1, accs[2:])
                finish(tile, groups - 2, accs[:2])
                issue(0, accs[:2], 0)
                finish(tile, groups - 1, accs[2:])

            return 0

        lax.fori_loop(0, active, tile_step, 0)
        for acc in accs[:2]:
            pltpu.matmul_pop(acc)

    def reduce_step(tile, _):
        seen = []
        for part in range(2):
            slot = tile * SLOTS + part * 8
            value = seen_ref[slot]
            for chunk in range(1, 8):
                value = jnp.where(lane // CHUNK == chunk, seen_ref[slot + chunk], value)
            seen.append(value[:1])
        found = [jnp.where(seen[part] <= at_ref[...], score_ref[2 * tile + part], mask_value) for part in range(2)]
        max_ref[tile] = folded(found[0], found[1], 8, wide)
        return 0

    lax.fori_loop(0, active, reduce_step, 0)
    found = [max_ref[tile] for tile in range(most)]
    for step in (4, 2, 1):
        found = [folded(a, b, step, wide) for a, b in zip(found[::2], found[1::2])]
    chunks = jnp.where((lane1 < 2 * blocks) & ((lane1 // per_row) % 2 == plane), (limit + (CHUNK - 1)) // CHUNK, 0)
    upto = chunks
    step = 1
    while step < 2 * blocks:
        upto = upto + jnp.where(lane1 >= step, pltpu.roll(upto, step, 1), 0)
        step *= 2
    before = upto - chunks
    pooled = None
    for part in range(PARTS):
        chunk = before + jnp.minimum(part, jnp.maximum(chunks - 1, 0))
        chunk = jnp.broadcast_to(jnp.minimum(chunk, most * SLOTS - 1), (tokens, 128))
        spot = lane_of(chunk)
        value = jnp.take_along_axis(found[0], spot, axis=1)
        if len(found) > 1:
            value = jnp.where(chunk < 128, value, jnp.take_along_axis(found[1], spot, axis=1))
        pooled = value if pooled is None else jnp.maximum(pooled, value)
    pooled_ref[...] = pooled.astype(jnp.bfloat16)


def restore(plane_ref, unsort_ref, spread_ref, near_ref, far_ref, mine_ref, theirs_ref):
    half = mine_ref.shape[0]
    lane = lax.broadcasted_iota(jnp.int32, near_ref.shape, 1)
    near = (lane // (2 * SIDES)) % 2 == plane_ref[0]
    pooled = jnp.where(near, near_ref[...].astype(jnp.float32), far_ref[...].astype(jnp.float32)).astype(jnp.bfloat16)
    ordered = jnp.dot(unsort_ref[...], pooled, preferred_element_type=jnp.float32).astype(jnp.bfloat16)
    placed = jnp.dot(ordered, spread_ref[...], preferred_element_type=jnp.float32).astype(jnp.bfloat16)
    mine_ref[...] = placed[:half]
    theirs_ref[...] = placed[half:]


def body(queries, head_weights, keys, query_pos, block_limits):
    shards = lax.axis_size("blk")
    me = lax.axis_index("blk")
    core = me % 2
    member = lax.axis_index("team")
    quarter = 2 * member + core
    count, heads, head_size = queries.shape
    tokens = 2 * count
    local_blocks = keys.shape[0] // BLOCK
    cores = [(i, i ^ 1) for i in range(shards)]
    smem = pl.BlockSpec(memory_space=pltpu.SMEM)
    vmem = pl.BlockSpec(memory_space=pltpu.VMEM)

    own = queries.reshape(count * heads, head_size)
    other = swapped(own, cores, "blk")
    other_pos = swapped(query_pos, cores, "blk")
    other_weights = swapped(head_weights, cores, "blk")

    piece_shape = jax.ShapeDtypeStruct((BLOCK, head_size), keys.dtype)
    keep, give = pl.pallas_call(
        marked,
        out_shape=(piece_shape, piece_shape),
        in_specs=[pl.BlockSpec(memory_space=pl.ANY)] * 2,
        out_specs=(vmem, vmem),
        scratch_shapes=[pltpu.SMEM(block_limits.shape, jnp.int32), pltpu.SemaphoreType.DMA((3,))],
        compiler_params=pltpu.CompilerParams(vmem_limit_bytes=4 * 2**20),
        name="marked",
    )(block_limits, keys)
    got = swapped(give, cores, "blk")
    piece = jnp.where(core == 0, jnp.stack([keep, got]), jnp.stack([got, keep]))

    def moved(y_step, z_step, x_step):
        pairs = []
        for source in range(shards):
            c, x, z, y = source % 2, source // 2 % SIDES, source // (2 * SIDES) % 2, source // (4 * SIDES)
            x, z, y = (x + x_step) % SIDES, (z + z_step) % 2, (y + y_step) % SIDES
            pairs.append((source, ((y * 2 + z) * SIDES + x) * 2 + c))
        return pairs

    piece = piece.reshape(2 * BLOCK, head_size)
    pieces = [piece] + [swapped(piece, moved(0, 0, step), "blk") for step in STEPS[1:]]

    piece, other_pos, other_weights = lax.optimization_barrier((piece, other_pos, other_weights))
    positions = jnp.concatenate([query_pos, other_pos])
    weights = jnp.concatenate([head_weights, other_weights]) * head_size ** (-0.5)
    wide = jnp.broadcast_to(weights.reshape(tokens * heads, 1), (tokens * heads, 128))

    index = jnp.arange(tokens, dtype=jnp.int32)
    ahead = (positions[None, :] > positions[:, None]) | (
        (positions[None, :] == positions[:, None]) & (index[None, :] < index[:, None])
    )
    rank = jnp.sum(ahead.astype(jnp.int32), axis=1)
    hit = rank[None, :] == index[:, None]
    in_order = jnp.sum(jnp.where(hit, positions[None, :], 0), axis=1)
    at = jnp.broadcast_to(in_order[:, None], (tokens, 128))
    unsort = (rank[:, None] == index[None, :]).astype(jnp.bfloat16)
    lane = jnp.arange(128, dtype=jnp.int32)
    target = lane * local_blocks + quarter
    spread = ((lane < shards)[:, None] & (target[:, None] == jnp.arange(shards * local_blocks)[None, :])).astype(jnp.bfloat16)

    q_rows, w_rows = pl.pallas_call(
        lambda *refs: arrange(tokens, heads, *refs),
        out_shape=(
            jax.ShapeDtypeStruct((tokens * heads, head_size), jnp.bfloat16),
            jax.ShapeDtypeStruct((tokens * heads, 128), jnp.float32),
        ),
        in_specs=[smem] + [vmem] * 3,
        out_specs=(vmem, vmem),
        compiler_params=pltpu.CompilerParams(vmem_limit_bytes=4 * 2**20),
        cost_estimate=pl.CostEstimate(flops=0, bytes_accessed=12 * 2**20, transcendentals=0),
        name="arranged",
    )(rank, own, other, wide)

    q_rows, w_rows, pieces = lax.optimization_barrier((q_rows, w_rows, pieces))
    row = jnp.concatenate(pieces)
    near = [row] + [swapped(row, moved(step, 0, 0), "blk") for step in STEPS[1:]]
    far = [swapped(value, moved(0, 1, 0), "blk") for value in near]

    result = jax.ShapeDtypeStruct((count, shards * local_blocks), jnp.bfloat16)
    slots = shards // 2 * PARTS
    accs = [pltpu.ACC(side)((GROUP // 2 * heads, TILE), jnp.float32) for _ in range(2) for side in range(2)]

    def kernel(*refs):
        pl.run_scoped(lambda *accs: scores(tokens, heads, local_blocks * BLOCK, *refs, *accs), *accs)

    def pooled(values, plane):
        place = jnp.stack([me // (4 * SIDES), me // 2 % SIDES, plane, quarter * BLOCK]).astype(jnp.int32)
        return pl.pallas_call(
            kernel,
            out_shape=jax.ShapeDtypeStruct((tokens, 128), jnp.bfloat16),
            in_specs=[smem] * 2 + [vmem] * 7,
            out_specs=vmem,
            scratch_shapes=[
                pltpu.VMEM((shards // 2 * BLOCK, head_size), jnp.bfloat16),
                pltpu.VMEM(((slots + PARTS) * CHUNK, head_size), jnp.bfloat16),
                pltpu.VMEM((slots + SLOTS, 8, 128), jnp.int32),
                pltpu.VMEM((2 * (slots // SLOTS), tokens, 128), jnp.float32),
                pltpu.VMEM((slots // SLOTS, tokens, 128), jnp.float32),
                pltpu.VMEM((8, 128), jnp.int32),
                pltpu.SMEM((8, 128), jnp.int32),
                pltpu.SMEM((slots + PARTS,), jnp.int32),
                pltpu.SemaphoreType.DMA(()),
            ],
            compiler_params=pltpu.CompilerParams(vmem_limit_bytes=8 * 2**20),
            cost_estimate=pl.CostEstimate(flops=2**32, bytes_accessed=8 * 2**20, transcendentals=0),
            name="pooled_scores",
        )(in_order, place, q_rows, w_rows, at, *values)

    plane = me // (2 * SIDES) % 2
    mine, theirs = pl.pallas_call(
        restore,
        out_shape=(result, result),
        in_specs=[smem] + [vmem] * 4,
        out_specs=(vmem, vmem),
        compiler_params=pltpu.CompilerParams(vmem_limit_bytes=4 * 2**20),
        name="restored",
    )(plane[None].astype(jnp.int32), unsort, spread, pooled(near, plane), pooled(far, 1 - plane))
    chip = mine + swapped(theirs, cores, "blk")
    return (chip + swapped(chip, [(0, 1), (1, 0)], "team")).astype(jnp.float32)


def solution(mesh):
    in_specs = (P("blk", None, None), P("blk", None), P("blk", None), P("blk"), P("blk"))
    out_specs = P("blk", None)

    def step(*args):
        with jax.sharding.use_abstract_mesh(mesh.abstract_mesh):
            return jax.shard_map(body, mesh=mesh, in_specs=in_specs, out_specs=out_specs, check_vma=False)(*args)

    return step
```

time: 59.4 us -> 48.8 us (0.82)
  waiting for transfers between devices: 18.5 us -> 3.9 us
  starting transfers between devices: 13.2 us -> 21.4 us
  other arithmetic: 6.44 us -> 2.71 us
  Pallas kernels: 18.1 us -> 17.3 us
    ppermute x6 -> x16, starting transfers between devices: 4.48 us -> 21.4 us  [swapped(): return lax.ppermute(value, axis, pairs)]
    all_to_all x1 -> x0, waiting for transfers between devices: 14.5 us -> none  [body(): lax.all_to_all(jnp.broadcast_to(piece[None], (chips,) + piece.shape), 'bl...]
    all_to_all x1 -> x0, starting transfers between devices: 8.75 us -> none  [body(): lax.all_to_all(jnp.broadcast_to(piece[None], (chips,) + piece.shape), 'bl...]
    convert_element_type x3 -> x1, other arithmetic: 2.04 us -> 0.1 us  [body(): ((lane < shards)[:, None] & (target[:, None] == jnp.arange(shards * local...]
    unnamed x2 -> x9, local copies, waits for them, and re-layouts: 0.01 us -> 1.61 us
    broadcast_in_dim x1 -> x0, local copies, waits for them, and re-layouts: 1.23 us -> none  [body(): jnp.broadcast_to(piece[None], (chips,) + piece.shape)]
    select_n x2 -> x0, other arithmetic: 1.04 us -> none  [the longest x1 0.94 us: body(): jnp.where((row == BLOCK - 1) & (limit < BLOCK), (limit + MARK).astype(key...]
    pallas_call x1 -> x5, Pallas kernels: 18.1 us -> 17.3 us  [the longest x2 15.2 us: pooled(): pl.pallas_call(kernel, out_shape=jax.ShapeDtypeStruct((tokens, 128), jnp....]
  transfers between devices with their start and end apart: 7 -> 16, of which waited for: 4 -> 4; matrix products, arithmetic and copies ran while one was open for 13% -> 7% of each run, Pallas kernels for 0% -> 20%
where the time goes in v2:
time: 48.8 us; the launch traced here: 48.4 us
  starting transfers between devices  21.4 us (44%)
  Pallas kernels  17.3 us (35%)
  waiting for transfers between devices  3.9 us (8%)
  local copies, waits for them, and re-layouts  2.9 us (6%)
  other arithmetic  2.71 us (6%)
    ppermute x16, starting transfers between devices, swapped(): return lax.ppermute(value, axis, pairs)  21.4 us
    pallas_call x2, Pallas kernels, pooled(): pl.pallas_call(kernel, out_shape=jax.ShapeDtypeStruct((tokens, 128), jnp....  15.2 us
    ppermute x16, waiting for transfers between devices, swapped(): return lax.ppermute(value, axis, pairs)  3.9 us
    unnamed x9, local copies, waits for them, and re-layouts  1.61 us
    pallas_call x1, Pallas kernels, body(): pl.pallas_call(lambda *refs: arrange(tokens, heads, *refs), out_shape=(ja...  1.15 us
    broadcast_in_dim x1, local copies, waits for them, and re-layouts, body(): jnp.broadcast_to(weights.reshape(tokens * heads, 1), (tokens * heads, 128))  1.13 us
  transfers between devices with their start and end apart: 16, of which 4 were waited for; matrix products, arithmetic and copies ran while one was open for 7% of the time, Pallas kernels for 20%

profile of v2, /device:TPU:0, one launch (start us, length us, event | category | flops | bytes accessed | tf_op | source)
XLA Modules:
  0.0 48.4 jit_solution(16279363776493655547)
XLA Ops:
  0.0 0.9 %copy-done.1 = bf16[256,128]{1,0:T(8,128)(2,1)S(1)} copy-done((bf16[256,128]{1,0:T(8,128)(2,1)S(1)}, bf16[256,128]{1,0:T(8,128)(2,1)}, u32[]{:S(2)}) %copy-start.1) | copy-done | bytes 65560
  0.9 0.7 %copy-done.2 = s32[4]{0:T(128)S(1)} copy-done((s32[4]{0:T(128)S(1)}, s32[4]{0:T(128)}, u32[]{:S(2)}) %copy-start.2) | copy-done | bytes 40
  1.6 0.6 %marked.1 = (bf16[64,128]{1,0:T(8,128)(2,1)S(1)}, bf16[64,128]{1,0:T(8,128)(2,1)S(1)}) custom-call(s32[4]{0:T(128)S(1)} %copy-done.2, bf16[256,128]{1,0:T(8,128)(2,1)S(1)} %copy-done.1), custom_call_target="tpu_custom_call" | custom-call | tf_op jit(solution)/shard_map/marked/pallas_call | solution.py:266
  2.2 0.5 %collective-permute-start = (bf16[64,128]{1,0:T(8,128)(2,1)S(1)}, bf16[64,128]{1,0:T(8,128)(2,1)S(1)}, u32[]{:S(2)}, u32[]{:S(2)}) collective-permute-start(bf16[64,128]{1,0:T(8,128)(2,1)S(1)} %get-tuple-element.20), channel_id=1, source_target_pairs={{0,2},{2,0},{4,6},{6,4},{8,10},{10,8},{12,14},{14,12},{16,18},{18,... | collective-permute-start | bytes 49160 | tf_op jit(solution)/shard_map/ppermute | solution.py:22
  2.7 0.1 collective-permute-start.2
  2.8 0.4 collective-permute-start.1
  3.2 0.1 fusion.1.spread_ref
  3.4 0.1 collective-permute-done
  3.5 1.6 %collective-permute-start.4 = (bf16[128,128]{1,0:T(8,128)(2,1)S(1)}, bf16[128,128]{1,0:T(8,128)(2,1)S(1)}, u32[]{:S(2)}, u32[]{:S(2)}) collective-permute-start(bf16[128,128]{1,0:T(8,128)(2,1)S(1)} %bitcast.12), channel_id=1, source_target_pairs={{0,4},{2,6},{4,8},{6,10},{8,12},{10,14},{12,0},{14,2},{16,20},{18,... | collective-permute-start | bytes 98312 | tf_op jit(solution)/shard_map/ppermute | solution.py:22
  5.1 1.7 %collective-permute-start.5 = (bf16[128,128]{1,0:T(8,128)(2,1)S(1)}, bf16[128,128]{1,0:T(8,128)(2,1)S(1)}, u32[]{:S(2)}, u32[]{:S(2)}) collective-permute-start(bf16[128,128]{1,0:T(8,128)(2,1)S(1)} %bitcast.13), channel_id=1, source_target_pairs={{0,12},{2,14},{4,0},{6,2},{8,4},{10,6},{12,8},{14,10},{16,28},{18,... | collective-permute-start | bytes 98312 | tf_op jit(solution)/shard_map/ppermute | solution.py:22
  6.8 1.9 %collective-permute-start.6 = (bf16[128,128]{1,0:T(8,128)(2,1)S(1)}, bf16[128,128]{1,0:T(8,128)(2,1)S(1)}, u32[]{:S(2)}, u32[]{:S(2)}) collective-permute-start(bf16[128,128]{1,0:T(8,128)(2,1)S(1)} %bitcast.14), channel_id=1, source_target_pairs={{0,8},{2,10},{4,12},{6,14},{8,0},{10,2},{12,4},{14,6},{16,24},{18,... | collective-permute-start | bytes 98312 | tf_op jit(solution)/shard_map/ppermute | solution.py:22
  8.7 0.7 %pad_add_fusion = s32[128]{0:T(128)S(1)} fusion(s32[64]{0:T(128)S(1)} %collective-permute-done.1, s32[64]{0:T(128)} %param.8), kind=kLoop, calls=%fused_computation.18 | loop fusion | flops 128 | bytes 1024 | tf_op jit(solution)/shard_map/concatenate | solution.py:290
  9.4 0.2 convert_reduce_fusion.refs_0_
  9.6 0.8 %maximum_multiply_fusion = f32[128,64]{1,0:T(8,128)S(1)} fusion(f32[64,64]{1,0:T(8,128)S(1)} %collective-permute-done.2, f32[64,64]{1,0:T(8,128)} %param.6), kind=kLoop, calls=%fused_computation.3 | loop fusion | flops 16384 | bytes 65536 | tf_op jit(solution)/shard_map/mul | solution.py:291
  10.5 1.1 %broadcast_in_dim.14.refs_3_ = f32[8192,128]{1,0:T(8,128)S(1)} broadcast(f32[8192]{0:T(1024)S(1)} %mul.36), dimensions={0} | broadcast | bytes 4227072 | tf_op jit(solution)/shard_map/broadcast_in_dim | solution.py:292
  11.6 1.1 %arranged.1 = (bf16[8192,128]{1,0:T(8,128)(2,1)S(1)}, f32[8192,128]{1,0:T(8,128)S(1)}) custom-call(s32[128]{0:T(128)S(1)} %convert_reduce_fusion.refs_0_, bf16[4096,128]{1,0:T(8,128)(2,1)S(1)} %bitcast.10, bf16[4096,128]{1,0:T(8,128)(2,1)S(1)} %collective-permute-done.3.refs_2_, f32[8192,128]{1,0:T(8,128)S(1)} %broadcast_in_dim.14.refs_3_), custom_call_target="tpu_custom_call" | custom-call | bytes 12582912 | tf_op jit(solution)/shard_map/arranged/pallas_call | solution.py:307
  12.9 1.6 %collective-permute-start.7 = (bf16[512,128]{1,0:T(8,128)(2,1)S(1)}, bf16[512,128]{1,0:T(8,128)(2,1)S(1)}, u32[]{:S(2)}, u32[]{:S(2)}) collective-permute-start(bf16[512,128]{1,0:T(8,128)(2,1)S(1)} %constant_dynamic-update-slice_fusion.refs_5_), channel_id=1, source_target_pairs={{0,32},{2,34},{4,36},{6,38},{8,40},{10,42},{12,44},{14,46},{16,48}... | collective-permute-start | bytes 393224 | tf_op jit(solution)/shard_map/ppermute | solution.py:22
  14.5 1.7 %collective-permute-start.8 = (bf16[512,128]{1,0:T(8,128)(2,1)S(1)}, bf16[512,128]{1,0:T(8,128)(2,1)S(1)}, u32[]{:S(2)}, u32[]{:S(2)}) collective-permute-start(bf16[512,128]{1,0:T(8,128)(2,1)S(1)} %constant_dynamic-update-slice_fusion.refs_5_), channel_id=1, source_target_pairs={{0,96},{2,98},{4,100},{6,102},{8,104},{10,106},{12,108},{14,110},{... | collective-permute-start | bytes 393224 | tf_op jit(solution)/shard_map/ppermute | solution.py:22
  16.2 2.0 %collective-permute-start.9 = (bf16[512,128]{1,0:T(8,128)(2,1)S(1)}, bf16[512,128]{1,0:T(8,128)(2,1)S(1)}, u32[]{:S(2)}, u32[]{:S(2)}) collective-permute-start(bf16[512,128]{1,0:T(8,128)(2,1)S(1)} %constant_dynamic-update-slice_fusion.refs_5_), channel_id=1, source_target_pairs={{0,64},{2,66},{4,68},{6,70},{8,72},{10,74},{12,76},{14,78},{16,80}... | collective-permute-start | bytes 393224 | tf_op jit(solution)/shard_map/ppermute | solution.py:22
  18.2 0.1 select_reduce_fusion.refs_0_
  18.4 2.0 %collective-permute-start.10 = (bf16[512,128]{1,0:T(8,128)(2,1)S(1)}, bf16[512,128]{1,0:T(8,128)(2,1)S(1)}, u32[]{:S(2)}, u32[]{:S(2)}) collective-permute-start(bf16[512,128]{1,0:T(8,128)(2,1)S(1)} %constant_dynamic-update-slice_fusion.refs_5_), channel_id=1, source_target_pairs={{0,16},{2,18},{4,20},{6,22},{8,24},{10,26},{12,28},{14,30},{16,0},... | collective-permute-start | bytes 393224 | tf_op jit(solution)/shard_map/ppermute | solution.py:22
  20.4 0.7 %collective-permute-start.11 = (bf16[512,128]{1,0:T(8,128)(2,1)S(1)}, bf16[512,128]{1,0:T(8,128)(2,1)S(1)}, u32[]{:S(2)}, u32[]{:S(2)}) collective-permute-start(bf16[512,128]{1,0:T(8,128)(2,1)S(1)} %collective-permute-done.7.refs_6_), channel_id=1, source_target_pairs={{0,16},{2,18},{4,20},{6,22},{8,24},{10,26},{12,28},{14,30},{16,0},... | collective-permute-start | bytes 393224 | tf_op jit(solution)/shard_map/ppermute | solution.py:22
  21.1 1.5 %collective-permute-start.12 = (bf16[512,128]{1,0:T(8,128)(2,1)S(1)}, bf16[512,128]{1,0:T(8,128)(2,1)S(1)}, u32[]{:S(2)}, u32[]{:S(2)}) collective-permute-start(bf16[512,128]{1,0:T(8,128)(2,1)S(1)} %collective-permute-done.8.refs_7_), channel_id=1, source_target_pairs={{0,16},{2,18},{4,20},{6,22},{8,24},{10,26},{12,28},{14,30},{16,0},... | collective-permute-start | bytes 393224 | tf_op jit(solution)/shard_map/ppermute | solution.py:22
  22.5 0.7 %collective-permute-done.9.refs_8_ = bf16[512,128]{1,0:T(8,128)(2,1)S(1)} collective-permute-done((bf16[512,128]{1,0:T(8,128)(2,1)S(1)}, bf16[512,128]{1,0:T(8,128)(2,1)S(1)}, u32[]{:S(2)}, u32[]{:S(2)}) %collective-permute-start.9) | collective-permute-done | bytes 131104 | tf_op jit(solution)/shard_map/ppermute | solution.py:22
  23.2 1.9 %collective-permute-start.13 = (bf16[512,128]{1,0:T(8,128)(2,1)S(1)}, bf16[512,128]{1,0:T(8,128)(2,1)S(1)}, u32[]{:S(2)}, u32[]{:S(2)}) collective-permute-start(bf16[512,128]{1,0:T(8,128)(2,1)S(1)} %collective-permute-done.9.refs_8_), channel_id=1, source_target_pairs={{0,16},{2,18},{4,20},{6,22},{8,24},{10,26},{12,28},{14,30},{16,0},... | collective-permute-start | bytes 393224 | tf_op jit(solution)/shard_map/ppermute | solution.py:22
  25.2 8.1 %pooled_scores.2.near_ref = bf16[128,128]{1,0:T(8,128)(2,1)S(1)} custom-call(s32[128]{0:T(128)S(1)} %select_reduce_fusion.refs_0_, s32[4]{0:T(128)S(1)} %get-tuple-element.33.refs_1_, bf16[8192,128]{1,0:T(8,128)(2,1)S(1)} %get-tuple-element.25.refs_2_, f32[8192,128]{1,0:T(8,128)S(1)} %get-tuple-element.26.refs_3_, s32[128,128]{1,0:T(8,128)S(1)} %broadcast_in_dim.15.refs_4_, ...), custom_call_target="tpu_custom_call" | custom-call | flops 4294967296 | bytes 8388608 | tf_op jit(solution)/shard_map/pooled_scores/pallas_call | solution.py:334
  33.3 7.1 %pooled_scores.3.far_ref = bf16[128,128]{1,0:T(8,128)(2,1)S(1)} custom-call(s32[128]{0:T(128)S(1)} %select_reduce_fusion.refs_0_, s32[4]{0:T(128)S(1)} %get-tuple-element.34.refs_1_, bf16[8192,128]{1,0:T(8,128)(2,1)S(1)} %get-tuple-element.25.refs_2_, f32[8192,128]{1,0:T(8,128)S(1)} %get-tuple-element.26.refs_3_, s32[128,128]{1,0:T(8,128)S(1)} %broadcast_in_dim.15.refs_4_, ...), custom_call_target="tpu_custom_call" | custom-call | flops 4294967296 | bytes 8388608 | tf_op jit(solution)/shard_map/pooled_scores/pallas_call | solution.py:334
  40.4 0.3 restored.1
  40.8 1.2 %collective-permute-done.14 = bf16[64,256]{1,0:T(8,128)(2,1)S(1)} collective-permute-done((bf16[64,256]{1,0:T(8,128)(2,1)S(1)}, bf16[64,256]{1,0:T(8,128)(2,1)S(1)}, u32[]{:S(2)}, u32[]{:S(2)}) %collective-permute-start.14) | collective-permute-done | bytes 32800 | tf_op jit(solution)/shard_map/ppermute | solution.py:22
  42.0 3.8 %collective-permute-start.15 = (bf16[64,256]{1,0:T(8,128)(2,1)S(1)}, bf16[64,256]{1,0:T(8,128)(2,1)S(1)}, u32[]{:S(2)}, u32[]{:S(2)}) collective-permute-start(bf16[64,256]{1,0:T(8,128)(2,1)S(1)} %add.39), channel_id=1, source_target_pairs={{0,1},{1,0},{2,3},{3,2},{4,5},{5,4},{6,7},{7,6},{8,9},{9,8},{10,11... | collective-permute-start | bytes 98312 | tf_op jit(solution)/shard_map/ppermute | solution.py:22
  45.9 1.9 %collective-permute-done.15 = bf16[64,256]{1,0:T(8,128)(2,1)S(1)} collective-permute-done((bf16[64,256]{1,0:T(8,128)(2,1)S(1)}, bf16[64,256]{1,0:T(8,128)(2,1)S(1)}, u32[]{:S(2)}, u32[]{:S(2)}) %collective-permute-start.15) | collective-permute-done | bytes 32800 | tf_op jit(solution)/shard_map/ppermute | solution.py:22
  47.8 0.6 %add_convert_fusion = f32[64,256]{1,0:T(8,128)} fusion(bf16[64,256]{1,0:T(8,128)(2,1)S(1)} %add.39, bf16[64,256]{1,0:T(8,128)(2,1)S(1)} %collective-permute-done.15), kind=kLoop, calls=%fused_computation.13 | loop fusion | flops 32768 | bytes 131072 | tf_op jit(solution)/shard_map/convert_element_type | solution.py:365
  (30 shorter events, 0.5 us)
Async XLA Ops:
  0.0 11.6 %copy-start = (bf16[64,64,128]{2,1,0:T(8,128)(2,1)S(1)}, bf16[64,64,128]{2,1,0:T(8,128)(2,1)}, u32[]{:S(2)}) copy-start(bf16[64,64,128]{2,1,0:T(8,128)(2,1)} %param.5) | copy-start | bytes 3145732
  0.0 10.5 %collective-permute-start.3 = (bf16[4096,128]{1,0:T(8,128)(2,1)}, bf16[4096,128]{1,0:T(8,128)(2,1)S(1)}, u32[]{:S(2)}, u32[]{:S(2)}) collective-permute-start(bf16[4096,128]{1,0:T(8,128)(2,1)} %bitcast.9), channel_id=1, source_target_pairs={{0,2},{2,0},{4,6},{6,4},{8,10},{10,8},{12,14},{14,12},{16,18},{18,... | collective-permute-start | bytes 3145736 | tf_op jit(solution)/shard_map/ppermute | solution.py:22
  0.0 0.9 %copy-start.1 = (bf16[256,128]{1,0:T(8,128)(2,1)S(1)}, bf16[256,128]{1,0:T(8,128)(2,1)}, u32[]{:S(2)}) copy-start(bf16[256,128]{1,0:T(8,128)(2,1)} %key_hbm.1) | copy-start | bytes 196612
  0.9 0.7 %copy-start.2 = (s32[4]{0:T(128)S(1)}, s32[4]{0:T(128)}, u32[]{:S(2)}) copy-start(s32[4]{0:T(128)} %limit_hbm.1) | copy-start | bytes 52
  2.2 1.3 %collective-permute-start = (bf16[64,128]{1,0:T(8,128)(2,1)S(1)}, bf16[64,128]{1,0:T(8,128)(2,1)S(1)}, u32[]{:S(2)}, u32[]{:S(2)}) collective-permute-start(bf16[64,128]{1,0:T(8,128)(2,1)S(1)} %get-tuple-element.20), channel_id=1, source_target_pairs={{0,2},{2,0},{4,6},{6,4},{8,10},{10,8},{12,14},{14,12},{16,18},{18,... | collective-permute-start | bytes 49160 | tf_op jit(solution)/shard_map/ppermute | solution.py:22
  2.7 6.0 %collective-permute-start.2 = (f32[64,64]{1,0:T(8,128)}, f32[64,64]{1,0:T(8,128)S(1)}, u32[]{:S(2)}, u32[]{:S(2)}) collective-permute-start(f32[64,64]{1,0:T(8,128)} %param.6), channel_id=1, source_target_pairs={{0,2},{2,0},{4,6},{6,4},{8,10},{10,8},{12,14},{14,12},{16,18},{18,... | collective-permute-start | bytes 49160 | tf_op jit(solution)/shard_map/ppermute | solution.py:22
  2.8 4.0 %collective-permute-start.1 = (s32[64]{0:T(128)}, s32[64]{0:T(128)S(1)}, u32[]{:S(2)}, u32[]{:S(2)}) collective-permute-start(s32[64]{0:T(128)} %param.8), channel_id=1, source_target_pairs={{0,2},{2,0},{4,6},{6,4},{8,10},{10,8},{12,14},{14,12},{16,18},{18,... | collective-permute-start | bytes 776 | tf_op jit(solution)/shard_map/ppermute | solution.py:22
  3.5 9.3 %collective-permute-start.4 = (bf16[128,128]{1,0:T(8,128)(2,1)S(1)}, bf16[128,128]{1,0:T(8,128)(2,1)S(1)}, u32[]{:S(2)}, u32[]{:S(2)}) collective-permute-start(bf16[128,128]{1,0:T(8,128)(2,1)S(1)} %bitcast.12), channel_id=1, source_target_pairs={{0,4},{2,6},{4,8},{6,10},{8,12},{10,14},{12,0},{14,2},{16,20},{18,... | collective-permute-start | bytes 98312 | tf_op jit(solution)/shard_map/ppermute | solution.py:22
  5.1 7.7 %collective-permute-start.5 = (bf16[128,128]{1,0:T(8,128)(2,1)S(1)}, bf16[128,128]{1,0:T(8,128)(2,1)S(1)}, u32[]{:S(2)}, u32[]{:S(2)}) collective-permute-start(bf16[128,128]{1,0:T(8,128)(2,1)S(1)} %bitcast.13), channel_id=1, source_target_pairs={{0,12},{2,14},{4,0},{6,2},{8,4},{10,6},{12,8},{14,10},{16,28},{18,... | collective-permute-start | bytes 98312 | tf_op jit(solution)/shard_map/ppermute | solution.py:22
  6.8 6.0 %collective-permute-start.6 = (bf16[128,128]{1,0:T(8,128)(2,1)S(1)}, bf16[128,128]{1,0:T(8,128)(2,1)S(1)}, u32[]{:S(2)}, u32[]{:S(2)}) collective-permute-start(bf16[128,128]{1,0:T(8,128)(2,1)S(1)} %bitcast.14), channel_id=1, source_target_pairs={{0,8},{2,10},{4,12},{6,14},{8,0},{10,2},{12,4},{14,6},{16,24},{18,... | collective-permute-start | bytes 98312 | tf_op jit(solution)/shard_map/ppermute | solution.py:22
  12.9 7.5 %collective-permute-start.7 = (bf16[512,128]{1,0:T(8,128)(2,1)S(1)}, bf16[512,128]{1,0:T(8,128)(2,1)S(1)}, u32[]{:S(2)}, u32[]{:S(2)}) collective-permute-start(bf16[512,128]{1,0:T(8,128)(2,1)S(1)} %constant_dynamic-update-slice_fusion.refs_5_), channel_id=1, source_target_pairs={{0,32},{2,34},{4,36},{6,38},{8,40},{10,42},{12,44},{14,46},{16,48}... | collective-permute-start | bytes 393224 | tf_op jit(solution)/shard_map/ppermute | solution.py:22
  14.5 6.5 %collective-permute-start.8 = (bf16[512,128]{1,0:T(8,128)(2,1)S(1)}, bf16[512,128]{1,0:T(8,128)(2,1)S(1)}, u32[]{:S(2)}, u32[]{:S(2)}) collective-permute-start(bf16[512,128]{1,0:T(8,128)(2,1)S(1)} %constant_dynamic-update-slice_fusion.refs_5_), channel_id=1, source_target_pairs={{0,96},{2,98},{4,100},{6,102},{8,104},{10,106},{12,108},{14,110},{... | collective-permute-start | bytes 393224 | tf_op jit(solution)/shard_map/ppermute | solution.py:22
  16.2 7.0 %collective-permute-start.9 = (bf16[512,128]{1,0:T(8,128)(2,1)S(1)}, bf16[512,128]{1,0:T(8,128)(2,1)S(1)}, u32[]{:S(2)}, u32[]{:S(2)}) collective-permute-start(bf16[512,128]{1,0:T(8,128)(2,1)S(1)} %constant_dynamic-update-slice_fusion.refs_5_), channel_id=1, source_target_pairs={{0,64},{2,66},{4,68},{6,70},{8,72},{10,74},{12,76},{14,78},{16,80}... | collective-permute-start | bytes 393224 | tf_op jit(solution)/shard_map/ppermute | solution.py:22
  18.4 14.9 %collective-permute-start.10 = (bf16[512,128]{1,0:T(8,128)(2,1)S(1)}, bf16[512,128]{1,0:T(8,128)(2,1)S(1)}, u32[]{:S(2)}, u32[]{:S(2)}) collective-permute-start(bf16[512,128]{1,0:T(8,128)(2,1)S(1)} %constant_dynamic-update-slice_fusion.refs_5_), channel_id=1, source_target_pairs={{0,16},{2,18},{4,20},{6,22},{8,24},{10,26},{12,28},{14,30},{16,0},... | collective-permute-start | bytes 393224 | tf_op jit(solution)/shard_map/ppermute | solution.py:22
  20.4 12.9 %collective-permute-start.11 = (bf16[512,128]{1,0:T(8,128)(2,1)S(1)}, bf16[512,128]{1,0:T(8,128)(2,1)S(1)}, u32[]{:S(2)}, u32[]{:S(2)}) collective-permute-start(bf16[512,128]{1,0:T(8,128)(2,1)S(1)} %collective-permute-done.7.refs_6_), channel_id=1, source_target_pairs={{0,16},{2,18},{4,20},{6,22},{8,24},{10,26},{12,28},{14,30},{16,0},... | collective-permute-start | bytes 393224 | tf_op jit(solution)/shard_map/ppermute | solution.py:22
  21.1 12.2 %collective-permute-start.12 = (bf16[512,128]{1,0:T(8,128)(2,1)S(1)}, bf16[512,128]{1,0:T(8,128)(2,1)S(1)}, u32[]{:S(2)}, u32[]{:S(2)}) collective-permute-start(bf16[512,128]{1,0:T(8,128)(2,1)S(1)} %collective-permute-done.8.refs_7_), channel_id=1, source_target_pairs={{0,16},{2,18},{4,20},{6,22},{8,24},{10,26},{12,28},{14,30},{16,0},... | collective-permute-start | bytes 393224 | tf_op jit(solution)/shard_map/ppermute | solution.py:22
  23.2 10.1 %collective-permute-start.13 = (bf16[512,128]{1,0:T(8,128)(2,1)S(1)}, bf16[512,128]{1,0:T(8,128)(2,1)S(1)}, u32[]{:S(2)}, u32[]{:S(2)}) collective-permute-start(bf16[512,128]{1,0:T(8,128)(2,1)S(1)} %collective-permute-done.9.refs_8_), channel_id=1, source_target_pairs={{0,16},{2,18},{4,20},{6,22},{8,24},{10,26},{12,28},{14,30},{16,0},... | collective-permute-start | bytes 393224 | tf_op jit(solution)/shard_map/ppermute | solution.py:22
  40.7 1.3 %collective-permute-start.14 = (bf16[64,256]{1,0:T(8,128)(2,1)S(1)}, bf16[64,256]{1,0:T(8,128)(2,1)S(1)}, u32[]{:S(2)}, u32[]{:S(2)}) collective-permute-start(bf16[64,256]{1,0:T(8,128)(2,1)S(1)} %get-tuple-element.32), channel_id=1, source_target_pairs={{0,2},{2,0},{4,6},{6,4},{8,10},{10,8},{12,14},{14,12},{16,18},{18,... | collective-permute-start | bytes 98312 | tf_op jit(solution)/shard_map/ppermute | solution.py:22
  42.0 5.7 %collective-permute-start.15 = (bf16[64,256]{1,0:T(8,128)(2,1)S(1)}, bf16[64,256]{1,0:T(8,128)(2,1)S(1)}, u32[]{:S(2)}, u32[]{:S(2)}) collective-permute-start(bf16[64,256]{1,0:T(8,128)(2,1)S(1)} %add.39), channel_id=1, source_target_pairs={{0,1},{1,0},{2,3},{3,2},{4,5},{5,4},{6,7},{7,6},{8,9},{9,8},{10,11... | collective-permute-start | bytes 98312 | tf_op jit(solution)/shard_map/ppermute | solution.py:22

commit v3 on v2

--- a/solution.py
+++ b/solution.py
@@ -44,18 +44,18 @@
         ref[BLOCK - CHUNK:, :] = jnp.where(row == unfilled, mark, last).astype(ref.dtype)
 
 
-def arrange(tokens, heads, rank_ref, own_ref, other_ref, weight_ref, q_ref, w_ref):
+def arrange(tokens, heads, scale, rank_ref, own_ref, other_ref, own_weight_ref, other_weight_ref, q_ref, w_ref):
     half = tokens // 2
 
     def step(token, _):
-        for ref, first in ((own_ref, 0), (other_ref, half)):
+        start = pl.multiple_of(token * heads, heads)
+        for ref, weight_ref, first in ((own_ref, own_weight_ref, 0), (other_ref, other_weight_ref, half)):
             to = pl.multiple_of(rank_ref[first + token] * heads, heads)
-            start = pl.multiple_of(token * heads, heads)
             q_ref[pl.ds(to, heads), :] = ref[pl.ds(start, heads), :]
-            w_ref[pl.ds(to, heads), :] = weight_ref[pl.ds(pl.multiple_of((first + token) * heads, heads), heads), :]
+            w_ref[pl.ds(to, heads), :] = weight_ref[pl.ds(start, heads), :] * scale
         return 0
 
-    lax.fori_loop(0, half, step, 0, unroll=2)
+    lax.fori_loop(0, half, step, 0, unroll=4)
 
 
 def lane_of(chunk):
@@ -70,8 +70,8 @@
     )
 
 
-def scores(tokens, heads, stride, sorted_ref, place_ref, q_ref, w_ref, at_ref, row0_ref, row1_ref, row2_ref, row3_ref,
-           pooled_ref, slab_ref, packed_ref, seen_ref, score_ref, max_ref, limit_ref, limit_smem, first_smem, sem, *accs):
+def scores(tokens, heads, stride, sorted_ref, place_ref, q_ref, w_ref, at_ref, row_ref, rest_ref,
+           pooled_ref, slab_ref, packed_ref, score_ref, max_ref, first_smem, *accs):
     blocks = slab_ref.shape[0] // BLOCK
     piece = 2 * BLOCK
     per_row = SIDES * 2
@@ -82,48 +82,53 @@
     lane = lax.broadcasted_iota(jnp.int32, (8, 128), 1)
     wide = lax.broadcasted_iota(jnp.int32, (tokens, 128), 1)
 
-    for y_step, row_ref in zip(STEPS, (row0_ref, row1_ref, row2_ref, row3_ref)):
+    marks = None
+    for ref in (row_ref, rest_ref):
+        for end in range(BLOCK, ref.shape[0] + 1, BLOCK):
+            last = ref[end - CHUNK:end, :]
+            marks = last if marks is None else jnp.maximum(marks, last)
+    mark = marks.astype(jnp.float32)[CHUNK - 1:CHUNK, :]
+    limit = jnp.where(mark > MARK / 2, mark - MARK, float(BLOCK)).astype(jnp.int32)
+    chunks = jnp.where((lane1 < 2 * blocks) & ((lane1 // per_row) % 2 == plane), (limit + (CHUNK - 1)) // CHUNK, 0)
+    upto = chunks
+    step = 1
+    while step < 2 * blocks:
+        upto = upto + jnp.where(lane1 >= step, pltpu.roll(upto, step, 1), 0)
+        step *= 2
+    before = upto - chunks
+    square = (128, 128)
+    down = jnp.broadcast_to(upto.astype(jnp.float32), square).T
+    at_chunk = lax.broadcasted_iota(jnp.int32, square, 1).astype(jnp.float32)
+    earlier = (down <= at_chunk) & (lax.broadcasted_iota(jnp.int32, square, 0) < 2 * blocks)
+    shard = jnp.sum(earlier.astype(jnp.float32), axis=0, keepdims=True).astype(jnp.int32)
+    shard = jnp.broadcast_to(jnp.minimum(shard, 2 * blocks - 1), (8, 128))
+    skipped = (lane - jnp.take_along_axis(jnp.broadcast_to(before, (8, 128)), shard, axis=1)) * CHUNK
+    position = place_ref[3] + shard * stride + skipped
+    held = jnp.take_along_axis(jnp.broadcast_to(limit, (8, 128)), shard, axis=1) - skipped
+    total = jnp.max(upto, axis=1, keepdims=True)
+    held = jnp.where(lane < total, held, 0)
+    length = SIDES * piece
+    for y_step, ref, start in zip(STEPS, (row_ref, rest_ref, rest_ref, rest_ref), (0, 0, length, 2 * length)):
         y = (place_ref[0] + SIDES - y_step) % SIDES
         for spot, x_step in enumerate(STEPS):
             x = (place_ref[1] + SIDES - x_step) % SIDES
             to = pl.multiple_of((y * SIDES + x) * piece, piece)
-            slab_ref[pl.ds(to, piece), :] = row_ref[spot * piece:(spot + 1) * piece, :]
-
-    def shard_of(block):
-        return (block // per_row) * (2 * per_row) + plane * per_row + block % per_row
-
-    marks = slab_ref[pl.ds(BLOCK - CHUNK, CHUNK), :]
-    for block in range(1, blocks):
-        marks = jnp.maximum(marks, slab_ref[pl.ds(block * BLOCK + BLOCK - CHUNK, CHUNK), :])
-    mark = marks.astype(jnp.float32)[CHUNK - 1:CHUNK, :]
-    limit = jnp.where(mark > MARK / 2, mark - MARK, float(BLOCK)).astype(jnp.int32)
-    limit_ref[...] = jnp.broadcast_to(limit, limit_ref.shape)
-    copy = pltpu.make_async_copy(limit_ref, limit_smem, sem)
-    copy.start()
+            slab_ref[pl.ds(to, piece), :] = ref[start + spot * piece:start + (spot + 1) * piece, :]
+
     max_ref[...] = jnp.full(max_ref.shape, mask_value, jnp.float32)
-    copy.wait()
-
-    inside = lane % CHUNK
-
-    def pack(block, at):
-        shard = shard_of(block)
-        filled = limit_smem[0, shard]
-        first = place_ref[3] + shard * stride
+    before_here = pltpu.roll(before, (128 - plane * per_row) % 128, 1)
+    for block in range(blocks):
+        at = before_here[0, (block // per_row) * (2 * per_row) + block % per_row]
         for part in range(PARTS):
-            packed_ref[pl.ds(pl.multiple_of((at + part) * CHUNK, CHUNK), CHUNK), :] = slab_ref[
-                pl.ds(pl.multiple_of(block * BLOCK + part * CHUNK, CHUNK), CHUNK), :
-            ]
-            offset = inside + part * CHUNK
-            seen_ref[at + part] = jnp.where(offset < filled, offset + first, FAR)
-            first_smem[at + part] = first + part * CHUNK
-        return at + (filled + (CHUNK - 1)) // CHUNK
-
-    total = lax.fori_loop(0, blocks, pack, jnp.int32(0), unroll=4)
-    for slot in range(SLOTS):
-        seen_ref[total + slot] = jnp.full((8, 128), FAR, jnp.int32)
+            start = block * BLOCK + part * CHUNK
+            packed_ref[pl.ds(pl.multiple_of((at + part) * CHUNK, CHUNK), CHUNK), :] = slab_ref[start:start + CHUNK, :]
+    total = upto[0, 2 * blocks - 1]
+    firsts = [position[0, tile * SLOTS] for tile in range(most)]
+    for tile in range(most):
+        first_smem[tile] = firsts[tile]
 
     def count(tile):
-        first = first_smem[tile * SLOTS]
+        first = first_smem[tile]
         groups = jnp.int32(0)
         for group in range(tokens // GROUP):
             groups = groups + (sorted_ref[group * GROUP] >= first).astype(jnp.int32)
@@ -132,7 +137,7 @@
     tiles = (total + SLOTS - 1) // SLOTS
     active = jnp.int32(0)
     for tile in range(most):
-        active = active + ((tile < tiles) & (sorted_ref[0] >= first_smem[tile * SLOTS])).astype(jnp.int32)
+        active = active + ((tile < tiles) & (sorted_ref[0] >= firsts[tile])).astype(jnp.int32)
 
     def push(tile):
         keys = packed_ref[pl.ds(pl.multiple_of(tile * TILE, TILE), TILE), :]
@@ -169,7 +174,7 @@
         def tile_step(tile, _):
             groups = count(tile)
             odd = groups % 2
-            push(jnp.minimum(tile + 1, active - 1))
+            later = jnp.minimum(tile + 1, active - 1)
 
             def pair_step(pair, _):
                 issue(2 * pair + 1, accs[2:])
@@ -182,12 +187,14 @@
 
             @pl.when(odd == 1)
             def _():
+                push(later)
                 finish(tile, groups - 1, accs[:2])
                 issue(0, accs[:2], 0)
 
             @pl.when(odd == 0)
             def _():
                 issue(groups - 1, accs[2:])
+                push(later)
                 finish(tile, groups - 2, accs[:2])
                 issue(0, accs[:2], 0)
                 finish(tile, groups - 1, accs[2:])
@@ -201,11 +208,10 @@
     def reduce_step(tile, _):
         seen = []
         for part in range(2):
-            slot = tile * SLOTS + part * 8
-            value = seen_ref[slot]
-            for chunk in range(1, 8):
-                value = jnp.where(lane // CHUNK == chunk, seen_ref[slot + chunk], value)
-            seen.append(value[:1])
+            chunk = tile * SLOTS + part * 8 + lane // CHUNK
+            filled = lane % CHUNK < jnp.take_along_axis(held, chunk, axis=1)
+            value = jnp.take_along_axis(position, chunk, axis=1) + lane % CHUNK
+            seen.append(jnp.where(filled, value, FAR)[:1])
         found = [jnp.where(seen[part] <= at_ref[...], score_ref[2 * tile + part], mask_value) for part in range(2)]
         max_ref[tile] = folded(found[0], found[1], 8, wide)
         return 0
@@ -214,13 +220,6 @@
     found = [max_ref[tile] for tile in range(most)]
     for step in (4, 2, 1):
         found = [folded(a, b, step, wide) for a, b in zip(found[::2], found[1::2])]
-    chunks = jnp.where((lane1 < 2 * blocks) & ((lane1 // per_row) % 2 == plane), (limit + (CHUNK - 1)) // CHUNK, 0)
-    upto = chunks
-    step = 1
-    while step < 2 * blocks:
-        upto = upto + jnp.where(lane1 >= step, pltpu.roll(upto, step, 1), 0)
-        step *= 2
-    before = upto - chunks
     pooled = None
     for part in range(PARTS):
         chunk = before + jnp.minimum(part, jnp.maximum(chunks - 1, 0))
@@ -286,10 +285,14 @@
     piece = piece.reshape(2 * BLOCK, head_size)
     pieces = [piece] + [swapped(piece, moved(0, 0, step), "blk") for step in STEPS[1:]]
 
-    piece, other_pos, other_weights = lax.optimization_barrier((piece, other_pos, other_weights))
+    row = jnp.concatenate(pieces)
+    row, query_pos, head_weights, other_pos, other_weights = lax.optimization_barrier(
+        (row, query_pos, head_weights, other_pos, other_weights)
+    )
     positions = jnp.concatenate([query_pos, other_pos])
-    weights = jnp.concatenate([head_weights, other_weights]) * head_size ** (-0.5)
-    wide = jnp.broadcast_to(weights.reshape(tokens * heads, 1), (tokens * heads, 128))
+    wide = [
+        jnp.broadcast_to(value.reshape(count * heads, 1), (count * heads, 128)) for value in (head_weights, other_weights)
+    ]
 
     index = jnp.arange(tokens, dtype=jnp.int32)
     ahead = (positions[None, :] > positions[:, None]) | (
@@ -305,21 +308,22 @@
     spread = ((lane < shards)[:, None] & (target[:, None] == jnp.arange(shards * local_blocks)[None, :])).astype(jnp.bfloat16)
 
     q_rows, w_rows = pl.pallas_call(
-        lambda *refs: arrange(tokens, heads, *refs),
+        lambda *refs: arrange(tokens, heads, head_size ** (-0.5), *refs),
         out_shape=(
             jax.ShapeDtypeStruct((tokens * heads, head_size), jnp.bfloat16),
             jax.ShapeDtypeStruct((tokens * heads, 128), jnp.float32),
         ),
-        in_specs=[smem] + [vmem] * 3,
+        in_specs=[smem] + [vmem] * 4,
         out_specs=(vmem, vmem),
         compiler_params=pltpu.CompilerParams(vmem_limit_bytes=4 * 2**20),
         cost_estimate=pl.CostEstimate(flops=0, bytes_accessed=12 * 2**20, transcendentals=0),
         name="arranged",
-    )(rank, own, other, wide)
-
-    q_rows, w_rows, pieces = lax.optimization_barrier((q_rows, w_rows, pieces))
-    row = jnp.concatenate(pieces)
-    near = [row] + [swapped(row, moved(step, 0, 0), "blk") for step in STEPS[1:]]
+    )(rank, own, other, *wide)
+
+    rest = [swapped(row, moved(step, 0, 0), "blk") for step in STEPS[1:]]
+    rest, q_rows, w_rows = lax.optimization_barrier((rest, q_rows, w_rows))
+    rest = jnp.concatenate(rest)
+    near = [row, rest]
     far = [swapped(value, moved(0, 1, 0), "blk") for value in near]
 
     result = jax.ShapeDtypeStruct((count, shards * local_blocks), jnp.bfloat16)
@@ -334,18 +338,14 @@
         return pl.pallas_call(
             kernel,
             out_shape=jax.ShapeDtypeStruct((tokens, 128), jnp.bfloat16),
-            in_specs=[smem] * 2 + [vmem] * 7,
+            in_specs=[smem] * 2 + [vmem] * 5,
             out_specs=vmem,
             scratch_shapes=[
                 pltpu.VMEM((shards // 2 * BLOCK, head_size), jnp.bfloat16),
                 pltpu.VMEM(((slots + PARTS) * CHUNK, head_size), jnp.bfloat16),
-                pltpu.VMEM((slots + SLOTS, 8, 128), jnp.int32),
-                pltpu.VMEM((2 * (slots // SLOTS), tokens, 128), jnp.float32),
+                    pltpu.VMEM((2 * (slots // SLOTS), tokens, 128), jnp.float32),
                 pltpu.VMEM((slots // SLOTS, tokens, 128), jnp.float32),
-                pltpu.VMEM((8, 128), jnp.int32),
-                pltpu.SMEM((8, 128), jnp.int32),
-                pltpu.SMEM((slots + PARTS,), jnp.int32),
-                pltpu.SemaphoreType.DMA(()),
+                pltpu.SMEM((slots // SLOTS,), jnp.int32),
             ],
             compiler_params=pltpu.CompilerParams(vmem_limit_bytes=8 * 2**20),
             cost_estimate=pl.CostEstimate(flops=2**32, bytes_accessed=8 * 2**20, transcendentals=0),

time: 48.8 us -> 47.5 us (0.973)
  starting transfers between devices: 21.4 us -> 17.5 us
  waiting for transfers between devices: 3.9 us -> 7.35 us
  Pallas kernels: 17.3 us -> 16.2 us
  local copies, waits for them, and re-layouts: 2.9 us -> 3.72 us
  other arithmetic: 2.71 us -> 1.95 us
    ppermute x16 -> x14, starting transfers between devices: 21.4 us -> 17.5 us  [swapped(): return lax.ppermute(value, axis, pairs)]
    ppermute x16 -> x14, waiting for transfers between devices: 3.9 us -> 7.35 us  [swapped(): return lax.ppermute(value, axis, pairs)]
    pallas_call x2, Pallas kernels: 15.2 us -> 14.1 us  [pooled(): pl.pallas_call(kernel, out_shape=jax.ShapeDtypeStruct((tokens, 128), jnp....]
    broadcast_in_dim x1 -> x4, local copies, waits for them, and re-layouts: 1.13 us -> 2.1 us  [body(): jnp.broadcast_to(value.reshape(count * heads, 1), (count * heads, 128))]
    mul x1 -> x0, other arithmetic: 0.78 us -> none  [body(): jnp.concatenate([head_weights, other_weights]) * head_size ** (-0.5)]
    unnamed x9 -> x8, local copies, waits for them, and re-layouts: 1.61 us -> 1.53 us
  transfers between devices with their start and end apart: 16 -> 14, of which waited for: 4 -> 6; matrix products, arithmetic and copies ran while one was open for 7% -> 7% of each run, Pallas kernels for 20% -> 19%
where the time goes in v3:
time: 47.5 us; the launch traced here: 47 us
  starting transfers between devices  17.5 us (37%)
  Pallas kernels  16.2 us (34%)
  waiting for transfers between devices  7.35 us (15%)
  local copies, waits for them, and re-layouts  3.72 us (8%)
  other arithmetic  1.95 us (4%)
    ppermute x14, starting transfers between devices, swapped(): return lax.ppermute(value, axis, pairs)  17.5 us
    pallas_call x2, Pallas kernels, pooled(): pl.pallas_call(kernel, out_shape=jax.ShapeDtypeStruct((tokens, 128), jnp....  14.1 us
    ppermute x14, waiting for transfers between devices, swapped(): return lax.ppermute(value, axis, pairs)  7.35 us
    broadcast_in_dim x4, local copies, waits for them, and re-layouts, body(): jnp.broadcast_to(value.reshape(count * heads, 1), (count * heads, 128))  2.1 us
    unnamed x8, local copies, waits for them, and re-layouts  1.53 us
    pallas_call x1, Pallas kernels, body(): pl.pallas_call(lambda *refs: arrange(tokens, heads, head_size ** (-0.5),...  1.25 us
  transfers between devices with their start and end apart: 14, of which 6 were waited for; matrix products, arithmetic and copies ran while one was open for 7% of the time, Pallas kernels for 19%

profile of v3, /device:TPU:0, one launch (start us, length us, event | category | flops | bytes accessed | tf_op | source)
XLA Modules:
  0.0 47.0 jit_solution(7490999945915171160)
XLA Ops:
  0.0 0.8 %copy-done.1 = bf16[256,128]{1,0:T(8,128)(2,1)S(1)} copy-done((bf16[256,128]{1,0:T(8,128)(2,1)S(1)}, bf16[256,128]{1,0:T(8,128)(2,1)}, u32[]{:S(2)}) %copy-start.1) | copy-done | bytes 65560
  0.8 0.7 %copy-done.2 = s32[4]{0:T(128)S(1)} copy-done((s32[4]{0:T(128)S(1)}, s32[4]{0:T(128)}, u32[]{:S(2)}) %copy-start.2) | copy-done | bytes 40
  1.5 0.6 %marked.1 = (bf16[64,128]{1,0:T(8,128)(2,1)S(1)}, bf16[64,128]{1,0:T(8,128)(2,1)S(1)}) custom-call(s32[4]{0:T(128)S(1)} %copy-done.2, bf16[256,128]{1,0:T(8,128)(2,1)S(1)} %copy-done.1), custom_call_target="tpu_custom_call" | custom-call | tf_op jit(solution)/shard_map/marked/pallas_call | solution.py:265
  2.2 0.5 %collective-permute-start.5 = (f32[64,64]{1,0:T(8,128)}, f32[64,64]{1,0:T(8,128)S(1)}, u32[]{:S(2)}, u32[]{:S(2)}) collective-permute-start(f32[64,64]{1,0:T(8,128)} %param.6), channel_id=1, source_target_pairs={{0,2},{2,0},{4,6},{6,4},{8,10},{10,8},{12,14},{14,12},{16,18},{18,... | collective-permute-start | bytes 49160 | tf_op jit(solution)/shard_map/ppermute | solution.py:22
  2.8 0.1 fusion.1.spread_ref
  3.0 0.4 collective-permute-done
  3.4 1.6 %collective-permute-start.1 = (bf16[128,128]{1,0:T(8,128)(2,1)S(1)}, bf16[128,128]{1,0:T(8,128)(2,1)S(1)}, u32[]{:S(2)}, u32[]{:S(2)}) collective-permute-start(bf16[128,128]{1,0:T(8,128)(2,1)S(1)} %bitcast.12), channel_id=1, source_target_pairs={{0,4},{2,6},{4,8},{6,10},{8,12},{10,14},{12,0},{14,2},{16,20},{18,... | collective-permute-start | bytes 98312 | tf_op jit(solution)/shard_map/ppermute | solution.py:22
  5.0 1.7 %collective-permute-start.2 = (bf16[128,128]{1,0:T(8,128)(2,1)S(1)}, bf16[128,128]{1,0:T(8,128)(2,1)S(1)}, u32[]{:S(2)}, u32[]{:S(2)}) collective-permute-start(bf16[128,128]{1,0:T(8,128)(2,1)S(1)} %bitcast.13), channel_id=1, source_target_pairs={{0,12},{2,14},{4,0},{6,2},{8,4},{10,6},{12,8},{14,10},{16,28},{18,... | collective-permute-start | bytes 98312 | tf_op jit(solution)/shard_map/ppermute | solution.py:22
  6.7 1.9 %collective-permute-start.3 = (bf16[128,128]{1,0:T(8,128)(2,1)S(1)}, bf16[128,128]{1,0:T(8,128)(2,1)S(1)}, u32[]{:S(2)}, u32[]{:S(2)}) collective-permute-start(bf16[128,128]{1,0:T(8,128)(2,1)S(1)} %bitcast.14), channel_id=1, source_target_pairs={{0,8},{2,10},{4,12},{6,14},{8,0},{10,2},{12,4},{14,6},{16,24},{18,... | collective-permute-start | bytes 98312 | tf_op jit(solution)/shard_map/ppermute | solution.py:22
  8.7 0.2 collective-permute-done.2
  8.9 3.2 %collective-permute-done.3 = bf16[128,128]{1,0:T(8,128)(2,1)S(1)} collective-permute-done((bf16[128,128]{1,0:T(8,128)(2,1)S(1)}, bf16[128,128]{1,0:T(8,128)(2,1)S(1)}, u32[]{:S(2)}, u32[]{:S(2)}) %collective-permute-start.3) | collective-permute-done | bytes 32800 | tf_op jit(solution)/shard_map/ppermute | solution.py:22
  12.1 1.7 %collective-permute-start.6 = (bf16[512,128]{1,0:T(8,128)(2,1)S(1)}, bf16[512,128]{1,0:T(8,128)(2,1)S(1)}, u32[]{:S(2)}, u32[]{:S(2)}) collective-permute-start(bf16[512,128]{1,0:T(8,128)(2,1)S(1)} %pad_maximum_fusion.refs_5_), channel_id=1, source_target_pairs={{0,32},{2,34},{4,36},{6,38},{8,40},{10,42},{12,44},{14,46},{16,48}... | collective-permute-start | bytes 393224 | tf_op jit(solution)/shard_map/ppermute | solution.py:22
  13.8 1.6 %collective-permute-start.7 = (bf16[512,128]{1,0:T(8,128)(2,1)S(1)}, bf16[512,128]{1,0:T(8,128)(2,1)S(1)}, u32[]{:S(2)}, u32[]{:S(2)}) collective-permute-start(bf16[512,128]{1,0:T(8,128)(2,1)S(1)} %pad_maximum_fusion.refs_5_), channel_id=1, source_target_pairs={{0,96},{2,98},{4,100},{6,102},{8,104},{10,106},{12,108},{14,110},{... | collective-permute-start | bytes 393224 | tf_op jit(solution)/shard_map/ppermute | solution.py:22
  15.4 2.1 %collective-permute-start.8 = (bf16[512,128]{1,0:T(8,128)(2,1)S(1)}, bf16[512,128]{1,0:T(8,128)(2,1)S(1)}, u32[]{:S(2)}, u32[]{:S(2)}) collective-permute-start(bf16[512,128]{1,0:T(8,128)(2,1)S(1)} %pad_maximum_fusion.refs_5_), channel_id=1, source_target_pairs={{0,64},{2,66},{4,68},{6,70},{8,72},{10,74},{12,76},{14,78},{16,80}... | collective-permute-start | bytes 393224 | tf_op jit(solution)/shard_map/ppermute | solution.py:22
  17.5 1.9 %collective-permute-start.10 = (bf16[512,128]{1,0:T(8,128)(2,1)S(1)}, bf16[512,128]{1,0:T(8,128)(2,1)S(1)}, u32[]{:S(2)}, u32[]{:S(2)}) collective-permute-start(bf16[512,128]{1,0:T(8,128)(2,1)S(1)} %pad_maximum_fusion.refs_5_), channel_id=1, source_target_pairs={{0,16},{2,18},{4,20},{6,22},{8,24},{10,26},{12,28},{14,30},{16,0},... | collective-permute-start | bytes 393224 | tf_op jit(solution)/shard_map/ppermute | solution.py:22
  19.4 0.7 %pad_add_fusion = s32[128]{0:T(128)S(1)} fusion(s32[64]{0:T(128)S(1)} %collective-permute-done.4, s32[64]{0:T(128)} %param.8), kind=kLoop, calls=%fused_computation.17 | loop fusion | flops 128 | bytes 1024 | tf_op jit(solution)/shard_map/concatenate | solution.py:292
  20.1 0.2 convert_reduce_fusion.refs_0_
  20.3 0.1 fusion.4.unsort_ref
  20.4 0.8 %broadcast_in_dim.24 = f32[4096]{0:T(1024)S(1)} reshape(f32[64,64]{1,0:T(8,128)} %param.6) | data formatting | bytes 32768 | tf_op jit(solution)/shard_map/broadcast_in_dim | solution.py:294
  21.3 0.1 select_reduce_fusion.refs_0_
  21.4 0.6 %broadcast_in_dim.25.refs_3_ = f32[4096,128]{1,0:T(8,128)S(1)} broadcast(f32[4096]{0:T(1024)S(1)} %broadcast_in_dim.24), dimensions={0} | broadcast | bytes 2113536 | tf_op jit(solution)/shard_map/broadcast_in_dim | solution.py:294
  22.0 0.6 %broadcast_in_dim.27.refs_4_ = f32[4096,128]{1,0:T(8,128)S(1)} broadcast(f32[4096]{0:T(1024)S(1)} %broadcast_in_dim.26), dimensions={0} | broadcast | bytes 2113536 | tf_op jit(solution)/shard_map/broadcast_in_dim | solution.py:294
  22.7 1.2 %arranged.1 = (bf16[8192,128]{1,0:T(8,128)(2,1)S(1)}, f32[8192,128]{1,0:T(8,128)S(1)}) custom-call(s32[128]{0:T(128)S(1)} %convert_reduce_fusion.refs_0_, bf16[4096,128]{1,0:T(8,128)(2,1)S(1)} %bitcast.10, bf16[4096,128]{1,0:T(8,128)(2,1)S(1)} %collective-permute-done.9.refs_2_, f32[4096,128]{1,0:T(8,128)S(1)} %broadcast_in_dim.25.refs_3_, ...), custom_call_target="tpu_custom_call" | custom-call | bytes 12582912 | tf_op jit(solution)/shard_map/arranged/pallas_call | solution.py:310
  24.0 0.2 collective-permute-start.11
  24.3 7.6 %pooled_scores.2.near_ref = bf16[128,128]{1,0:T(8,128)(2,1)S(1)} custom-call(s32[128]{0:T(128)S(1)} %select_reduce_fusion.refs_0_, s32[4]{0:T(128)S(1)} %get-tuple-element.37.refs_1_, bf16[8192,128]{1,0:T(8,128)(2,1)S(1)} %get-tuple-element.30.refs_2_, f32[8192,128]{1,0:T(8,128)S(1)} %get-tuple-element.31.refs_3_, s32[128,128]{1,0:T(8,128)S(1)} %broadcast_in_dim.28.refs_4_, ...), custom_call_target="tpu_custom_call" | custom-call | flops 4294967296 | bytes 8388608 | tf_op jit(solution)/shard_map/pooled_scores/pallas_call | solution.py:338
  31.9 0.4 collective-permute-done.11.refs_6_
  32.4 6.4 %pooled_scores.3.far_ref = bf16[128,128]{1,0:T(8,128)(2,1)S(1)} custom-call(s32[128]{0:T(128)S(1)} %select_reduce_fusion.refs_0_, s32[4]{0:T(128)S(1)} %get-tuple-element.38.refs_1_, bf16[8192,128]{1,0:T(8,128)(2,1)S(1)} %get-tuple-element.30.refs_2_, f32[8192,128]{1,0:T(8,128)S(1)} %get-tuple-element.31.refs_3_, s32[128,128]{1,0:T(8,128)S(1)} %broadcast_in_dim.28.refs_4_, ...), custom_call_target="tpu_custom_call" | custom-call | flops 4294967296 | bytes 8388608 | tf_op jit(solution)/shard_map/pooled_scores/pallas_call | solution.py:338
  38.8 0.3 restored.1
  39.2 1.2 %collective-permute-done.12 = bf16[64,256]{1,0:T(8,128)(2,1)S(1)} collective-permute-done((bf16[64,256]{1,0:T(8,128)(2,1)S(1)}, bf16[64,256]{1,0:T(8,128)(2,1)S(1)}, u32[]{:S(2)}, u32[]{:S(2)}) %collective-permute-start.12) | collective-permute-done | bytes 32800 | tf_op jit(solution)/shard_map/ppermute | solution.py:22
  40.4 4.1 %collective-permute-start.13 = (bf16[64,256]{1,0:T(8,128)(2,1)S(1)}, bf16[64,256]{1,0:T(8,128)(2,1)S(1)}, u32[]{:S(2)}, u32[]{:S(2)}) collective-permute-start(bf16[64,256]{1,0:T(8,128)(2,1)S(1)} %add.39), channel_id=1, source_target_pairs={{0,1},{1,0},{2,3},{3,2},{4,5},{5,4},{6,7},{7,6},{8,9},{9,8},{10,11... | collective-permute-start | bytes 98312 | tf_op jit(solution)/shard_map/ppermute | solution.py:22
  44.5 1.9 %collective-permute-done.13 = bf16[64,256]{1,0:T(8,128)(2,1)S(1)} collective-permute-done((bf16[64,256]{1,0:T(8,128)(2,1)S(1)}, bf16[64,256]{1,0:T(8,128)(2,1)S(1)}, u32[]{:S(2)}, u32[]{:S(2)}) %collective-permute-start.13) | collective-permute-done | bytes 32800 | tf_op jit(solution)/shard_map/ppermute | solution.py:22
  46.4 0.6 %add_convert_fusion = f32[64,256]{1,0:T(8,128)} fusion(bf16[64,256]{1,0:T(8,128)(2,1)S(1)} %add.39, bf16[64,256]{1,0:T(8,128)(2,1)S(1)} %collective-permute-done.13), kind=kLoop, calls=%fused_computation.13 | loop fusion | flops 32768 | bytes 131072 | tf_op jit(solution)/shard_map/convert_element_type | solution.py:365
  (27 shorter events, 0.6 us)
Async XLA Ops:
  0.0 0.8 %copy-start.1 = (bf16[256,128]{1,0:T(8,128)(2,1)S(1)}, bf16[256,128]{1,0:T(8,128)(2,1)}, u32[]{:S(2)}) copy-start(bf16[256,128]{1,0:T(8,128)(2,1)} %key_hbm.1) | copy-start | bytes 196612
  0.8 0.7 %copy-start.2 = (s32[4]{0:T(128)S(1)}, s32[4]{0:T(128)}, u32[]{:S(2)}) copy-start(s32[4]{0:T(128)} %limit_hbm.1) | copy-start | bytes 52
  2.1 1.3 %collective-permute-start = (bf16[64,128]{1,0:T(8,128)(2,1)S(1)}, bf16[64,128]{1,0:T(8,128)(2,1)S(1)}, u32[]{:S(2)}, u32[]{:S(2)}) collective-permute-start(bf16[64,128]{1,0:T(8,128)(2,1)S(1)} %get-tuple-element.22), channel_id=1, source_target_pairs={{0,2},{2,0},{4,6},{6,4},{8,10},{10,8},{12,14},{14,12},{16,18},{18,... | collective-permute-start | bytes 49160 | tf_op jit(solution)/shard_map/ppermute | solution.py:22
  2.2 9.9 %collective-permute-start.5 = (f32[64,64]{1,0:T(8,128)}, f32[64,64]{1,0:T(8,128)S(1)}, u32[]{:S(2)}, u32[]{:S(2)}) collective-permute-start(f32[64,64]{1,0:T(8,128)} %param.6), channel_id=1, source_target_pairs={{0,2},{2,0},{4,6},{6,4},{8,10},{10,8},{12,14},{14,12},{16,18},{18,... | collective-permute-start | bytes 49160 | tf_op jit(solution)/shard_map/ppermute | solution.py:22
  2.7 18.8 %collective-permute-start.9 = (bf16[4096,128]{1,0:T(8,128)(2,1)}, bf16[4096,128]{1,0:T(8,128)(2,1)S(1)}, u32[]{:S(2)}, u32[]{:S(2)}) collective-permute-start(bf16[4096,128]{1,0:T(8,128)(2,1)} %bitcast.9), channel_id=1, source_target_pairs={{0,2},{2,0},{4,6},{6,4},{8,10},{10,8},{12,14},{14,12},{16,18},{18,... | collective-permute-start | bytes 3145736 | tf_op jit(solution)/shard_map/ppermute | solution.py:22
  3.4 5.3 %collective-permute-start.1 = (bf16[128,128]{1,0:T(8,128)(2,1)S(1)}, bf16[128,128]{1,0:T(8,128)(2,1)S(1)}, u32[]{:S(2)}, u32[]{:S(2)}) collective-permute-start(bf16[128,128]{1,0:T(8,128)(2,1)S(1)} %bitcast.12), channel_id=1, source_target_pairs={{0,4},{2,6},{4,8},{6,10},{8,12},{10,14},{12,0},{14,2},{16,20},{18,... | collective-permute-start | bytes 98312 | tf_op jit(solution)/shard_map/ppermute | solution.py:22
  5.0 3.9 %collective-permute-start.2 = (bf16[128,128]{1,0:T(8,128)(2,1)S(1)}, bf16[128,128]{1,0:T(8,128)(2,1)S(1)}, u32[]{:S(2)}, u32[]{:S(2)}) collective-permute-start(bf16[128,128]{1,0:T(8,128)(2,1)S(1)} %bitcast.13), channel_id=1, source_target_pairs={{0,12},{2,14},{4,0},{6,2},{8,4},{10,6},{12,8},{14,10},{16,28},{18,... | collective-permute-start | bytes 98312 | tf_op jit(solution)/shard_map/ppermute | solution.py:22
  6.7 5.4 %collective-permute-start.3 = (bf16[128,128]{1,0:T(8,128)(2,1)S(1)}, bf16[128,128]{1,0:T(8,128)(2,1)S(1)}, u32[]{:S(2)}, u32[]{:S(2)}) collective-permute-start(bf16[128,128]{1,0:T(8,128)(2,1)S(1)} %bitcast.14), channel_id=1, source_target_pairs={{0,8},{2,10},{4,12},{6,14},{8,0},{10,2},{12,4},{14,6},{16,24},{18,... | collective-permute-start | bytes 98312 | tf_op jit(solution)/shard_map/ppermute | solution.py:22
  8.6 3.5 %collective-permute-start.4 = (s32[64]{0:T(128)}, s32[64]{0:T(128)S(1)}, u32[]{:S(2)}, u32[]{:S(2)}) collective-permute-start(s32[64]{0:T(128)} %param.8), channel_id=1, source_target_pairs={{0,2},{2,0},{4,6},{6,4},{8,10},{10,8},{12,14},{14,12},{16,18},{18,... | collective-permute-start | bytes 776 | tf_op jit(solution)/shard_map/ppermute | solution.py:22
  12.1 11.8 %collective-permute-start.6 = (bf16[512,128]{1,0:T(8,128)(2,1)S(1)}, bf16[512,128]{1,0:T(8,128)(2,1)S(1)}, u32[]{:S(2)}, u32[]{:S(2)}) collective-permute-start(bf16[512,128]{1,0:T(8,128)(2,1)S(1)} %pad_maximum_fusion.refs_5_), channel_id=1, source_target_pairs={{0,32},{2,34},{4,36},{6,38},{8,40},{10,42},{12,44},{14,46},{16,48}... | collective-permute-start | bytes 393224 | tf_op jit(solution)/shard_map/ppermute | solution.py:22
  13.8 10.1 %collective-permute-start.7 = (bf16[512,128]{1,0:T(8,128)(2,1)S(1)}, bf16[512,128]{1,0:T(8,128)(2,1)S(1)}, u32[]{:S(2)}, u32[]{:S(2)}) collective-permute-start(bf16[512,128]{1,0:T(8,128)(2,1)S(1)} %pad_maximum_fusion.refs_5_), channel_id=1, source_target_pairs={{0,96},{2,98},{4,100},{6,102},{8,104},{10,106},{12,108},{14,110},{... | collective-permute-start | bytes 393224 | tf_op jit(solution)/shard_map/ppermute | solution.py:22
  15.4 8.5 %collective-permute-start.8 = (bf16[512,128]{1,0:T(8,128)(2,1)S(1)}, bf16[512,128]{1,0:T(8,128)(2,1)S(1)}, u32[]{:S(2)}, u32[]{:S(2)}) collective-permute-start(bf16[512,128]{1,0:T(8,128)(2,1)S(1)} %pad_maximum_fusion.refs_5_), channel_id=1, source_target_pairs={{0,64},{2,66},{4,68},{6,70},{8,72},{10,74},{12,76},{14,78},{16,80}... | collective-permute-start | bytes 393224 | tf_op jit(solution)/shard_map/ppermute | solution.py:22
  17.5 14.5 %collective-permute-start.10 = (bf16[512,128]{1,0:T(8,128)(2,1)S(1)}, bf16[512,128]{1,0:T(8,128)(2,1)S(1)}, u32[]{:S(2)}, u32[]{:S(2)}) collective-permute-start(bf16[512,128]{1,0:T(8,128)(2,1)S(1)} %pad_maximum_fusion.refs_5_), channel_id=1, source_target_pairs={{0,16},{2,18},{4,20},{6,22},{8,24},{10,26},{12,28},{14,30},{16,0},... | collective-permute-start | bytes 393224 | tf_op jit(solution)/shard_map/ppermute | solution.py:22
  21.4 1.2 %copy-start = (bf16[64,64,128]{2,1,0:T(8,128)(2,1)S(1)}, bf16[64,64,128]{2,1,0:T(8,128)(2,1)}, u32[]{:S(2)}) copy-start(bf16[64,64,128]{2,1,0:T(8,128)(2,1)} %param.5) | copy-start | bytes 3145732
  24.0 8.4 %collective-permute-start.11 = (bf16[1536,128]{1,0:T(8,128)(2,1)S(1)}, bf16[1536,128]{1,0:T(8,128)(2,1)S(1)}, u32[]{:S(2)}, u32[]{:S(2)}) collective-permute-start(bf16[1536,128]{1,0:T(8,128)(2,1)S(1)} %constant_dynamic-update-slice_fusion.refs_6_), channel_id=1, source_target_pairs={{0,16},{2,18},{4,20},{6,22},{8,24},{10,26},{12,28},{14,30},{16,0},... | collective-permute-start | bytes 1179656 | tf_op jit(solution)/shard_map/ppermute | solution.py:22
  39.1 1.3 %collective-permute-start.12 = (bf16[64,256]{1,0:T(8,128)(2,1)S(1)}, bf16[64,256]{1,0:T(8,128)(2,1)S(1)}, u32[]{:S(2)}, u32[]{:S(2)}) collective-permute-start(bf16[64,256]{1,0:T(8,128)(2,1)S(1)} %get-tuple-element.36), channel_id=1, source_target_pairs={{0,2},{2,0},{4,6},{6,4},{8,10},{10,8},{12,14},{14,12},{16,18},{18,... | collective-permute-start | bytes 98312 | tf_op jit(solution)/shard_map/ppermute | solution.py:22
  40.4 6.0 %collective-permute-start.13 = (bf16[64,256]{1,0:T(8,128)(2,1)S(1)}, bf16[64,256]{1,0:T(8,128)(2,1)S(1)}, u32[]{:S(2)}, u32[]{:S(2)}) collective-permute-start(bf16[64,256]{1,0:T(8,128)(2,1)S(1)} %add.39), channel_id=1, source_target_pairs={{0,1},{1,0},{2,3},{3,2},{4,5},{5,4},{6,7},{7,6},{8,9},{9,8},{10,11... | collective-permute-start | bytes 98312 | tf_op jit(solution)/shard_map/ppermute | solution.py:22

commit v4 on v3

--- a/solution.py
+++ b/solution.py
@@ -285,14 +285,11 @@
     piece = piece.reshape(2 * BLOCK, head_size)
     pieces = [piece] + [swapped(piece, moved(0, 0, step), "blk") for step in STEPS[1:]]
 
-    row = jnp.concatenate(pieces)
-    row, query_pos, head_weights, other_pos, other_weights = lax.optimization_barrier(
-        (row, query_pos, head_weights, other_pos, other_weights)
+    piece, query_pos, head_weights, other_pos, other_weights = lax.optimization_barrier(
+        (piece, query_pos, head_weights, other_pos, other_weights)
     )
     positions = jnp.concatenate([query_pos, other_pos])
-    wide = [
-        jnp.broadcast_to(value.reshape(count * heads, 1), (count * heads, 128)) for value in (head_weights, other_weights)
-    ]
+    flat = [value.reshape(count * heads) for value in (head_weights, other_weights)]
 
     index = jnp.arange(tokens, dtype=jnp.int32)
     ahead = (positions[None, :] > positions[:, None]) | (
@@ -303,6 +300,10 @@
     in_order = jnp.sum(jnp.where(hit, positions[None, :], 0), axis=1)
     at = jnp.broadcast_to(in_order[:, None], (tokens, 128))
     unsort = (rank[:, None] == index[None, :]).astype(jnp.bfloat16)
+    pieces, rank, *flat = lax.optimization_barrier((pieces, rank, *flat))
+    row = jnp.concatenate(pieces)
+    row, *flat = lax.optimization_barrier((row, *flat))
+    wide = [jnp.broadcast_to(value[:, None], (count * heads, 128)) for value in flat]
     lane = jnp.arange(128, dtype=jnp.int32)
     target = lane * local_blocks + quarter
     spread = ((lane < shards)[:, None] & (target[:, None] == jnp.arange(shards * local_blocks)[None, :])).astype(jnp.bfloat16)

time: 47.5 us -> 47.1 us (level); the launches traced: 47 us -> 47.1 us
  waiting for transfers between devices: 7.35 us -> 5.34 us
  Pallas kernels: 16.2 us -> 17.3 us
  starting transfers between devices: 17.5 us -> 18.6 us
    ppermute x14, waiting for transfers between devices: 7.35 us -> 5.34 us  [swapped(): return lax.ppermute(value, axis, pairs)]
    pallas_call x2, Pallas kernels: 14.1 us -> 15.2 us  [pooled(): pl.pallas_call(kernel, out_shape=jax.ShapeDtypeStruct((tokens, 128), jnp....]
    ppermute x14, starting transfers between devices: 17.5 us -> 18.6 us  [swapped(): return lax.ppermute(value, axis, pairs)]
    reshape x0 -> x2, local copies, waits for them, and re-layouts: none -> 0.91 us  [body(): value.reshape(count * heads)]
    broadcast_in_dim x4 -> x2, local copies, waits for them, and re-layouts: 2.1 us -> 1.19 us  [body(): jnp.broadcast_to(value[:, None], (count * heads, 128))]
  transfers between devices with their start and end apart: 14 -> 14, of which waited for: 6 -> 3; matrix products, arithmetic and copies ran while one was open for 7% -> 7% of each run, Pallas kernels for 19% -> 19%
where the time goes in v4:
time: 47.1 us
  starting transfers between devices  18.6 us (39%)
  Pallas kernels  17.3 us (37%)
  waiting for transfers between devices  5.34 us (11%)
  local copies, waits for them, and re-layouts  3.72 us (8%)
  other arithmetic  1.95 us (4%)
    ppermute x14, starting transfers between devices, swapped(): return lax.ppermute(value, axis, pairs)  18.6 us
    pallas_call x2, Pallas kernels, pooled(): pl.pallas_call(kernel, out_shape=jax.ShapeDtypeStruct((tokens, 128), jnp....  15.2 us
    ppermute x14, waiting for transfers between devices, swapped(): return lax.ppermute(value, axis, pairs)  5.34 us
    unnamed x8, local copies, waits for them, and re-layouts  1.53 us
    pallas_call x1, Pallas kernels, body(): pl.pallas_call(lambda *refs: arrange(tokens, heads, head_size ** (-0.5),...  1.25 us
    broadcast_in_dim x2, local copies, waits for them, and re-layouts, body(): jnp.broadcast_to(value[:, None], (count * heads, 128))  1.19 us
  transfers between devices with their start and end apart: 14, of which 3 were waited for; matrix products, arithmetic and copies ran while one was open for 7% of the time, Pallas kernels for 19%

profile of v4, /device:TPU:0, one launch (start us, length us, event | category | flops | bytes accessed | tf_op | source)
XLA Modules:
  0.0 47.1 jit_solution(1262807294680999265)
XLA Ops:
  0.0 0.8 %copy-done.1 = bf16[256,128]{1,0:T(8,128)(2,1)S(1)} copy-done((bf16[256,128]{1,0:T(8,128)(2,1)S(1)}, bf16[256,128]{1,0:T(8,128)(2,1)}, u32[]{:S(2)}) %copy-start.1) | copy-done | bytes 65560
  0.8 0.7 %copy-done.2 = s32[4]{0:T(128)S(1)} copy-done((s32[4]{0:T(128)S(1)}, s32[4]{0:T(128)}, u32[]{:S(2)}) %copy-start.2) | copy-done | bytes 40
  1.5 0.6 %marked.1 = (bf16[64,128]{1,0:T(8,128)(2,1)S(1)}, bf16[64,128]{1,0:T(8,128)(2,1)S(1)}) custom-call(s32[4]{0:T(128)S(1)} %copy-done.2, bf16[256,128]{1,0:T(8,128)(2,1)S(1)} %copy-done.1), custom_call_target="tpu_custom_call" | custom-call | tf_op jit(solution)/shard_map/marked/pallas_call | solution.py:265
  2.1 0.1 collective-permute-start
  2.2 0.5 %collective-permute-start.2 = (f32[64,64]{1,0:T(8,128)}, f32[64,64]{1,0:T(8,128)S(1)}, u32[]{:S(2)}, u32[]{:S(2)}) collective-permute-start(f32[64,64]{1,0:T(8,128)} %param.6), channel_id=1, source_target_pairs={{0,2},{2,0},{4,6},{6,4},{8,10},{10,8},{12,14},{14,12},{16,18},{18,... | collective-permute-start | bytes 49160 | tf_op jit(solution)/shard_map/ppermute | solution.py:22
  2.7 0.1 collective-permute-start.1
  2.8 0.4 collective-permute-start.9
  3.2 0.1 fusion.1.spread_ref
  3.4 1.6 %collective-permute-start.3 = (bf16[128,128]{1,0:T(8,128)(2,1)S(1)}, bf16[128,128]{1,0:T(8,128)(2,1)S(1)}, u32[]{:S(2)}, u32[]{:S(2)}) collective-permute-start(bf16[128,128]{1,0:T(8,128)(2,1)S(1)} %bitcast.12), channel_id=1, source_target_pairs={{0,4},{2,6},{4,8},{6,10},{8,12},{10,14},{12,0},{14,2},{16,20},{18,... | collective-permute-start | bytes 98312 | tf_op jit(solution)/shard_map/ppermute | solution.py:22
  5.0 1.7 %collective-permute-start.4 = (bf16[128,128]{1,0:T(8,128)(2,1)S(1)}, bf16[128,128]{1,0:T(8,128)(2,1)S(1)}, u32[]{:S(2)}, u32[]{:S(2)}) collective-permute-start(bf16[128,128]{1,0:T(8,128)(2,1)S(1)} %bitcast.13), channel_id=1, source_target_pairs={{0,12},{2,14},{4,0},{6,2},{8,4},{10,6},{12,8},{14,10},{16,28},{18,... | collective-permute-start | bytes 98312 | tf_op jit(solution)/shard_map/ppermute | solution.py:22
  6.7 1.9 %collective-permute-start.5 = (bf16[128,128]{1,0:T(8,128)(2,1)S(1)}, bf16[128,128]{1,0:T(8,128)(2,1)S(1)}, u32[]{:S(2)}, u32[]{:S(2)}) collective-permute-start(bf16[128,128]{1,0:T(8,128)(2,1)S(1)} %bitcast.14), channel_id=1, source_target_pairs={{0,8},{2,10},{4,12},{6,14},{8,0},{10,2},{12,4},{14,6},{16,24},{18,... | collective-permute-start | bytes 98312 | tf_op jit(solution)/shard_map/ppermute | solution.py:22
  8.6 0.7 %pad_add_fusion = s32[128]{0:T(128)S(1)} fusion(s32[64]{0:T(128)S(1)} %collective-permute-done.1, s32[64]{0:T(128)} %param.8), kind=kLoop, calls=%fused_computation.17 | loop fusion | flops 128 | bytes 1024 | tf_op jit(solution)/shard_map/concatenate | solution.py:291
  9.3 0.2 convert_reduce_fusion.refs_0_
  9.5 0.8 %reshape.30 = f32[4096]{0:T(1024)S(1)} reshape(f32[64,64]{1,0:T(8,128)} %param.6) | data formatting | bytes 32768 | tf_op jit(solution)/shard_map/reshape | solution.py:292
  10.4 1.7 %collective-permute-done.5 = bf16[128,128]{1,0:T(8,128)(2,1)S(1)} collective-permute-done((bf16[128,128]{1,0:T(8,128)(2,1)S(1)}, bf16[128,128]{1,0:T(8,128)(2,1)S(1)}, u32[]{:S(2)}, u32[]{:S(2)}) %collective-permute-start.5) | collective-permute-done | bytes 32800 | tf_op jit(solution)/shard_map/ppermute | solution.py:22
  12.1 1.7 %collective-permute-start.6 = (bf16[512,128]{1,0:T(8,128)(2,1)S(1)}, bf16[512,128]{1,0:T(8,128)(2,1)S(1)}, u32[]{:S(2)}, u32[]{:S(2)}) collective-permute-start(bf16[512,128]{1,0:T(8,128)(2,1)S(1)} %pad_maximum_fusion.refs_5_), channel_id=1, source_target_pairs={{0,32},{2,34},{4,36},{6,38},{8,40},{10,42},{12,44},{14,46},{16,48}... | collective-permute-start | bytes 393224 | tf_op jit(solution)/shard_map/ppermute | solution.py:22
  13.9 1.6 %collective-permute-start.7 = (bf16[512,128]{1,0:T(8,128)(2,1)S(1)}, bf16[512,128]{1,0:T(8,128)(2,1)S(1)}, u32[]{:S(2)}, u32[]{:S(2)}) collective-permute-start(bf16[512,128]{1,0:T(8,128)(2,1)S(1)} %pad_maximum_fusion.refs_5_), channel_id=1, source_target_pairs={{0,96},{2,98},{4,100},{6,102},{8,104},{10,106},{12,108},{14,110},{... | collective-permute-start | bytes 393224 | tf_op jit(solution)/shard_map/ppermute | solution.py:22
  15.5 2.1 %collective-permute-start.8 = (bf16[512,128]{1,0:T(8,128)(2,1)S(1)}, bf16[512,128]{1,0:T(8,128)(2,1)S(1)}, u32[]{:S(2)}, u32[]{:S(2)}) collective-permute-start(bf16[512,128]{1,0:T(8,128)(2,1)S(1)} %pad_maximum_fusion.refs_5_), channel_id=1, source_target_pairs={{0,64},{2,66},{4,68},{6,70},{8,72},{10,74},{12,76},{14,78},{16,80}... | collective-permute-start | bytes 393224 | tf_op jit(solution)/shard_map/ppermute | solution.py:22
  17.6 0.1 select_reduce_fusion.refs_0_
  17.7 2.0 %collective-permute-start.10 = (bf16[512,128]{1,0:T(8,128)(2,1)S(1)}, bf16[512,128]{1,0:T(8,128)(2,1)S(1)}, u32[]{:S(2)}, u32[]{:S(2)}) collective-permute-start(bf16[512,128]{1,0:T(8,128)(2,1)S(1)} %pad_maximum_fusion.refs_5_), channel_id=1, source_target_pairs={{0,16},{2,18},{4,20},{6,22},{8,24},{10,26},{12,28},{14,30},{16,0},... | collective-permute-start | bytes 393224 | tf_op jit(solution)/shard_map/ppermute | solution.py:22
  19.7 0.6 %broadcast_in_dim.20.refs_3_ = f32[4096,128]{1,0:T(8,128)S(1)} broadcast(f32[4096]{0:T(1024)S(1)} %reshape.30), dimensions={0} | broadcast | bytes 2113536 | tf_op jit(solution)/shard_map/broadcast_in_dim | solution.py:306
  20.3 0.6 %broadcast_in_dim.21.refs_4_ = f32[4096,128]{1,0:T(8,128)S(1)} broadcast(f32[4096]{0:T(1024)S(1)} %reshape.31), dimensions={0} | broadcast | bytes 2113536 | tf_op jit(solution)/shard_map/broadcast_in_dim | solution.py:306
  20.9 1.2 %arranged.1 = (bf16[8192,128]{1,0:T(8,128)(2,1)S(1)}, f32[8192,128]{1,0:T(8,128)S(1)}) custom-call(s32[128]{0:T(128)S(1)} %convert_reduce_fusion.refs_0_, bf16[4096,128]{1,0:T(8,128)(2,1)S(1)} %bitcast.10, bf16[4096,128]{1,0:T(8,128)(2,1)S(1)} %collective-permute-done.9.refs_2_, f32[4096,128]{1,0:T(8,128)S(1)} %broadcast_in_dim.20.refs_3_, ...), custom_call_target="tpu_custom_call" | custom-call | bytes 12582912 | tf_op jit(solution)/shard_map/arranged/pallas_call | solution.py:311
  22.3 1.8 %collective-permute-start.11 = (bf16[1536,128]{1,0:T(8,128)(2,1)S(1)}, bf16[1536,128]{1,0:T(8,128)(2,1)S(1)}, u32[]{:S(2)}, u32[]{:S(2)}) collective-permute-start(bf16[1536,128]{1,0:T(8,128)(2,1)S(1)} %constant_dynamic-update-slice_fusion.refs_6_), channel_id=1, source_target_pairs={{0,16},{2,18},{4,20},{6,22},{8,24},{10,26},{12,28},{14,30},{16,0},... | collective-permute-start | bytes 1179656 | tf_op jit(solution)/shard_map/ppermute | solution.py:22
  24.1 7.8 %pooled_scores.2.near_ref = bf16[128,128]{1,0:T(8,128)(2,1)S(1)} custom-call(s32[128]{0:T(128)S(1)} %select_reduce_fusion.refs_0_, s32[4]{0:T(128)S(1)} %get-tuple-element.55.refs_1_, bf16[8192,128]{1,0:T(8,128)(2,1)S(1)} %get-tuple-element.48.refs_2_, f32[8192,128]{1,0:T(8,128)S(1)} %get-tuple-element.49.refs_3_, s32[128,128]{1,0:T(8,128)S(1)} %broadcast_in_dim.22.refs_4_, ...), custom_call_target="tpu_custom_call" | custom-call | flops 4294967296 | bytes 8388608 | tf_op jit(solution)/shard_map/pooled_scores/pallas_call | solution.py:339
  32.0 7.4 %pooled_scores.3.far_ref = bf16[128,128]{1,0:T(8,128)(2,1)S(1)} custom-call(s32[128]{0:T(128)S(1)} %select_reduce_fusion.refs_0_, s32[4]{0:T(128)S(1)} %get-tuple-element.56.refs_1_, bf16[8192,128]{1,0:T(8,128)(2,1)S(1)} %get-tuple-element.48.refs_2_, f32[8192,128]{1,0:T(8,128)S(1)} %get-tuple-element.49.refs_3_, s32[128,128]{1,0:T(8,128)S(1)} %broadcast_in_dim.22.refs_4_, ...), custom_call_target="tpu_custom_call" | custom-call | flops 4294967296 | bytes 8388608 | tf_op jit(solution)/shard_map/pooled_scores/pallas_call | solution.py:339
  39.4 0.3 restored.1
  39.7 0.1 collective-permute-start.12
  39.8 1.2 %collective-permute-done.12 = bf16[64,256]{1,0:T(8,128)(2,1)S(1)} collective-permute-done((bf16[64,256]{1,0:T(8,128)(2,1)S(1)}, bf16[64,256]{1,0:T(8,128)(2,1)S(1)}, u32[]{:S(2)}, u32[]{:S(2)}) %collective-permute-start.12) | collective-permute-done | bytes 32800 | tf_op jit(solution)/shard_map/ppermute | solution.py:22
  41.0 3.1 %collective-permute-start.13 = (bf16[64,256]{1,0:T(8,128)(2,1)S(1)}, bf16[64,256]{1,0:T(8,128)(2,1)S(1)}, u32[]{:S(2)}, u32[]{:S(2)}) collective-permute-start(bf16[64,256]{1,0:T(8,128)(2,1)S(1)} %add.39), channel_id=1, source_target_pairs={{0,1},{1,0},{2,3},{3,2},{4,5},{5,4},{6,7},{7,6},{8,9},{9,8},{10,11... | collective-permute-start | bytes 98312 | tf_op jit(solution)/shard_map/ppermute | solution.py:22
  44.1 2.4 %collective-permute-done.13 = bf16[64,256]{1,0:T(8,128)(2,1)S(1)} collective-permute-done((bf16[64,256]{1,0:T(8,128)(2,1)S(1)}, bf16[64,256]{1,0:T(8,128)(2,1)S(1)}, u32[]{:S(2)}, u32[]{:S(2)}) %collective-permute-start.13) | collective-permute-done | bytes 32800 | tf_op jit(solution)/shard_map/ppermute | solution.py:22
  46.5 0.6 %add_convert_fusion = f32[64,256]{1,0:T(8,128)} fusion(bf16[64,256]{1,0:T(8,128)(2,1)S(1)} %add.39, bf16[64,256]{1,0:T(8,128)(2,1)S(1)} %collective-permute-done.13), kind=kLoop, calls=%fused_computation.13 | loop fusion | flops 32768 | bytes 131072 | tf_op jit(solution)/shard_map/convert_element_type | solution.py:366
  (27 shorter events, 0.4 us)
Async XLA Ops:
  0.0 0.8 %copy-start.1 = (bf16[256,128]{1,0:T(8,128)(2,1)S(1)}, bf16[256,128]{1,0:T(8,128)(2,1)}, u32[]{:S(2)}) copy-start(bf16[256,128]{1,0:T(8,128)(2,1)} %key_hbm.1) | copy-start | bytes 196612
  0.8 0.7 %copy-start.2 = (s32[4]{0:T(128)S(1)}, s32[4]{0:T(128)}, u32[]{:S(2)}) copy-start(s32[4]{0:T(128)} %limit_hbm.1) | copy-start | bytes 52
  2.1 1.3 %collective-permute-start = (bf16[64,128]{1,0:T(8,128)(2,1)S(1)}, bf16[64,128]{1,0:T(8,128)(2,1)S(1)}, u32[]{:S(2)}, u32[]{:S(2)}) collective-permute-start(bf16[64,128]{1,0:T(8,128)(2,1)S(1)} %get-tuple-element.31), channel_id=1, source_target_pairs={{0,2},{2,0},{4,6},{6,4},{8,10},{10,8},{12,14},{14,12},{16,18},{18,... | collective-permute-start | bytes 49160 | tf_op jit(solution)/shard_map/ppermute | solution.py:22
  2.2 6.4 %collective-permute-start.2 = (f32[64,64]{1,0:T(8,128)}, f32[64,64]{1,0:T(8,128)S(1)}, u32[]{:S(2)}, u32[]{:S(2)}) collective-permute-start(f32[64,64]{1,0:T(8,128)} %param.6), channel_id=1, source_target_pairs={{0,2},{2,0},{4,6},{6,4},{8,10},{10,8},{12,14},{14,12},{16,18},{18,... | collective-permute-start | bytes 49160 | tf_op jit(solution)/shard_map/ppermute | solution.py:22
  2.7 4.0 %collective-permute-start.1 = (s32[64]{0:T(128)}, s32[64]{0:T(128)S(1)}, u32[]{:S(2)}, u32[]{:S(2)}) collective-permute-start(s32[64]{0:T(128)} %param.8), channel_id=1, source_target_pairs={{0,2},{2,0},{4,6},{6,4},{8,10},{10,8},{12,14},{14,12},{16,18},{18,... | collective-permute-start | bytes 776 | tf_op jit(solution)/shard_map/ppermute | solution.py:22
  2.8 17.0 %collective-permute-start.9 = (bf16[4096,128]{1,0:T(8,128)(2,1)}, bf16[4096,128]{1,0:T(8,128)(2,1)S(1)}, u32[]{:S(2)}, u32[]{:S(2)}) collective-permute-start(bf16[4096,128]{1,0:T(8,128)(2,1)} %bitcast.9), channel_id=1, source_target_pairs={{0,2},{2,0},{4,6},{6,4},{8,10},{10,8},{12,14},{14,12},{16,18},{18,... | collective-permute-start | bytes 3145736 | tf_op jit(solution)/shard_map/ppermute | solution.py:22
  3.4 7.0 %collective-permute-start.3 = (bf16[128,128]{1,0:T(8,128)(2,1)S(1)}, bf16[128,128]{1,0:T(8,128)(2,1)S(1)}, u32[]{:S(2)}, u32[]{:S(2)}) collective-permute-start(bf16[128,128]{1,0:T(8,128)(2,1)S(1)} %bitcast.12), channel_id=1, source_target_pairs={{0,4},{2,6},{4,8},{6,10},{8,12},{10,14},{12,0},{14,2},{16,20},{18,... | collective-permute-start | bytes 98312 | tf_op jit(solution)/shard_map/ppermute | solution.py:22
  5.0 5.4 %collective-permute-start.4 = (bf16[128,128]{1,0:T(8,128)(2,1)S(1)}, bf16[128,128]{1,0:T(8,128)(2,1)S(1)}, u32[]{:S(2)}, u32[]{:S(2)}) collective-permute-start(bf16[128,128]{1,0:T(8,128)(2,1)S(1)} %bitcast.13), channel_id=1, source_target_pairs={{0,12},{2,14},{4,0},{6,2},{8,4},{10,6},{12,8},{14,10},{16,28},{18,... | collective-permute-start | bytes 98312 | tf_op jit(solution)/shard_map/ppermute | solution.py:22
  6.7 5.4 %collective-permute-start.5 = (bf16[128,128]{1,0:T(8,128)(2,1)S(1)}, bf16[128,128]{1,0:T(8,128)(2,1)S(1)}, u32[]{:S(2)}, u32[]{:S(2)}) collective-permute-start(bf16[128,128]{1,0:T(8,128)(2,1)S(1)} %bitcast.14), channel_id=1, source_target_pairs={{0,8},{2,10},{4,12},{6,14},{8,0},{10,2},{12,4},{14,6},{16,24},{18,... | collective-permute-start | bytes 98312 | tf_op jit(solution)/shard_map/ppermute | solution.py:22
  12.1 10.1 %collective-permute-start.6 = (bf16[512,128]{1,0:T(8,128)(2,1)S(1)}, bf16[512,128]{1,0:T(8,128)(2,1)S(1)}, u32[]{:S(2)}, u32[]{:S(2)}) collective-permute-start(bf16[512,128]{1,0:T(8,128)(2,1)S(1)} %pad_maximum_fusion.refs_5_), channel_id=1, source_target_pairs={{0,32},{2,34},{4,36},{6,38},{8,40},{10,42},{12,44},{14,46},{16,48}... | collective-permute-start | bytes 393224 | tf_op jit(solution)/shard_map/ppermute | solution.py:22
  13.9 8.3 %collective-permute-start.7 = (bf16[512,128]{1,0:T(8,128)(2,1)S(1)}, bf16[512,128]{1,0:T(8,128)(2,1)S(1)}, u32[]{:S(2)}, u32[]{:S(2)}) collective-permute-start(bf16[512,128]{1,0:T(8,128)(2,1)S(1)} %pad_maximum_fusion.refs_5_), channel_id=1, source_target_pairs={{0,96},{2,98},{4,100},{6,102},{8,104},{10,106},{12,108},{14,110},{... | collective-permute-start | bytes 393224 | tf_op jit(solution)/shard_map/ppermute | solution.py:22
  15.5 6.8 %collective-permute-start.8 = (bf16[512,128]{1,0:T(8,128)(2,1)S(1)}, bf16[512,128]{1,0:T(8,128)(2,1)S(1)}, u32[]{:S(2)}, u32[]{:S(2)}) collective-permute-start(bf16[512,128]{1,0:T(8,128)(2,1)S(1)} %pad_maximum_fusion.refs_5_), channel_id=1, source_target_pairs={{0,64},{2,66},{4,68},{6,70},{8,72},{10,74},{12,76},{14,78},{16,80}... | collective-permute-start | bytes 393224 | tf_op jit(solution)/shard_map/ppermute | solution.py:22
  17.7 3.2 %copy-start = (bf16[64,64,128]{2,1,0:T(8,128)(2,1)S(1)}, bf16[64,64,128]{2,1,0:T(8,128)(2,1)}, u32[]{:S(2)}) copy-start(bf16[64,64,128]{2,1,0:T(8,128)(2,1)} %param.5) | copy-start | bytes 3145732
  17.7 14.3 %collective-permute-start.10 = (bf16[512,128]{1,0:T(8,128)(2,1)S(1)}, bf16[512,128]{1,0:T(8,128)(2,1)S(1)}, u32[]{:S(2)}, u32[]{:S(2)}) collective-permute-start(bf16[512,128]{1,0:T(8,128)(2,1)S(1)} %pad_maximum_fusion.refs_5_), channel_id=1, source_target_pairs={{0,16},{2,18},{4,20},{6,22},{8,24},{10,26},{12,28},{14,30},{16,0},... | collective-permute-start | bytes 393224 | tf_op jit(solution)/shard_map/ppermute | solution.py:22
  22.3 9.7 %collective-permute-start.11 = (bf16[1536,128]{1,0:T(8,128)(2,1)S(1)}, bf16[1536,128]{1,0:T(8,128)(2,1)S(1)}, u32[]{:S(2)}, u32[]{:S(2)}) collective-permute-start(bf16[1536,128]{1,0:T(8,128)(2,1)S(1)} %constant_dynamic-update-slice_fusion.refs_6_), channel_id=1, source_target_pairs={{0,16},{2,18},{4,20},{6,22},{8,24},{10,26},{12,28},{14,30},{16,0},... | collective-permute-start | bytes 1179656 | tf_op jit(solution)/shard_map/ppermute | solution.py:22
  39.7 1.3 %collective-permute-start.12 = (bf16[64,256]{1,0:T(8,128)(2,1)S(1)}, bf16[64,256]{1,0:T(8,128)(2,1)S(1)}, u32[]{:S(2)}, u32[]{:S(2)}) collective-permute-start(bf16[64,256]{1,0:T(8,128)(2,1)S(1)} %get-tuple-element.54), channel_id=1, source_target_pairs={{0,2},{2,0},{4,6},{6,4},{8,10},{10,8},{12,14},{14,12},{16,18},{18,... | collective-permute-start | bytes 98312 | tf_op jit(solution)/shard_map/ppermute | solution.py:22
  41.0 5.5 %collective-permute-start.13 = (bf16[64,256]{1,0:T(8,128)(2,1)S(1)}, bf16[64,256]{1,0:T(8,128)(2,1)S(1)}, u32[]{:S(2)}, u32[]{:S(2)}) collective-permute-start(bf16[64,256]{1,0:T(8,128)(2,1)S(1)} %add.39), channel_id=1, source_target_pairs={{0,1},{1,0},{2,3},{3,2},{4,5},{5,4},{6,7},{7,6},{8,9},{9,8},{10,11... | collective-permute-start | bytes 98312 | tf_op jit(solution)/shard_map/ppermute | solution.py:22

commit v5 on v4

--- a/solution.py
+++ b/solution.py
@@ -90,16 +90,14 @@
     mark = marks.astype(jnp.float32)[CHUNK - 1:CHUNK, :]
     limit = jnp.where(mark > MARK / 2, mark - MARK, float(BLOCK)).astype(jnp.int32)
     chunks = jnp.where((lane1 < 2 * blocks) & ((lane1 // per_row) % 2 == plane), (limit + (CHUNK - 1)) // CHUNK, 0)
-    upto = chunks
-    step = 1
-    while step < 2 * blocks:
-        upto = upto + jnp.where(lane1 >= step, pltpu.roll(upto, step, 1), 0)
-        step *= 2
+    square = (128, 128)
+    across_lanes = lax.broadcasted_iota(jnp.int32, square, 1)
+    down_rows = lax.broadcasted_iota(jnp.int32, square, 0)
+    along = jnp.broadcast_to(chunks.astype(jnp.float32), square)
+    upto = jnp.sum(jnp.where(down_rows <= across_lanes, along.T, 0.0), axis=0, keepdims=True).astype(jnp.int32)
     before = upto - chunks
-    square = (128, 128)
-    down = jnp.broadcast_to(upto.astype(jnp.float32), square).T
-    at_chunk = lax.broadcasted_iota(jnp.int32, square, 1).astype(jnp.float32)
-    earlier = (down <= at_chunk) & (lax.broadcasted_iota(jnp.int32, square, 0) < 2 * blocks)
+    down = jnp.sum(jnp.where(across_lanes <= down_rows, along, 0.0), axis=1, keepdims=True)
+    earlier = (down <= across_lanes.astype(jnp.float32)) & (down_rows < 2 * blocks)
     shard = jnp.sum(earlier.astype(jnp.float32), axis=0, keepdims=True).astype(jnp.int32)
     shard = jnp.broadcast_to(jnp.minimum(shard, 2 * blocks - 1), (8, 128))
     skipped = (lane - jnp.take_along_axis(jnp.broadcast_to(before, (8, 128)), shard, axis=1)) * CHUNK

time: 47.1 us -> 46.6 us (0.989)
  Pallas kernels: 17.3 us -> 16.6 us
    pallas_call x2, Pallas kernels: 15.2 us -> 14.5 us  [pooled(): pl.pallas_call(kernel, out_shape=jax.ShapeDtypeStruct((tokens, 128), jnp....]
  transfers between devices with their start and end apart: 14 -> 14, of which waited for: 3 -> 3; matrix products, arithmetic and copies ran while one was open for 7% -> 8% of each run, Pallas kernels for 19% -> 19%
where the time goes in v5:
time: 46.6 us; the launch traced here: 46.4 us
  starting transfers between devices  18.5 us (40%)
  Pallas kernels  16.6 us (36%)
  waiting for transfers between devices  5.45 us (12%)
  local copies, waits for them, and re-layouts  3.72 us (8%)
  other arithmetic  1.95 us (4%)
    ppermute x14, starting transfers between devices, swapped(): return lax.ppermute(value, axis, pairs)  18.5 us
    pallas_call x2, Pallas kernels, pooled(): pl.pallas_call(kernel, out_shape=jax.ShapeDtypeStruct((tokens, 128), jnp....  14.5 us
    ppermute x14, waiting for transfers between devices, swapped(): return lax.ppermute(value, axis, pairs)  5.45 us
    unnamed x8, local copies, waits for them, and re-layouts  1.53 us
    pallas_call x1, Pallas kernels, body(): pl.pallas_call(lambda *refs: arrange(tokens, heads, head_size ** (-0.5),...  1.25 us
    broadcast_in_dim x2, local copies, waits for them, and re-layouts, body(): jnp.broadcast_to(value[:, None], (count * heads, 128))  1.19 us
  transfers between devices with their start and end apart: 14, of which 3 were waited for; matrix products, arithmetic and copies ran while one was open for 8% of the time, Pallas kernels for 19%

profile of v5, /device:TPU:0, one launch (start us, length us, event | category | flops | bytes accessed | tf_op | source)
XLA Modules:
  0.0 46.4 jit_solution(4963555783492301584)
XLA Ops:
  0.0 0.8 %copy-done.1 = bf16[256,128]{1,0:T(8,128)(2,1)S(1)} copy-done((bf16[256,128]{1,0:T(8,128)(2,1)S(1)}, bf16[256,128]{1,0:T(8,128)(2,1)}, u32[]{:S(2)}) %copy-start.1) | copy-done | bytes 65560
  0.8 0.7 %copy-done.2 = s32[4]{0:T(128)S(1)} copy-done((s32[4]{0:T(128)S(1)}, s32[4]{0:T(128)}, u32[]{:S(2)}) %copy-start.2) | copy-done | bytes 40
  1.5 0.6 %marked.1 = (bf16[64,128]{1,0:T(8,128)(2,1)S(1)}, bf16[64,128]{1,0:T(8,128)(2,1)S(1)}) custom-call(s32[4]{0:T(128)S(1)} %copy-done.2, bf16[256,128]{1,0:T(8,128)(2,1)S(1)} %copy-done.1), custom_call_target="tpu_custom_call" | custom-call | tf_op jit(solution)/shard_map/marked/pallas_call | solution.py:263
  2.1 0.1 collective-permute-start
  2.2 0.5 %collective-permute-start.2 = (f32[64,64]{1,0:T(8,128)}, f32[64,64]{1,0:T(8,128)S(1)}, u32[]{:S(2)}, u32[]{:S(2)}) collective-permute-start(f32[64,64]{1,0:T(8,128)} %param.6), channel_id=1, source_target_pairs={{0,2},{2,0},{4,6},{6,4},{8,10},{10,8},{12,14},{14,12},{16,18},{18,... | collective-permute-start | bytes 49160 | tf_op jit(solution)/shard_map/ppermute | solution.py:22
  2.7 0.1 collective-permute-start.1
  2.8 0.4 collective-permute-start.9
  3.2 0.1 fusion.1.spread_ref
  3.4 1.6 %collective-permute-start.3 = (bf16[128,128]{1,0:T(8,128)(2,1)S(1)}, bf16[128,128]{1,0:T(8,128)(2,1)S(1)}, u32[]{:S(2)}, u32[]{:S(2)}) collective-permute-start(bf16[128,128]{1,0:T(8,128)(2,1)S(1)} %bitcast.12), channel_id=1, source_target_pairs={{0,4},{2,6},{4,8},{6,10},{8,12},{10,14},{12,0},{14,2},{16,20},{18,... | collective-permute-start | bytes 98312 | tf_op jit(solution)/shard_map/ppermute | solution.py:22
  5.0 1.7 %collective-permute-start.4 = (bf16[128,128]{1,0:T(8,128)(2,1)S(1)}, bf16[128,128]{1,0:T(8,128)(2,1)S(1)}, u32[]{:S(2)}, u32[]{:S(2)}) collective-permute-start(bf16[128,128]{1,0:T(8,128)(2,1)S(1)} %bitcast.13), channel_id=1, source_target_pairs={{0,12},{2,14},{4,0},{6,2},{8,4},{10,6},{12,8},{14,10},{16,28},{18,... | collective-permute-start | bytes 98312 | tf_op jit(solution)/shard_map/ppermute | solution.py:22
  6.7 1.9 %collective-permute-start.5 = (bf16[128,128]{1,0:T(8,128)(2,1)S(1)}, bf16[128,128]{1,0:T(8,128)(2,1)S(1)}, u32[]{:S(2)}, u32[]{:S(2)}) collective-permute-start(bf16[128,128]{1,0:T(8,128)(2,1)S(1)} %bitcast.14), channel_id=1, source_target_pairs={{0,8},{2,10},{4,12},{6,14},{8,0},{10,2},{12,4},{14,6},{16,24},{18,... | collective-permute-start | bytes 98312 | tf_op jit(solution)/shard_map/ppermute | solution.py:22
  8.6 0.7 %pad_add_fusion = s32[128]{0:T(128)S(1)} fusion(s32[64]{0:T(128)S(1)} %collective-permute-done.1, s32[64]{0:T(128)} %param.8), kind=kLoop, calls=%fused_computation.17 | loop fusion | flops 128 | bytes 1024 | tf_op jit(solution)/shard_map/concatenate | solution.py:289
  9.3 0.2 convert_reduce_fusion.refs_0_
  9.5 0.8 %reshape.30 = f32[4096]{0:T(1024)S(1)} reshape(f32[64,64]{1,0:T(8,128)} %param.6) | data formatting | bytes 32768 | tf_op jit(solution)/shard_map/reshape | solution.py:290
  10.4 1.7 %collective-permute-done.5 = bf16[128,128]{1,0:T(8,128)(2,1)S(1)} collective-permute-done((bf16[128,128]{1,0:T(8,128)(2,1)S(1)}, bf16[128,128]{1,0:T(8,128)(2,1)S(1)}, u32[]{:S(2)}, u32[]{:S(2)}) %collective-permute-start.5) | collective-permute-done | bytes 32800 | tf_op jit(solution)/shard_map/ppermute | solution.py:22
  12.1 1.7 %collective-permute-start.6 = (bf16[512,128]{1,0:T(8,128)(2,1)S(1)}, bf16[512,128]{1,0:T(8,128)(2,1)S(1)}, u32[]{:S(2)}, u32[]{:S(2)}) collective-permute-start(bf16[512,128]{1,0:T(8,128)(2,1)S(1)} %pad_maximum_fusion.refs_5_), channel_id=1, source_target_pairs={{0,32},{2,34},{4,36},{6,38},{8,40},{10,42},{12,44},{14,46},{16,48}... | collective-permute-start | bytes 393224 | tf_op jit(solution)/shard_map/ppermute | solution.py:22
  13.9 1.6 %collective-permute-start.7 = (bf16[512,128]{1,0:T(8,128)(2,1)S(1)}, bf16[512,128]{1,0:T(8,128)(2,1)S(1)}, u32[]{:S(2)}, u32[]{:S(2)}) collective-permute-start(bf16[512,128]{1,0:T(8,128)(2,1)S(1)} %pad_maximum_fusion.refs_5_), channel_id=1, source_target_pairs={{0,96},{2,98},{4,100},{6,102},{8,104},{10,106},{12,108},{14,110},{... | collective-permute-start | bytes 393224 | tf_op jit(solution)/shard_map/ppermute | solution.py:22
  15.5 2.1 %collective-permute-start.8 = (bf16[512,128]{1,0:T(8,128)(2,1)S(1)}, bf16[512,128]{1,0:T(8,128)(2,1)S(1)}, u32[]{:S(2)}, u32[]{:S(2)}) collective-permute-start(bf16[512,128]{1,0:T(8,128)(2,1)S(1)} %pad_maximum_fusion.refs_5_), channel_id=1, source_target_pairs={{0,64},{2,66},{4,68},{6,70},{8,72},{10,74},{12,76},{14,78},{16,80}... | collective-permute-start | bytes 393224 | tf_op jit(solution)/shard_map/ppermute | solution.py:22
  17.6 0.1 select_reduce_fusion.refs_0_
  17.7 2.0 %collective-permute-start.10 = (bf16[512,128]{1,0:T(8,128)(2,1)S(1)}, bf16[512,128]{1,0:T(8,128)(2,1)S(1)}, u32[]{:S(2)}, u32[]{:S(2)}) collective-permute-start(bf16[512,128]{1,0:T(8,128)(2,1)S(1)} %pad_maximum_fusion.refs_5_), channel_id=1, source_target_pairs={{0,16},{2,18},{4,20},{6,22},{8,24},{10,26},{12,28},{14,30},{16,0},... | collective-permute-start | bytes 393224 | tf_op jit(solution)/shard_map/ppermute | solution.py:22
  19.7 0.6 %broadcast_in_dim.20.refs_3_ = f32[4096,128]{1,0:T(8,128)S(1)} broadcast(f32[4096]{0:T(1024)S(1)} %reshape.30), dimensions={0} | broadcast | bytes 2113536 | tf_op jit(solution)/shard_map/broadcast_in_dim | solution.py:304
  20.3 0.6 %broadcast_in_dim.21.refs_4_ = f32[4096,128]{1,0:T(8,128)S(1)} broadcast(f32[4096]{0:T(1024)S(1)} %reshape.31), dimensions={0} | broadcast | bytes 2113536 | tf_op jit(solution)/shard_map/broadcast_in_dim | solution.py:304
  20.9 1.2 %arranged.1 = (bf16[8192,128]{1,0:T(8,128)(2,1)S(1)}, f32[8192,128]{1,0:T(8,128)S(1)}) custom-call(s32[128]{0:T(128)S(1)} %convert_reduce_fusion.refs_0_, bf16[4096,128]{1,0:T(8,128)(2,1)S(1)} %bitcast.10, bf16[4096,128]{1,0:T(8,128)(2,1)S(1)} %collective-permute-done.9.refs_2_, f32[4096,128]{1,0:T(8,128)S(1)} %broadcast_in_dim.20.refs_3_, ...), custom_call_target="tpu_custom_call" | custom-call | bytes 12582912 | tf_op jit(solution)/shard_map/arranged/pallas_call | solution.py:309
  22.3 1.8 %collective-permute-start.11 = (bf16[1536,128]{1,0:T(8,128)(2,1)S(1)}, bf16[1536,128]{1,0:T(8,128)(2,1)S(1)}, u32[]{:S(2)}, u32[]{:S(2)}) collective-permute-start(bf16[1536,128]{1,0:T(8,128)(2,1)S(1)} %constant_dynamic-update-slice_fusion.refs_6_), channel_id=1, source_target_pairs={{0,16},{2,18},{4,20},{6,22},{8,24},{10,26},{12,28},{14,30},{16,0},... | collective-permute-start | bytes 1179656 | tf_op jit(solution)/shard_map/ppermute | solution.py:22
  24.1 7.5 %pooled_scores.2.near_ref = bf16[128,128]{1,0:T(8,128)(2,1)S(1)} custom-call(s32[128]{0:T(128)S(1)} %select_reduce_fusion.refs_0_, s32[4]{0:T(128)S(1)} %get-tuple-element.55.refs_1_, bf16[8192,128]{1,0:T(8,128)(2,1)S(1)} %get-tuple-element.48.refs_2_, f32[8192,128]{1,0:T(8,128)S(1)} %get-tuple-element.49.refs_3_, s32[128,128]{1,0:T(8,128)S(1)} %broadcast_in_dim.22.refs_4_, ...), custom_call_target="tpu_custom_call" | custom-call | flops 4294967296 | bytes 8388608 | tf_op jit(solution)/shard_map/pooled_scores/pallas_call | solution.py:337
  31.7 7.0 %pooled_scores.3.far_ref = bf16[128,128]{1,0:T(8,128)(2,1)S(1)} custom-call(s32[128]{0:T(128)S(1)} %select_reduce_fusion.refs_0_, s32[4]{0:T(128)S(1)} %get-tuple-element.56.refs_1_, bf16[8192,128]{1,0:T(8,128)(2,1)S(1)} %get-tuple-element.48.refs_2_, f32[8192,128]{1,0:T(8,128)S(1)} %get-tuple-element.49.refs_3_, s32[128,128]{1,0:T(8,128)S(1)} %broadcast_in_dim.22.refs_4_, ...), custom_call_target="tpu_custom_call" | custom-call | flops 4294967296 | bytes 8388608 | tf_op jit(solution)/shard_map/pooled_scores/pallas_call | solution.py:337
  38.7 0.3 restored.1
  39.0 0.1 collective-permute-start.12
  39.0 1.2 %collective-permute-done.12 = bf16[64,256]{1,0:T(8,128)(2,1)S(1)} collective-permute-done((bf16[64,256]{1,0:T(8,128)(2,1)S(1)}, bf16[64,256]{1,0:T(8,128)(2,1)S(1)}, u32[]{:S(2)}, u32[]{:S(2)}) %collective-permute-start.12) | collective-permute-done | bytes 32800 | tf_op jit(solution)/shard_map/ppermute | solution.py:22
  40.3 3.0 %collective-permute-start.13 = (bf16[64,256]{1,0:T(8,128)(2,1)S(1)}, bf16[64,256]{1,0:T(8,128)(2,1)S(1)}, u32[]{:S(2)}, u32[]{:S(2)}) collective-permute-start(bf16[64,256]{1,0:T(8,128)(2,1)S(1)} %add.39), channel_id=1, source_target_pairs={{0,1},{1,0},{2,3},{3,2},{4,5},{5,4},{6,7},{7,6},{8,9},{9,8},{10,11... | collective-permute-start | bytes 98312 | tf_op jit(solution)/shard_map/ppermute | solution.py:22
  43.2 2.5 %collective-permute-done.13 = bf16[64,256]{1,0:T(8,128)(2,1)S(1)} collective-permute-done((bf16[64,256]{1,0:T(8,128)(2,1)S(1)}, bf16[64,256]{1,0:T(8,128)(2,1)S(1)}, u32[]{:S(2)}, u32[]{:S(2)}) %collective-permute-start.13) | collective-permute-done | bytes 32800 | tf_op jit(solution)/shard_map/ppermute | solution.py:22
  45.8 0.6 %add_convert_fusion = f32[64,256]{1,0:T(8,128)} fusion(bf16[64,256]{1,0:T(8,128)(2,1)S(1)} %add.39, bf16[64,256]{1,0:T(8,128)(2,1)S(1)} %collective-permute-done.13), kind=kLoop, calls=%fused_computation.13 | loop fusion | flops 32768 | bytes 131072 | tf_op jit(solution)/shard_map/convert_element_type | solution.py:364
  (27 shorter events, 0.4 us)
Async XLA Ops:
  0.0 0.8 %copy-start.1 = (bf16[256,128]{1,0:T(8,128)(2,1)S(1)}, bf16[256,128]{1,0:T(8,128)(2,1)}, u32[]{:S(2)}) copy-start(bf16[256,128]{1,0:T(8,128)(2,1)} %key_hbm.1) | copy-start | bytes 196612
  0.8 0.7 %copy-start.2 = (s32[4]{0:T(128)S(1)}, s32[4]{0:T(128)}, u32[]{:S(2)}) copy-start(s32[4]{0:T(128)} %limit_hbm.1) | copy-start | bytes 52
  2.1 1.3 %collective-permute-start = (bf16[64,128]{1,0:T(8,128)(2,1)S(1)}, bf16[64,128]{1,0:T(8,128)(2,1)S(1)}, u32[]{:S(2)}, u32[]{:S(2)}) collective-permute-start(bf16[64,128]{1,0:T(8,128)(2,1)S(1)} %get-tuple-element.31), channel_id=1, source_target_pairs={{0,2},{2,0},{4,6},{6,4},{8,10},{10,8},{12,14},{14,12},{16,18},{18,... | collective-permute-start | bytes 49160 | tf_op jit(solution)/shard_map/ppermute | solution.py:22
  2.2 6.4 %collective-permute-start.2 = (f32[64,64]{1,0:T(8,128)}, f32[64,64]{1,0:T(8,128)S(1)}, u32[]{:S(2)}, u32[]{:S(2)}) collective-permute-start(f32[64,64]{1,0:T(8,128)} %param.6), channel_id=1, source_target_pairs={{0,2},{2,0},{4,6},{6,4},{8,10},{10,8},{12,14},{14,12},{16,18},{18,... | collective-permute-start | bytes 49160 | tf_op jit(solution)/shard_map/ppermute | solution.py:22
  2.7 4.0 %collective-permute-start.1 = (s32[64]{0:T(128)}, s32[64]{0:T(128)S(1)}, u32[]{:S(2)}, u32[]{:S(2)}) collective-permute-start(s32[64]{0:T(128)} %param.8), channel_id=1, source_target_pairs={{0,2},{2,0},{4,6},{6,4},{8,10},{10,8},{12,14},{14,12},{16,18},{18,... | collective-permute-start | bytes 776 | tf_op jit(solution)/shard_map/ppermute | solution.py:22
  2.8 17.0 %collective-permute-start.9 = (bf16[4096,128]{1,0:T(8,128)(2,1)}, bf16[4096,128]{1,0:T(8,128)(2,1)S(1)}, u32[]{:S(2)}, u32[]{:S(2)}) collective-permute-start(bf16[4096,128]{1,0:T(8,128)(2,1)} %bitcast.9), channel_id=1, source_target_pairs={{0,2},{2,0},{4,6},{6,4},{8,10},{10,8},{12,14},{14,12},{16,18},{18,... | collective-permute-start | bytes 3145736 | tf_op jit(solution)/shard_map/ppermute | solution.py:22
  3.4 7.0 %collective-permute-start.3 = (bf16[128,128]{1,0:T(8,128)(2,1)S(1)}, bf16[128,128]{1,0:T(8,128)(2,1)S(1)}, u32[]{:S(2)}, u32[]{:S(2)}) collective-permute-start(bf16[128,128]{1,0:T(8,128)(2,1)S(1)} %bitcast.12), channel_id=1, source_target_pairs={{0,4},{2,6},{4,8},{6,10},{8,12},{10,14},{12,0},{14,2},{16,20},{18,... | collective-permute-start | bytes 98312 | tf_op jit(solution)/shard_map/ppermute | solution.py:22
  5.0 5.4 %collective-permute-start.4 = (bf16[128,128]{1,0:T(8,128)(2,1)S(1)}, bf16[128,128]{1,0:T(8,128)(2,1)S(1)}, u32[]{:S(2)}, u32[]{:S(2)}) collective-permute-start(bf16[128,128]{1,0:T(8,128)(2,1)S(1)} %bitcast.13), channel_id=1, source_target_pairs={{0,12},{2,14},{4,0},{6,2},{8,4},{10,6},{12,8},{14,10},{16,28},{18,... | collective-permute-start | bytes 98312 | tf_op jit(solution)/shard_map/ppermute | solution.py:22
  6.7 5.4 %collective-permute-start.5 = (bf16[128,128]{1,0:T(8,128)(2,1)S(1)}, bf16[128,128]{1,0:T(8,128)(2,1)S(1)}, u32[]{:S(2)}, u32[]{:S(2)}) collective-permute-start(bf16[128,128]{1,0:T(8,128)(2,1)S(1)} %bitcast.14), channel_id=1, source_target_pairs={{0,8},{2,10},{4,12},{6,14},{8,0},{10,2},{12,4},{14,6},{16,24},{18,... | collective-permute-start | bytes 98312 | tf_op jit(solution)/shard_map/ppermute | solution.py:22
  12.1 10.1 %collective-permute-start.6 = (bf16[512,128]{1,0:T(8,128)(2,1)S(1)}, bf16[512,128]{1,0:T(8,128)(2,1)S(1)}, u32[]{:S(2)}, u32[]{:S(2)}) collective-permute-start(bf16[512,128]{1,0:T(8,128)(2,1)S(1)} %pad_maximum_fusion.refs_5_), channel_id=1, source_target_pairs={{0,32},{2,34},{4,36},{6,38},{8,40},{10,42},{12,44},{14,46},{16,48}... | collective-permute-start | bytes 393224 | tf_op jit(solution)/shard_map/ppermute | solution.py:22
  13.9 8.3 %collective-permute-start.7 = (bf16[512,128]{1,0:T(8,128)(2,1)S(1)}, bf16[512,128]{1,0:T(8,128)(2,1)S(1)}, u32[]{:S(2)}, u32[]{:S(2)}) collective-permute-start(bf16[512,128]{1,0:T(8,128)(2,1)S(1)} %pad_maximum_fusion.refs_5_), channel_id=1, source_target_pairs={{0,96},{2,98},{4,100},{6,102},{8,104},{10,106},{12,108},{14,110},{... | collective-permute-start | bytes 393224 | tf_op jit(solution)/shard_map/ppermute | solution.py:22
  15.5 6.8 %collective-permute-start.8 = (bf16[512,128]{1,0:T(8,128)(2,1)S(1)}, bf16[512,128]{1,0:T(8,128)(2,1)S(1)}, u32[]{:S(2)}, u32[]{:S(2)}) collective-permute-start(bf16[512,128]{1,0:T(8,128)(2,1)S(1)} %pad_maximum_fusion.refs_5_), channel_id=1, source_target_pairs={{0,64},{2,66},{4,68},{6,70},{8,72},{10,74},{12,76},{14,78},{16,80}... | collective-permute-start | bytes 393224 | tf_op jit(solution)/shard_map/ppermute | solution.py:22
  17.7 3.2 %copy-start = (bf16[64,64,128]{2,1,0:T(8,128)(2,1)S(1)}, bf16[64,64,128]{2,1,0:T(8,128)(2,1)}, u32[]{:S(2)}) copy-start(bf16[64,64,128]{2,1,0:T(8,128)(2,1)} %param.5) | copy-start | bytes 3145732
  17.7 13.9 %collective-permute-start.10 = (bf16[512,128]{1,0:T(8,128)(2,1)S(1)}, bf16[512,128]{1,0:T(8,128)(2,1)S(1)}, u32[]{:S(2)}, u32[]{:S(2)}) collective-permute-start(bf16[512,128]{1,0:T(8,128)(2,1)S(1)} %pad_maximum_fusion.refs_5_), channel_id=1, source_target_pairs={{0,16},{2,18},{4,20},{6,22},{8,24},{10,26},{12,28},{14,30},{16,0},... | collective-permute-start | bytes 393224 | tf_op jit(solution)/shard_map/ppermute | solution.py:22
  22.3 9.4 %collective-permute-start.11 = (bf16[1536,128]{1,0:T(8,128)(2,1)S(1)}, bf16[1536,128]{1,0:T(8,128)(2,1)S(1)}, u32[]{:S(2)}, u32[]{:S(2)}) collective-permute-start(bf16[1536,128]{1,0:T(8,128)(2,1)S(1)} %constant_dynamic-update-slice_fusion.refs_6_), channel_id=1, source_target_pairs={{0,16},{2,18},{4,20},{6,22},{8,24},{10,26},{12,28},{14,30},{16,0},... | collective-permute-start | bytes 1179656 | tf_op jit(solution)/shard_map/ppermute | solution.py:22
  39.0 1.3 %collective-permute-start.12 = (bf16[64,256]{1,0:T(8,128)(2,1)S(1)}, bf16[64,256]{1,0:T(8,128)(2,1)S(1)}, u32[]{:S(2)}, u32[]{:S(2)}) collective-permute-start(bf16[64,256]{1,0:T(8,128)(2,1)S(1)} %get-tuple-element.54), channel_id=1, source_target_pairs={{0,2},{2,0},{4,6},{6,4},{8,10},{10,8},{12,14},{14,12},{16,18},{18,... | collective-permute-start | bytes 98312 | tf_op jit(solution)/shard_map/ppermute | solution.py:22
  40.3 5.5 %collective-permute-start.13 = (bf16[64,256]{1,0:T(8,128)(2,1)S(1)}, bf16[64,256]{1,0:T(8,128)(2,1)S(1)}, u32[]{:S(2)}, u32[]{:S(2)}) collective-permute-start(bf16[64,256]{1,0:T(8,128)(2,1)S(1)} %add.39), channel_id=1, source_target_pairs={{0,1},{1,0},{2,3},{3,2},{4,5},{5,4},{6,7},{7,6},{8,9},{9,8},{10,11... | collective-permute-start | bytes 98312 | tf_op jit(solution)/shard_map/ppermute | solution.py:22

commit v6 on v5

--- a/solution.py
+++ b/solution.py
@@ -44,7 +44,7 @@
         ref[BLOCK - CHUNK:, :] = jnp.where(row == unfilled, mark, last).astype(ref.dtype)
 
 
-def arrange(tokens, heads, scale, rank_ref, own_ref, other_ref, own_weight_ref, other_weight_ref, q_ref, w_ref):
+def arrange(tokens, heads, rank_ref, own_ref, other_ref, own_weight_ref, other_weight_ref, q_ref, w_ref):
     half = tokens // 2
 
     def step(token, _):
@@ -52,7 +52,7 @@
         for ref, weight_ref, first in ((own_ref, own_weight_ref, 0), (other_ref, other_weight_ref, half)):
             to = pl.multiple_of(rank_ref[first + token] * heads, heads)
             q_ref[pl.ds(to, heads), :] = ref[pl.ds(start, heads), :]
-            w_ref[pl.ds(to, heads), :] = weight_ref[pl.ds(start, heads), :] * scale
+            w_ref[pl.ds(to, heads), :] = weight_ref[pl.ds(start, heads), :]
         return 0
 
     lax.fori_loop(0, half, step, 0, unroll=4)
@@ -78,6 +78,7 @@
     most = max_ref.shape[0]
     rows = GROUP // 2 * heads
     plane = place_ref[2]
+    scale = q_ref.shape[1] ** (-0.5)
     lane1 = lax.broadcasted_iota(jnp.int32, (1, 128), 1)
     lane = lax.broadcasted_iota(jnp.int32, (8, 128), 1)
     wide = lax.broadcasted_iota(jnp.int32, (tokens, 128), 1)
@@ -210,7 +211,7 @@
             filled = lane % CHUNK < jnp.take_along_axis(held, chunk, axis=1)
             value = jnp.take_along_axis(position, chunk, axis=1) + lane % CHUNK
             seen.append(jnp.where(filled, value, FAR)[:1])
-        found = [jnp.where(seen[part] <= at_ref[...], score_ref[2 * tile + part], mask_value) for part in range(2)]
+        found = [jnp.where(seen[part] <= at_ref[...], score_ref[2 * tile + part] * scale, mask_value) for part in range(2)]
         max_ref[tile] = folded(found[0], found[1], 8, wide)
         return 0
 
@@ -307,7 +308,7 @@
     spread = ((lane < shards)[:, None] & (target[:, None] == jnp.arange(shards * local_blocks)[None, :])).astype(jnp.bfloat16)
 
     q_rows, w_rows = pl.pallas_call(
-        lambda *refs: arrange(tokens, heads, head_size ** (-0.5), *refs),
+        lambda *refs: arrange(tokens, heads, *refs),
         out_shape=(
             jax.ShapeDtypeStruct((tokens * heads, head_size), jnp.bfloat16),
             jax.ShapeDtypeStruct((tokens * heads, 128), jnp.float32),

time: 46.6 us -> 46.9 us (level); the launches traced: 46.4 us -> 46.1 us
  transfers between devices with their start and end apart: 14 -> 14, of which waited for: 3 -> 4; matrix products, arithmetic and copies ran while one was open for 8% -> 8% of each run, Pallas kernels for 19% -> 18%
where the time goes in v6:
time: 46.9 us; the launch traced here: 46.1 us
  starting transfers between devices  18.7 us (40%)
  Pallas kernels  16.2 us (35%)
  waiting for transfers between devices  5.32 us (11%)
  local copies, waits for them, and re-layouts  3.72 us (8%)
  other arithmetic  1.95 us (4%)
    ppermute x14, starting transfers between devices, swapped(): return lax.ppermute(value, axis, pairs)  18.7 us
    pallas_call x2, Pallas kernels, pooled(): pl.pallas_call(kernel, out_shape=jax.ShapeDtypeStruct((tokens, 128), jnp....  14.1 us
    ppermute x14, waiting for transfers between devices, swapped(): return lax.ppermute(value, axis, pairs)  5.32 us
    unnamed x8, local copies, waits for them, and re-layouts  1.53 us
    pallas_call x1, Pallas kernels, body(): pl.pallas_call(lambda *refs: arrange(tokens, heads, *refs), out_shape=(ja...  1.23 us
    broadcast_in_dim x2, local copies, waits for them, and re-layouts, body(): jnp.broadcast_to(value[:, None], (count * heads, 128))  1.19 us
  transfers between devices with their start and end apart: 14, of which 4 were waited for; matrix products, arithmetic and copies ran while one was open for 8% of the time, Pallas kernels for 18%

profile of v6, /device:TPU:0, one launch (start us, length us, event | category | flops | bytes accessed | tf_op | source)
XLA Modules:
  0.0 46.1 jit_solution(3381034268670847955)
XLA Ops:
  0.0 0.8 %copy-done.1 = bf16[256,128]{1,0:T(8,128)(2,1)S(1)} copy-done((bf16[256,128]{1,0:T(8,128)(2,1)S(1)}, bf16[256,128]{1,0:T(8,128)(2,1)}, u32[]{:S(2)}) %copy-start.1) | copy-done | bytes 65560
  0.8 0.7 %copy-done.2 = s32[4]{0:T(128)S(1)} copy-done((s32[4]{0:T(128)S(1)}, s32[4]{0:T(128)}, u32[]{:S(2)}) %copy-start.2) | copy-done | bytes 40
  1.5 0.6 %marked.1 = (bf16[64,128]{1,0:T(8,128)(2,1)S(1)}, bf16[64,128]{1,0:T(8,128)(2,1)S(1)}) custom-call(s32[4]{0:T(128)S(1)} %copy-done.2, bf16[256,128]{1,0:T(8,128)(2,1)S(1)} %copy-done.1), custom_call_target="tpu_custom_call" | custom-call | tf_op jit(solution)/shard_map/marked/pallas_call | solution.py:264
  2.1 0.1 collective-permute-start
  2.2 0.5 %collective-permute-start.2 = (f32[64,64]{1,0:T(8,128)}, f32[64,64]{1,0:T(8,128)S(1)}, u32[]{:S(2)}, u32[]{:S(2)}) collective-permute-start(f32[64,64]{1,0:T(8,128)} %param.6), channel_id=1, source_target_pairs={{0,2},{2,0},{4,6},{6,4},{8,10},{10,8},{12,14},{14,12},{16,18},{18,... | collective-permute-start | bytes 49160 | tf_op jit(solution)/shard_map/ppermute | solution.py:22
  2.7 0.1 collective-permute-start.1
  2.8 0.4 collective-permute-start.9
  3.2 0.1 fusion.1.spread_ref
  3.4 1.6 %collective-permute-start.3 = (bf16[128,128]{1,0:T(8,128)(2,1)S(1)}, bf16[128,128]{1,0:T(8,128)(2,1)S(1)}, u32[]{:S(2)}, u32[]{:S(2)}) collective-permute-start(bf16[128,128]{1,0:T(8,128)(2,1)S(1)} %bitcast.12), channel_id=1, source_target_pairs={{0,4},{2,6},{4,8},{6,10},{8,12},{10,14},{12,0},{14,2},{16,20},{18,... | collective-permute-start | bytes 98312 | tf_op jit(solution)/shard_map/ppermute | solution.py:22
  5.0 1.7 %collective-permute-start.4 = (bf16[128,128]{1,0:T(8,128)(2,1)S(1)}, bf16[128,128]{1,0:T(8,128)(2,1)S(1)}, u32[]{:S(2)}, u32[]{:S(2)}) collective-permute-start(bf16[128,128]{1,0:T(8,128)(2,1)S(1)} %bitcast.13), channel_id=1, source_target_pairs={{0,12},{2,14},{4,0},{6,2},{8,4},{10,6},{12,8},{14,10},{16,28},{18,... | collective-permute-start | bytes 98312 | tf_op jit(solution)/shard_map/ppermute | solution.py:22
  6.7 1.9 %collective-permute-start.5 = (bf16[128,128]{1,0:T(8,128)(2,1)S(1)}, bf16[128,128]{1,0:T(8,128)(2,1)S(1)}, u32[]{:S(2)}, u32[]{:S(2)}) collective-permute-start(bf16[128,128]{1,0:T(8,128)(2,1)S(1)} %bitcast.14), channel_id=1, source_target_pairs={{0,8},{2,10},{4,12},{6,14},{8,0},{10,2},{12,4},{14,6},{16,24},{18,... | collective-permute-start | bytes 98312 | tf_op jit(solution)/shard_map/ppermute | solution.py:22
  8.6 0.7 %pad_add_fusion = s32[128]{0:T(128)S(1)} fusion(s32[64]{0:T(128)S(1)} %collective-permute-done.1, s32[64]{0:T(128)} %param.8), kind=kLoop, calls=%fused_computation.17 | loop fusion | flops 128 | bytes 1024 | tf_op jit(solution)/shard_map/concatenate | solution.py:290
  9.3 0.2 convert_reduce_fusion.refs_0_
  9.5 0.8 %reshape.30 = f32[4096]{0:T(1024)S(1)} reshape(f32[64,64]{1,0:T(8,128)} %param.6) | data formatting | bytes 32768 | tf_op jit(solution)/shard_map/reshape | solution.py:291
  10.4 1.7 %collective-permute-done.5 = bf16[128,128]{1,0:T(8,128)(2,1)S(1)} collective-permute-done((bf16[128,128]{1,0:T(8,128)(2,1)S(1)}, bf16[128,128]{1,0:T(8,128)(2,1)S(1)}, u32[]{:S(2)}, u32[]{:S(2)}) %collective-permute-start.5) | collective-permute-done | bytes 32800 | tf_op jit(solution)/shard_map/ppermute | solution.py:22
  12.1 1.7 %collective-permute-start.6 = (bf16[512,128]{1,0:T(8,128)(2,1)S(1)}, bf16[512,128]{1,0:T(8,128)(2,1)S(1)}, u32[]{:S(2)}, u32[]{:S(2)}) collective-permute-start(bf16[512,128]{1,0:T(8,128)(2,1)S(1)} %pad_maximum_fusion.refs_5_), channel_id=1, source_target_pairs={{0,32},{2,34},{4,36},{6,38},{8,40},{10,42},{12,44},{14,46},{16,48}... | collective-permute-start | bytes 393224 | tf_op jit(solution)/shard_map/ppermute | solution.py:22
  13.9 1.6 %collective-permute-start.7 = (bf16[512,128]{1,0:T(8,128)(2,1)S(1)}, bf16[512,128]{1,0:T(8,128)(2,1)S(1)}, u32[]{:S(2)}, u32[]{:S(2)}) collective-permute-start(bf16[512,128]{1,0:T(8,128)(2,1)S(1)} %pad_maximum_fusion.refs_5_), channel_id=1, source_target_pairs={{0,96},{2,98},{4,100},{6,102},{8,104},{10,106},{12,108},{14,110},{... | collective-permute-start | bytes 393224 | tf_op jit(solution)/shard_map/ppermute | solution.py:22
  15.5 2.1 %collective-permute-start.8 = (bf16[512,128]{1,0:T(8,128)(2,1)S(1)}, bf16[512,128]{1,0:T(8,128)(2,1)S(1)}, u32[]{:S(2)}, u32[]{:S(2)}) collective-permute-start(bf16[512,128]{1,0:T(8,128)(2,1)S(1)} %pad_maximum_fusion.refs_5_), channel_id=1, source_target_pairs={{0,64},{2,66},{4,68},{6,70},{8,72},{10,74},{12,76},{14,78},{16,80}... | collective-permute-start | bytes 393224 | tf_op jit(solution)/shard_map/ppermute | solution.py:22
  17.6 0.1 select_reduce_fusion.refs_0_
  17.7 2.0 %collective-permute-start.10 = (bf16[512,128]{1,0:T(8,128)(2,1)S(1)}, bf16[512,128]{1,0:T(8,128)(2,1)S(1)}, u32[]{:S(2)}, u32[]{:S(2)}) collective-permute-start(bf16[512,128]{1,0:T(8,128)(2,1)S(1)} %pad_maximum_fusion.refs_5_), channel_id=1, source_target_pairs={{0,16},{2,18},{4,20},{6,22},{8,24},{10,26},{12,28},{14,30},{16,0},... | collective-permute-start | bytes 393224 | tf_op jit(solution)/shard_map/ppermute | solution.py:22
  19.7 0.6 %broadcast_in_dim.20.refs_3_ = f32[4096,128]{1,0:T(8,128)S(1)} broadcast(f32[4096]{0:T(1024)S(1)} %reshape.30), dimensions={0} | broadcast | bytes 2113536 | tf_op jit(solution)/shard_map/broadcast_in_dim | solution.py:305
  20.3 0.6 %broadcast_in_dim.21.refs_4_ = f32[4096,128]{1,0:T(8,128)S(1)} broadcast(f32[4096]{0:T(1024)S(1)} %reshape.31), dimensions={0} | broadcast | bytes 2113536 | tf_op jit(solution)/shard_map/broadcast_in_dim | solution.py:305
  20.9 1.2 %arranged.1 = (bf16[8192,128]{1,0:T(8,128)(2,1)S(1)}, f32[8192,128]{1,0:T(8,128)S(1)}) custom-call(s32[128]{0:T(128)S(1)} %convert_reduce_fusion.refs_0_, bf16[4096,128]{1,0:T(8,128)(2,1)S(1)} %bitcast.10, bf16[4096,128]{1,0:T(8,128)(2,1)S(1)} %collective-permute-done.9.refs_2_, f32[4096,128]{1,0:T(8,128)S(1)} %broadcast_in_dim.20.refs_3_, ...), custom_call_target="tpu_custom_call" | custom-call | bytes 12582912 | tf_op jit(solution)/shard_map/arranged/pallas_call | solution.py:310
  22.3 1.8 %collective-permute-start.11 = (bf16[1536,128]{1,0:T(8,128)(2,1)S(1)}, bf16[1536,128]{1,0:T(8,128)(2,1)S(1)}, u32[]{:S(2)}, u32[]{:S(2)}) collective-permute-start(bf16[1536,128]{1,0:T(8,128)(2,1)S(1)} %constant_dynamic-update-slice_fusion.refs_6_), channel_id=1, source_target_pairs={{0,16},{2,18},{4,20},{6,22},{8,24},{10,26},{12,28},{14,30},{16,0},... | collective-permute-start | bytes 1179656 | tf_op jit(solution)/shard_map/ppermute | solution.py:22
  24.1 7.0 %pooled_scores.2.near_ref = bf16[128,128]{1,0:T(8,128)(2,1)S(1)} custom-call(s32[128]{0:T(128)S(1)} %select_reduce_fusion.refs_0_, s32[4]{0:T(128)S(1)} %get-tuple-element.55.refs_1_, bf16[8192,128]{1,0:T(8,128)(2,1)S(1)} %get-tuple-element.48.refs_2_, f32[8192,128]{1,0:T(8,128)S(1)} %get-tuple-element.49.refs_3_, s32[128,128]{1,0:T(8,128)S(1)} %broadcast_in_dim.22.refs_4_, ...), custom_call_target="tpu_custom_call" | custom-call | flops 4294967296 | bytes 8388608 | tf_op jit(solution)/shard_map/pooled_scores/pallas_call | solution.py:338
  31.2 7.1 %pooled_scores.3.far_ref = bf16[128,128]{1,0:T(8,128)(2,1)S(1)} custom-call(s32[128]{0:T(128)S(1)} %select_reduce_fusion.refs_0_, s32[4]{0:T(128)S(1)} %get-tuple-element.56.refs_1_, bf16[8192,128]{1,0:T(8,128)(2,1)S(1)} %get-tuple-element.48.refs_2_, f32[8192,128]{1,0:T(8,128)S(1)} %get-tuple-element.49.refs_3_, s32[128,128]{1,0:T(8,128)S(1)} %broadcast_in_dim.22.refs_4_, ...), custom_call_target="tpu_custom_call" | custom-call | flops 4294967296 | bytes 8388608 | tf_op jit(solution)/shard_map/pooled_scores/pallas_call | solution.py:338
  38.3 0.3 restored.1
  38.6 0.1 collective-permute-start.12
  38.7 1.2 %collective-permute-done.12 = bf16[64,256]{1,0:T(8,128)(2,1)S(1)} collective-permute-done((bf16[64,256]{1,0:T(8,128)(2,1)S(1)}, bf16[64,256]{1,0:T(8,128)(2,1)S(1)}, u32[]{:S(2)}, u32[]{:S(2)}) %collective-permute-start.12) | collective-permute-done | bytes 32800 | tf_op jit(solution)/shard_map/ppermute | solution.py:22
  39.9 3.2 %collective-permute-start.13 = (bf16[64,256]{1,0:T(8,128)(2,1)S(1)}, bf16[64,256]{1,0:T(8,128)(2,1)S(1)}, u32[]{:S(2)}, u32[]{:S(2)}) collective-permute-start(bf16[64,256]{1,0:T(8,128)(2,1)S(1)} %add.39), channel_id=1, source_target_pairs={{0,1},{1,0},{2,3},{3,2},{4,5},{5,4},{6,7},{7,6},{8,9},{9,8},{10,11... | collective-permute-start | bytes 98312 | tf_op jit(solution)/shard_map/ppermute | solution.py:22
  43.1 2.3 %collective-permute-done.13 = bf16[64,256]{1,0:T(8,128)(2,1)S(1)} collective-permute-done((bf16[64,256]{1,0:T(8,128)(2,1)S(1)}, bf16[64,256]{1,0:T(8,128)(2,1)S(1)}, u32[]{:S(2)}, u32[]{:S(2)}) %collective-permute-start.13) | collective-permute-done | bytes 32800 | tf_op jit(solution)/shard_map/ppermute | solution.py:22
  45.4 0.6 %add_convert_fusion = f32[64,256]{1,0:T(8,128)} fusion(bf16[64,256]{1,0:T(8,128)(2,1)S(1)} %add.39, bf16[64,256]{1,0:T(8,128)(2,1)S(1)} %collective-permute-done.13), kind=kLoop, calls=%fused_computation.13 | loop fusion | flops 32768 | bytes 131072 | tf_op jit(solution)/shard_map/convert_element_type | solution.py:365
  (27 shorter events, 0.5 us)
Async XLA Ops:
  0.0 0.8 %copy-start.1 = (bf16[256,128]{1,0:T(8,128)(2,1)S(1)}, bf16[256,128]{1,0:T(8,128)(2,1)}, u32[]{:S(2)}) copy-start(bf16[256,128]{1,0:T(8,128)(2,1)} %key_hbm.1) | copy-start | bytes 196612
  0.8 0.7 %copy-start.2 = (s32[4]{0:T(128)S(1)}, s32[4]{0:T(128)}, u32[]{:S(2)}) copy-start(s32[4]{0:T(128)} %limit_hbm.1) | copy-start | bytes 52
  2.1 1.3 %collective-permute-start = (bf16[64,128]{1,0:T(8,128)(2,1)S(1)}, bf16[64,128]{1,0:T(8,128)(2,1)S(1)}, u32[]{:S(2)}, u32[]{:S(2)}) collective-permute-start(bf16[64,128]{1,0:T(8,128)(2,1)S(1)} %get-tuple-element.31), channel_id=1, source_target_pairs={{0,2},{2,0},{4,6},{6,4},{8,10},{10,8},{12,14},{14,12},{16,18},{18,... | collective-permute-start | bytes 49160 | tf_op jit(solution)/shard_map/ppermute | solution.py:22
  2.2 6.4 %collective-permute-start.2 = (f32[64,64]{1,0:T(8,128)}, f32[64,64]{1,0:T(8,128)S(1)}, u32[]{:S(2)}, u32[]{:S(2)}) collective-permute-start(f32[64,64]{1,0:T(8,128)} %param.6), channel_id=1, source_target_pairs={{0,2},{2,0},{4,6},{6,4},{8,10},{10,8},{12,14},{14,12},{16,18},{18,... | collective-permute-start | bytes 49160 | tf_op jit(solution)/shard_map/ppermute | solution.py:22
  2.7 4.0 %collective-permute-start.1 = (s32[64]{0:T(128)}, s32[64]{0:T(128)S(1)}, u32[]{:S(2)}, u32[]{:S(2)}) collective-permute-start(s32[64]{0:T(128)} %param.8), channel_id=1, source_target_pairs={{0,2},{2,0},{4,6},{6,4},{8,10},{10,8},{12,14},{14,12},{16,18},{18,... | collective-permute-start | bytes 776 | tf_op jit(solution)/shard_map/ppermute | solution.py:22
  2.8 17.0 %collective-permute-start.9 = (bf16[4096,128]{1,0:T(8,128)(2,1)}, bf16[4096,128]{1,0:T(8,128)(2,1)S(1)}, u32[]{:S(2)}, u32[]{:S(2)}) collective-permute-start(bf16[4096,128]{1,0:T(8,128)(2,1)} %bitcast.9), channel_id=1, source_target_pairs={{0,2},{2,0},{4,6},{6,4},{8,10},{10,8},{12,14},{14,12},{16,18},{18,... | collective-permute-start | bytes 3145736 | tf_op jit(solution)/shard_map/ppermute | solution.py:22
  3.4 7.0 %collective-permute-start.3 = (bf16[128,128]{1,0:T(8,128)(2,1)S(1)}, bf16[128,128]{1,0:T(8,128)(2,1)S(1)}, u32[]{:S(2)}, u32[]{:S(2)}) collective-permute-start(bf16[128,128]{1,0:T(8,128)(2,1)S(1)} %bitcast.12), channel_id=1, source_target_pairs={{0,4},{2,6},{4,8},{6,10},{8,12},{10,14},{12,0},{14,2},{16,20},{18,... | collective-permute-start | bytes 98312 | tf_op jit(solution)/shard_map/ppermute | solution.py:22
  5.0 5.4 %collective-permute-start.4 = (bf16[128,128]{1,0:T(8,128)(2,1)S(1)}, bf16[128,128]{1,0:T(8,128)(2,1)S(1)}, u32[]{:S(2)}, u32[]{:S(2)}) collective-permute-start(bf16[128,128]{1,0:T(8,128)(2,1)S(1)} %bitcast.13), channel_id=1, source_target_pairs={{0,12},{2,14},{4,0},{6,2},{8,4},{10,6},{12,8},{14,10},{16,28},{18,... | collective-permute-start | bytes 98312 | tf_op jit(solution)/shard_map/ppermute | solution.py:22
  6.7 5.4 %collective-permute-start.5 = (bf16[128,128]{1,0:T(8,128)(2,1)S(1)}, bf16[128,128]{1,0:T(8,128)(2,1)S(1)}, u32[]{:S(2)}, u32[]{:S(2)}) collective-permute-start(bf16[128,128]{1,0:T(8,128)(2,1)S(1)} %bitcast.14), channel_id=1, source_target_pairs={{0,8},{2,10},{4,12},{6,14},{8,0},{10,2},{12,4},{14,6},{16,24},{18,... | collective-permute-start | bytes 98312 | tf_op jit(solution)/shard_map/ppermute | solution.py:22
  12.1 10.0 %collective-permute-start.6 = (bf16[512,128]{1,0:T(8,128)(2,1)S(1)}, bf16[512,128]{1,0:T(8,128)(2,1)S(1)}, u32[]{:S(2)}, u32[]{:S(2)}) collective-permute-start(bf16[512,128]{1,0:T(8,128)(2,1)S(1)} %pad_maximum_fusion.refs_5_), channel_id=1, source_target_pairs={{0,32},{2,34},{4,36},{6,38},{8,40},{10,42},{12,44},{14,46},{16,48}... | collective-permute-start | bytes 393224 | tf_op jit(solution)/shard_map/ppermute | solution.py:22
  13.9 8.3 %collective-permute-start.7 = (bf16[512,128]{1,0:T(8,128)(2,1)S(1)}, bf16[512,128]{1,0:T(8,128)(2,1)S(1)}, u32[]{:S(2)}, u32[]{:S(2)}) collective-permute-start(bf16[512,128]{1,0:T(8,128)(2,1)S(1)} %pad_maximum_fusion.refs_5_), channel_id=1, source_target_pairs={{0,96},{2,98},{4,100},{6,102},{8,104},{10,106},{12,108},{14,110},{... | collective-permute-start | bytes 393224 | tf_op jit(solution)/shard_map/ppermute | solution.py:22
  15.5 6.8 %collective-permute-start.8 = (bf16[512,128]{1,0:T(8,128)(2,1)S(1)}, bf16[512,128]{1,0:T(8,128)(2,1)S(1)}, u32[]{:S(2)}, u32[]{:S(2)}) collective-permute-start(bf16[512,128]{1,0:T(8,128)(2,1)S(1)} %pad_maximum_fusion.refs_5_), channel_id=1, source_target_pairs={{0,64},{2,66},{4,68},{6,70},{8,72},{10,74},{12,76},{14,78},{16,80}... | collective-permute-start | bytes 393224 | tf_op jit(solution)/shard_map/ppermute | solution.py:22
  17.7 3.2 %copy-start = (bf16[64,64,128]{2,1,0:T(8,128)(2,1)S(1)}, bf16[64,64,128]{2,1,0:T(8,128)(2,1)}, u32[]{:S(2)}) copy-start(bf16[64,64,128]{2,1,0:T(8,128)(2,1)} %param.5) | copy-start | bytes 3145732
  17.7 13.4 %collective-permute-start.10 = (bf16[512,128]{1,0:T(8,128)(2,1)S(1)}, bf16[512,128]{1,0:T(8,128)(2,1)S(1)}, u32[]{:S(2)}, u32[]{:S(2)}) collective-permute-start(bf16[512,128]{1,0:T(8,128)(2,1)S(1)} %pad_maximum_fusion.refs_5_), channel_id=1, source_target_pairs={{0,16},{2,18},{4,20},{6,22},{8,24},{10,26},{12,28},{14,30},{16,0},... | collective-permute-start | bytes 393224 | tf_op jit(solution)/shard_map/ppermute | solution.py:22
  22.3 8.9 %collective-permute-start.11 = (bf16[1536,128]{1,0:T(8,128)(2,1)S(1)}, bf16[1536,128]{1,0:T(8,128)(2,1)S(1)}, u32[]{:S(2)}, u32[]{:S(2)}) collective-permute-start(bf16[1536,128]{1,0:T(8,128)(2,1)S(1)} %constant_dynamic-update-slice_fusion.refs_6_), channel_id=1, source_target_pairs={{0,16},{2,18},{4,20},{6,22},{8,24},{10,26},{12,28},{14,30},{16,0},... | collective-permute-start | bytes 1179656 | tf_op jit(solution)/shard_map/ppermute | solution.py:22
  38.6 1.3 %collective-permute-start.12 = (bf16[64,256]{1,0:T(8,128)(2,1)S(1)}, bf16[64,256]{1,0:T(8,128)(2,1)S(1)}, u32[]{:S(2)}, u32[]{:S(2)}) collective-permute-start(bf16[64,256]{1,0:T(8,128)(2,1)S(1)} %get-tuple-element.54), channel_id=1, source_target_pairs={{0,2},{2,0},{4,6},{6,4},{8,10},{10,8},{12,14},{14,12},{16,18},{18,... | collective-permute-start | bytes 98312 | tf_op jit(solution)/shard_map/ppermute | solution.py:22
  39.9 5.5 %collective-permute-start.13 = (bf16[64,256]{1,0:T(8,128)(2,1)S(1)}, bf16[64,256]{1,0:T(8,128)(2,1)S(1)}, u32[]{:S(2)}, u32[]{:S(2)}) collective-permute-start(bf16[64,256]{1,0:T(8,128)(2,1)S(1)} %add.39), channel_id=1, source_target_pairs={{0,1},{1,0},{2,3},{3,2},{4,5},{5,4},{6,7},{7,6},{8,9},{9,8},{10,11... | collective-permute-start | bytes 98312 | tf_op jit(solution)/shard_map/ppermute | solution.py:22
